TPU v7x, 32 devices: a whole 2x2x4 slice. The times are simulated.
32 devices in a mesh: batch: 4 (over x, core), space: 8 (over z, y).
Axes of the slice: x: 2, y: 2, z: 4, core: 2. Of those that a mesh axis runs over, the one named last changes fastest.
Arguments:
- inputs: bfloat16 [4, 32, 128, 128, 128], P('batch', None, None, 'space'), may hold values from -6 to 6
- pre_act: bfloat16 [4, 32, 128, 128, 128], P('batch', None, None, 'space'), may hold values from -8 to 8
- cotangent: bfloat16 [4, 32, 128, 128, 128], P('batch', None, None, 'space'), may hold values from -6 to 6
- spectral_weight: bfloat16 [2, 32, 32, 16384], P(None, None, None, 'space'), may hold values from -6 to 6
- skip_weight: bfloat16 [32, 32], replicated, may hold values from -1 to 1
Outputs:
- grad_inputs: bfloat16 [4, 32, 128, 128, 128], P('batch', None, None, 'space')
- grad_spectral: float32 [2, 32, 32, 16384], P(None, None, 'batch', 'space')
- grad_skip: float32 [32, 32], replicated
All inputs are finite; a program needn't handle non-finite values.
Results may differ from a plain program's by a relative error of at most 0.0055.
Values sent between devices are 32-bit elements; how exact they have to be, the bound alone decides.
No kernel may reach another device: no remote copies, remote signals or barrier semaphores. Data moves between devices by JAX's collectives and lax.ppermute only.
A program may use at most 256 MiB of HBM per device.

v0:
```python
import math

import jax
import jax.numpy as jnp
from jax import lax
from jax.sharding import PartitionSpec as P

NX = 128
NY = 128
NZ = 128
MX = 16
MY = 16
MZ = 16


HIGHEST = lax.Precision.HIGHEST


def phase_table(length, count, signed):
    points = jnp.arange(length, dtype=jnp.int32)
    orders = jnp.arange(count, dtype=jnp.int32)
    if signed:
        orders = jnp.where(orders < count // 2, orders, orders - count)
    residues = jnp.mod(points[:, None] * orders[None, :], length)
    radians = residues.astype(jnp.float32) * (2.0 * math.pi / length)
    return (jnp.cos(radians), jnp.sin(radians))


def forward_block(cosine, sine):
    return jnp.stack(
        [jnp.stack([cosine, -sine], axis=1), jnp.stack([sine, cosine], axis=1)], axis=0
    )


def inverse_block(cosine, sine):
    cos_rows = cosine.T
    sin_rows = sine.T
    return jnp.stack(
        [jnp.stack([cos_rows, sin_rows], axis=1), jnp.stack([-sin_rows, cos_rows], axis=1)], axis=0
    )


def gelu_slope(values):
    normal_cdf = 0.5 * (1.0 + jax.scipy.special.erf(values * (1.0 / math.sqrt(2.0))))
    density = jnp.exp(-0.5 * values * values) * (1.0 / math.sqrt(2.0 * math.pi))
    return normal_cdf + values * density


def local_spectrum(grid_in):
    cos_x, sin_x = phase_table(NX, 2 * MX, True)
    table_x = jnp.stack([cos_x, -sin_x], axis=1).astype(jnp.bfloat16)
    section_x = jnp.einsum(
        "scxyz,xpa->scpayz", grid_in, table_x, preferred_element_type=jnp.float32
    )
    cos_z, sin_z = phase_table(NZ, MZ, False)
    section_z = jnp.einsum(
        "scpayz,pzqk->scqyak", section_x, forward_block(cos_z, sin_z), precision=HIGHEST
    )
    return section_z.reshape(
        section_z.shape[0], section_z.shape[1], 2, section_z.shape[3], 2 * MX * MZ
    )


def along_y(spectra):
    cos_y, sin_y = phase_table(NY, 2 * MY, True)
    section_y = jnp.einsum(
        "scpym,pyqk->scqmk", spectra, forward_block(cos_y, sin_y), precision=HIGHEST
    )
    return section_y.reshape(section_y.shape[0], section_y.shape[1], 2, section_y.shape[3] * 2 * MY)


def both_along_y(spectra_pair):
    return (along_y(spectra_pair[0]), along_y(spectra_pair[1]))


def to_grid(spectra):
    shaped = spectra.reshape(spectra.shape[0], spectra.shape[1], 2, spectra.shape[3], 2 * MX, MZ)
    cos_z, sin_z = phase_table(NZ, MZ, False)
    grid_z = jnp.einsum(
        "scpyak,pkqz->scqayz", shaped, inverse_block(cos_z, sin_z), precision=HIGHEST
    )
    cos_x, sin_x = phase_table(NX, 2 * MX, True)
    table_x = jnp.stack([cos_x.T, -sin_x.T], axis=0)
    return jnp.einsum("scpayz,pax->scxyz", grid_z, table_x, precision=HIGHEST)


def cross_terms(spec_left, spec_right):
    real_part = jnp.einsum(
        "sim,som->iom", spec_left[:, :, 0], spec_right[:, :, 0], precision=HIGHEST
    )
    real_part = real_part + jnp.einsum(
        "sim,som->iom", spec_left[:, :, 1], spec_right[:, :, 1], precision=HIGHEST
    )
    imag_part = jnp.einsum(
        "sim,som->iom", spec_left[:, :, 0], spec_right[:, :, 1], precision=HIGHEST
    )
    imag_part = imag_part - jnp.einsum(
        "sim,som->iom", spec_left[:, :, 1], spec_right[:, :, 0], precision=HIGHEST
    )
    return jnp.stack([real_part, imag_part], axis=0)


def contract(weight_part, spec_part):
    return jnp.einsum("iom,som->sim", weight_part, spec_part, preferred_element_type=jnp.float32)


def skip_gradient(grid_in, cot_pre):
    partial_sum = jnp.einsum(
        "sixyz,soxyz->io", grid_in, cot_pre, preferred_element_type=jnp.float32
    )
    summed = lax.psum(partial_sum, ("batch", "space"))
    return summed / math.sqrt(grid_in.shape[0] * lax.axis_size("batch") * NX * NY * NZ)


def on_device(inputs, pre_act, cotangent, spectral_weight, skip_weight):
    samples = inputs.shape[0]
    channels = inputs.shape[1]
    slope_pre = gelu_slope(pre_act.astype(jnp.float32))
    cot_pre = (cotangent.astype(jnp.float32) * slope_pre).astype(jnp.bfloat16)
    spec_u, spec_e = both_along_y(
        (
            lax.all_to_all(
                local_spectrum(inputs), "space", split_axis=4, concat_axis=3, tiled=True
            ),
            lax.all_to_all(
                local_spectrum(cot_pre), "space", split_axis=4, concat_axis=3, tiled=True
            ),
        )
    )
    mode_count = spec_u.shape[3]
    position = jnp.arange(mode_count, dtype=jnp.int32)
    kxz_index = lax.axis_index("space") * (mode_count // (2 * MY)) + position // (2 * MY)
    mode_weights = jnp.where(kxz_index % MZ == 0, 1.0, 2.0).astype(jnp.float32) / float(
        NX * NY * NZ
    )
    mode_grad = lax.psum_scatter(
        cross_terms(spec_u, spec_e), "batch", scatter_dimension=2, tiled=True
    )
    grad_spectral = mode_grad * mode_weights
    rounded = spec_e.astype(jnp.bfloat16)
    weight_real = spectral_weight[0]
    weight_imag = spectral_weight[1]
    back_real = contract(weight_real, rounded[:, :, 0]) + contract(weight_imag, rounded[:, :, 1])
    back_imag = contract(weight_real, rounded[:, :, 1]) - contract(weight_imag, rounded[:, :, 0])
    back_modes = jnp.stack([back_real, back_imag], axis=2) * mode_weights
    shaped = back_modes.reshape(samples, channels, 2, mode_count // (2 * MY), 2 * MY)
    cos_y, sin_y = phase_table(NY, 2 * MY, True)
    grid_y = jnp.einsum("scpmk,pkqy->scqym", shaped, inverse_block(cos_y, sin_y), precision=HIGHEST)
    spatial = to_grid(lax.all_to_all(grid_y, "space", split_axis=3, concat_axis=4, tiled=True))
    mixed = jnp.einsum("io,soxyz->sixyz", skip_weight, cot_pre, preferred_element_type=jnp.float32)
    grad_inputs = (spatial + mixed).astype(jnp.bfloat16)
    grad_skip = skip_gradient(inputs, cot_pre)
    return (grad_inputs, grad_spectral, grad_skip)


def solution(mesh):
    placed = (
        P("batch", None, None, "space", None),
        P("batch", None, None, "space", None),
        P("batch", None, None, "space", None),
        P(None, None, None, "space"),
        P(),
    )
    return jax.shard_map(
        on_device,
        mesh=mesh,
        in_specs=placed,
        out_specs=(P("batch", None, None, "space", None), P(None, None, "batch", "space"), P()),
        check_vma=False,
    )
```

profile of v0, /device:TPU:0, one launch (start us, length us, event | category | flops | bytes accessed | tf_op | source)
XLA Modules:
  0.0 555.8 jit_solution(13616769091836154259)
XLA Ops:
  7.5 19.8 %fusion.25 = bf16[32,128,16,128]{3,2,1,0:T(8,128)(2,1)} fusion(bf16[1,32,128,16,128]{4,3,2,1,0:T(8,128)(2,1)} %param.6, bf16[1,32,128,16,128]{4,3,2,1,0:T(8,128)(2,1)} %param.7), kind=kLoop, calls=%fused_computation.31 | loop fusion | flops 100663296 | bytes 50331648 | tf_op jit(solution)/shard_map/reshape
  27.3 14.3 %fusion.37 = f32[32,2,32,16,128]{4,2,3,0,1:T(8,128)} fusion(bf16[32,128,16,128]{3,2,1,0:T(8,128)(2,1)} %fusion.25, f32[128,1,32]{0,2,1:T(8,128)S(1)} %get-tuple-element.40, f32[128,1,32]{0,2,1:T(8,128)S(1)} %get-tuple-element.41), kind=kOutput, calls=%fused_computation.47 | convolution fusion | flops 1073774592 | bytes 33587200 | tf_op jit(solution)/shard_map/scxyz,xpa->scpayz/dot_general | solution.py:52
  41.6 43.9 %fusion.43 = f32[1,32,2,16,32,16]{4,5,3,1,2,0:T(8,128)} fusion(f32[32,2,32,16,128]{4,2,3,0,1:T(8,128)} %fusion.37, f32[1,128,2,16]{1,3,0,2:T(8,128)S(1)} %get-tuple-element.33, f32[1,128,2,16]{1,3,0,2:T(8,128)S(1)} %get-tuple-element.32), kind=kOutput, calls=%fused_computation.49 | convolution fusion | flops 1610620928 | bytes 18907136 | tf_op jit(solution)/shard_map/scpayz,pzqk->scqyak/dot_general | solution.py:56
  85.5 12.1 %copy.132 = f32[1,32,2,16,32,16]{1,3,2,5,4,0:T(8,128)} copy(f32[1,32,2,16,32,16]{4,5,3,1,2,0:T(8,128)} %fusion.43) | data formatting | bytes 4194304 | tf_op jit(solution)/shard_map/reshape | solution.py:59
  97.6 8.6 %reshape.684 = f32[8,1,65536]{2,1,0:T(1,128)} reshape(f32[512,1,2,16,32]{4,3,2,1,0:T(8,128)} %bitcast.269) | data formatting | bytes 4194304
  106.1 7.5 %all-to-all-start = ((f32[8,1,65536]{2,1,0:T(1,128)}), f32[8,1,65536]{2,1,0:T(1,128)S(1)}, u32[]{:S(2)}, u32[]{:S(2)}) async-start(f32[8,1,65536]{2,1,0:T(1,128)} %reshape.684), calls=%async_computation | async-start | bytes 4194304 | tf_op jit(solution)/shard_map/all_to_all | solution.py:125
  113.6 14.3 %fusion.40 = f32[32,2,32,16,128]{4,2,3,0,1:T(8,128)} fusion(bf16[32,128,16,128]{3,2,1,0:T(8,128)(2,1)} %bitcast.272, f32[128,1,32]{0,2,1:T(8,128)S(1)} %get-tuple-element.40, f32[128,1,32]{0,2,1:T(8,128)S(1)} %get-tuple-element.41), kind=kOutput, calls=%fused_computation.48 | convolution fusion | flops 1073774592 | bytes 33587200 | tf_op jit(solution)/shard_map/scxyz,xpa->scpayz/dot_general | solution.py:52
  127.9 43.4 %fusion.46 = f32[1,32,2,16,32,16]{4,5,3,1,2,0:T(8,128)} fusion(f32[32,2,32,16,128]{4,2,3,0,1:T(8,128)} %fusion.40, f32[1,128,2,16]{1,3,0,2:T(8,128)S(1)} %get-tuple-element.33, f32[1,128,2,16]{1,3,0,2:T(8,128)S(1)} %get-tuple-element.32), kind=kOutput, calls=%fused_computation.50 | convolution fusion | flops 1610620928 | bytes 18907136 | tf_op jit(solution)/shard_map/scpayz,pzqk->scqyak/dot_general | solution.py:56
  171.3 12.3 %copy.139 = f32[1,32,2,16,32,16]{1,3,2,5,4,0:T(8,128)} copy(f32[1,32,2,16,32,16]{4,5,3,1,2,0:T(8,128)} %fusion.46) | data formatting | bytes 4194304 | tf_op jit(solution)/shard_map/reshape | solution.py:59
  183.6 8.6 %reshape.688 = f32[8,1,65536]{2,1,0:T(1,128)} reshape(f32[512,1,2,16,32]{4,3,2,1,0:T(8,128)} %bitcast.270) | data formatting | bytes 4194304
  212.1 7.9 %copy.133 = f32[1,32,2,16,8,64]{5,4,3,2,1,0:T(8,128)} copy(f32[1,32,2,16,8,64]{1,3,2,5,4,0:T(8,128)} %bitcast.267) | data formatting | bytes 4194304 | tf_op jit(solution)/shard_map/all_to_all | solution.py:125
  228.1 17.9 %all-to-all-done.2 = f32[8,1,65536]{2,1,0:T(1,128)} async-done(((f32[8,1,65536]{2,1,0:T(1,128)}), f32[8,1,65536]{2,1,0:T(1,128)}, u32[]{:S(2)}, u32[]{:S(2)}) %all-to-all-start.2) | async-done | bytes 2097184 | tf_op jit(solution)/shard_map/all_to_all | solution.py:122
  246.0 7.3 %reduce.10 = f32[8,65536]{1,0:T(8,128)S(1)} reduce(f32[8,1,65536]{2,1,0:T(1,128)} %all-to-all-done.2, f32[]{:T(128)} %broadcast.824), dimensions={1}, to_apply=%all_to_all.39.reduce_sub_computation | reduce | bytes 4194308 | tf_op jit(solution)/shard_map/all_to_all | solution.py:122
  259.5 7.5 %copy.140 = f32[1,32,2,16,8,64]{5,4,3,2,1,0:T(8,128)} copy(f32[1,32,2,16,8,64]{1,3,2,5,4,0:T(8,128)} %bitcast.268) | data formatting | bytes 4194304 | tf_op jit(solution)/shard_map/all_to_all | solution.py:122
  286.4 8.1 %fusion.33 = (f32[2048,32]{0,1:T(8,128)S(1)}, f32[2048,32]{0,1:T(8,128)S(1)}, f32[2048,32]{0,1:T(8,128)S(1)}, f32[2048,32]{0,1:T(8,128)S(1)}) fusion(f32[2048,32]{0,1:T(8,128)S(1)} %get-tuple-element.25, bf16[2,32,32,2048]{3,2,1,0:T(8,128)(2,1)} %param.8, f32[2048,32]{0,1:T(8,128)S(1)} %get-tuple-element.24), kind=kLoop, calls=%fused_computation.41 | loop fusion | flops 20709376 | bytes 9961472 | tf_op jit(solution)/shard_map/iom,som->sim/dot_general | solution.py:104
  304.2 7.7 %reshape.686 = f32[8,1,65536]{2,1,0:T(1,128)} reshape(f32[128,1,2,32,64]{4,3,2,1,0:T(8,128)} %bitcast.277) | data formatting | bytes 4194304
  316.3 34.0 %fusion.57 = f32[32,32]{0,1:T(8,128)S(1)} fusion(bf16[32,128,16,128]{3,2,1,0:T(8,128)(2,1)} %bitcast.273, bf16[32,128,16,128]{3,2,1,0:T(8,128)(2,1)} %fusion.25), kind=kOutput, calls=%fused_computation.60 | convolution fusion | flops 536870912 | bytes 33558528 | tf_op jit(solution)/shard_map/sixyz,soxyz->io/dot_general | solution.py:108
  350.3 41.4 %psum.7 = f32[32,32]{0,1:T(8,128)S(1)} all-reduce(f32[32,32]{0,1:T(8,128)S(1)} %fusion.57), channel_id=1, replica_groups=mesh['batch'=4,'space'=8] {'batch','space'}, use_global_device_ids=true, to_apply=%region_1.2 | all-reduce | flops 1024 | bytes 8192 | tf_op jit(solution)/shard_map/psum | solution.py:111
  392.8 22.7 %fusion.27 = f32[128,16,128,32]{2,3,1,0:T(8,128)} fusion(bf16[32,128,16,128]{3,2,1,0:T(8,128)(2,1)} %fusion.25, bf16[32,32]{1,0:T(8,128)(2,1)S(1)} %copy-done), kind=kOutput, calls=%fused_computation.33 | convolution fusion | flops 536870912 | bytes 50333696 | tf_op jit(solution)/shard_map/io,soxyz->sixyz/dot_general | solution.py:150
  415.5 7.3 %reduce.9 = f32[8,65536]{1,0:T(8,128)S(1)} reduce(f32[8,1,65536]{2,1,0:T(1,128)} %all-to-all-done.1, f32[]{:T(128)} %broadcast.824), dimensions={1}, to_apply=%all_to_all.36.reduce_sub_computation | reduce | bytes 4194308 | tf_op jit(solution)/shard_map/all_to_all | solution.py:149
  440.2 11.2 %copy.70 = f32[32,2,16,32,16]{3,4,1,2,0:T(8,128)} copy(f32[32,2,16,32,16]{0,4,3,2,1:T(8,128)} %bitcast.271) | data formatting | bytes 4194304 | tf_op jit(solution)/shard_map/reshape.27
  451.4 18.3 %fusion.35 = f32[2,128,32,16,32,1]{1,4,5,3,2,0:T(8,128)} fusion(f32[32,2,16,32,16]{3,4,1,2,0:T(8,128)} %copy.70, f32[1,16,2,128]{3,1,0,2:T(8,128)S(1)} %get-tuple-element.31, f32[1,16,2,128]{3,1,0,2:T(8,128)S(1)} %get-tuple-element.30), kind=kOutput, calls=%fused_computation.43 | convolution fusion | flops 1610620928 | bytes 18907136 | tf_op jit(solution)/shard_map/scpyak,pkqz->scqayz/dot_general | solution.py:79
  469.7 55.7 %fusion.7 = bf16[1,32,128,16,128]{4,2,3,1,0:T(8,128)(2,1)} fusion(f32[128,16,128,32]{2,3,1,0:T(8,128)} %fusion.27, f32[2,128,32,16,32,1]{1,4,5,3,2,0:T(8,128)} %fusion.35, f32[1,32,128]{2,1,0:T(8,128)S(1)} %get-tuple-element.35, f32[1,32,128]{2,1,0:T(8,128)S(1)} %get-tuple-element.34), kind=kOutput, calls=%fused_computation.12 | convolution fusion | flops 6459236352 | bytes 67141632 | tf_op jit(solution)/shard_map/scpayz,pax->scxyz/dot_general | solution.py:84
  525.4 18.5 %copy.85 = bf16[1,32,128,16,128]{4,3,2,1,0:T(8,128)(2,1)} copy(bf16[1,32,128,16,128]{4,2,3,1,0:T(8,128)(2,1)} %fusion.7) | data formatting | bytes 33554432
  (55 shorter events, 90.8 us)
Async XLA Ops:
  7.2 385.6 %copy-start = (bf16[32,32]{1,0:T(8,128)(2,1)S(1)}, bf16[32,32]{1,0:T(8,128)(2,1)}, u32[]{:S(2)}) copy-start(bf16[32,32]{1,0:T(8,128)(2,1)} %param.9) | copy-start | bytes 6148
  106.1 86.1 %all-to-all-start = ((f32[8,1,65536]{2,1,0:T(1,128)}), f32[8,1,65536]{2,1,0:T(1,128)S(1)}, u32[]{:S(2)}, u32[]{:S(2)}) async-start(f32[8,1,65536]{2,1,0:T(1,128)} %reshape.684), calls=%async_computation | async-start | bytes 4194304 | tf_op jit(solution)/shard_map/all_to_all | solution.py:125
  192.2 6.1 %copy-start.1 = (f32[8,1,65536]{2,1,0:T(1,128)}, f32[8,1,65536]{2,1,0:T(1,128)S(1)}, u32[]{:S(2)}) copy-start(f32[8,1,65536]{2,1,0:T(1,128)S(1)} %all-to-all-done) | copy-start | bytes 6291460
  192.2 53.8 %all-to-all-start.2 = ((f32[8,1,65536]{2,1,0:T(1,128)}), f32[8,1,65536]{2,1,0:T(1,128)}, u32[]{:S(2)}, u32[]{:S(2)}) async-start(f32[8,1,65536]{2,1,0:T(1,128)} %reshape.688), calls=%async_computation.2 | async-start | bytes 4194304 | tf_op jit(solution)/shard_map/all_to_all | solution.py:122
  198.2 345.7 %reduce-scatter.2.cloned.1.call-start = ((), (), s32[]{:S(2)}) async-start(), calls=%async_computation.4 | async-start | bytes 20971520 | tf_op jit(solution)/shard_map/reduce_scatter | solution.py:136
  311.9 103.6 %all-to-all-start.1 = ((f32[8,1,65536]{2,1,0:T(1,128)}), f32[8,1,65536]{2,1,0:T(1,128)}, u32[]{:S(2)}, u32[]{:S(2)}) async-start(f32[8,1,65536]{2,1,0:T(1,128)} %reshape.686), calls=%async_computation.1 | async-start | bytes 4194304 | tf_op jit(solution)/shard_map/all_to_all | solution.py:149
Sparse Core Ops, SparseCore 0:
  286.2 126.5 reduce-scatter.1
where the time goes:
time: 562 us; the launch traced here: 556 us
  matrix products  256 us (46%)
  local copies, waits for them, and re-layouts  143 us (25%)
  other arithmetic  65.2 us (12%)
  blocking collectives  41.4 us (7%)
  starting transfers between devices  17.9 us (3%)
  waiting for transfers between devices  17.9 us (3%)
  between operations  14.5 us (3%)
    dot_general x2, matrix products, local_spectrum(): jnp.einsum('scpayz,pzqk->scqyak', section_x, forward_block(cos_z, sin_z),...  87.3 us
    unnamed x12, local copies, waits for them, and re-layouts  59.9 us
    dot_general x1, matrix products, to_grid(): return jnp.einsum('scpayz,pax->scxyz', grid_z, table_x, precision=HIGHEST)  55.7 us
    psum x1, blocking collectives, skip_gradient(): summed = lax.psum(partial_sum, ('batch', 'space'))  41.4 us
    dot_general x1, matrix products, skip_gradient(): jnp.einsum('sixyz,soxyz->io', grid_in, cot_pre, preferred_element_type=jn...  34 us
    dot_general x2, matrix products, local_spectrum(): jnp.einsum('scxyz,xpa->scpayz', grid_in, table_x, preferred_element_type=...  28.6 us
    reshape x2, local copies, waits for them, and re-layouts, local_spectrum(): section_z.reshape(section_z.shape[0], section_z.shape[1], 2, section_z.sh...  24.4 us
    dot_general x1, matrix products, on_device(): jnp.einsum('io,soxyz->sixyz', skip_weight, cot_pre, preferred_element_typ...  22.7 us
  transfers between devices with their start and end apart: 4, of which 1 were waited for; matrix products, arithmetic and copies ran while one was open for 58% of the time, Pallas kernels for 0%

commit v1 on v0

--- a/solution.py
+++ b/solution.py
@@ -1,8 +1,13 @@
+import functools
 import math
 
 import jax
 import jax.numpy as jnp
+import ml_dtypes
+import numpy as np
 from jax import lax
+from jax.experimental import pallas as pl
+from jax.experimental.pallas import tpu as pltpu
 from jax.sharding import PartitionSpec as P
 
 NX = 128
@@ -11,6 +16,492 @@
 MX = 16
 MY = 16
 MZ = 16
+GROUP = 8
+LANES = GROUP * MZ
+BF16 = jnp.bfloat16
+F32 = jnp.float32
+VMEM_LIMIT = 56 * 1024 * 1024
+
+
+def waves(length, count, signed):
+    points = np.arange(length)
+    orders = np.arange(count)
+    if signed:
+        orders = np.where(orders < count // 2, orders, orders - count)
+    radians = np.mod(points[:, None] * orders[None, :], length) * (2.0 * math.pi / length)
+    return np.cos(radians), np.sin(radians)
+
+
+def rounded_table(table):
+    return np.asarray(table, np.float32).astype(ml_dtypes.bfloat16)
+
+
+def z_forward_table():
+    cos, sin = waves(NZ, MZ, False)
+    table = np.zeros((GROUP, NZ, 2, GROUP, MZ))
+    for c in range(GROUP):
+        table[c, :, 0, c, :] = cos
+        table[c, :, 1, c, :] = -sin
+    return jnp.asarray(rounded_table(table.reshape(GROUP * NZ, 2 * LANES)))
+
+
+def z_inverse_table():
+    cos, sin = waves(NZ, MZ, False)
+    table = np.zeros((2, GROUP, MZ, GROUP, NZ))
+    for c in range(GROUP):
+        table[0, c, :, c, :] = cos.T
+        table[1, c, :, c, :] = -sin.T
+    return jnp.asarray(rounded_table(table.reshape(2 * LANES, GROUP * NZ)))
+
+
+def x_forward_table(spaces):
+    cos, sin = waves(NX, 2 * MX, True)
+    cos = cos.T.reshape(spaces, 2 * MX // spaces, NX)
+    sin = sin.T.reshape(spaces, 2 * MX // spaces, NX)
+    table = np.stack([np.stack([cos, sin], axis=2), np.stack([-sin, cos], axis=2)], axis=1)
+    return jnp.asarray(rounded_table(table.reshape(4 * MX, 2 * NX)))
+
+
+def x_inverse_table(spaces):
+    cos, sin = waves(NX, 2 * MX, True)
+    cos = cos.reshape(NX, spaces, 2 * MX // spaces)
+    sin = sin.reshape(NX, spaces, 2 * MX // spaces)
+    table = np.stack([np.stack([cos, -sin], axis=2), np.stack([sin, cos], axis=2)], axis=0)
+    return jnp.asarray(rounded_table(table.reshape(2 * NX, 4 * MX)))
+
+
+def split_pair(table):
+    high = rounded_table(table)
+    low = rounded_table(table - high.astype(np.float64))
+    return jnp.asarray(high), jnp.asarray(low)
+
+
+def y_forward_table(kx_local):
+    cos, sin = waves(NY, 2 * MY, True)
+    table = np.zeros((2, kx_local, 2 * MY, NY, 2, kx_local))
+    for j in range(kx_local):
+        table[0, j, :, :, 0, j] = cos.T
+        table[0, j, :, :, 1, j] = sin.T
+        table[1, j, :, :, 0, j] = -sin.T
+        table[1, j, :, :, 1, j] = cos.T
+    return split_pair(table.reshape(4 * MY * kx_local, 2 * NY * kx_local))
+
+
+def y_inverse_table(kx_local):
+    cos, sin = waves(NY, 2 * MY, True)
+    table = np.zeros((NY, 2, kx_local, 2, kx_local, 2 * MY))
+    for j in range(kx_local):
+        table[:, 0, j, 0, j, :] = cos
+        table[:, 0, j, 1, j, :] = -sin
+        table[:, 1, j, 0, j, :] = sin
+        table[:, 1, j, 1, j, :] = cos
+    return split_pair(table.reshape(2 * NY * kx_local, 4 * MY * kx_local))
+
+
+def dot(left, right):
+    return lax.dot_general(left, right, (((1,), (0,)), ((), ())), preferred_element_type=F32)
+
+
+def dot_split(table_high, table_low, values):
+    high = values.astype(BF16)
+    low = (values - high.astype(F32)).astype(BF16)
+    return dot(table_high, high) + dot(table_high, low) + dot(table_low, high)
+
+
+def params(count=1):
+    return pltpu.CompilerParams(
+        vmem_limit_bytes=VMEM_LIMIT, dimension_semantics=("arbitrary",) * count
+    )
+
+
+def z_then_x(load, table_z, table_x, send_ref, real_ref, imag_ref, planes, spaces):
+    rows = NX * planes
+    step = min(rows, 512)
+    for start in range(0, rows, step):
+        line = jnp.concatenate([load(c, start, step) for c in range(GROUP)], axis=1)
+        found = dot(line, table_z[...])
+        real_ref[start : start + step, :] = found[:, :LANES]
+        imag_ref[start : start + step, :] = found[:, LANES:]
+    part = 4 * MX // spaces
+    for y in range(0, planes, 2):
+        pair = []
+        for at in (y, y + 1):
+            real = real_ref[pl.ds(at, NX, stride=planes), :]
+            imag = imag_ref[pl.ds(at, NX, stride=planes), :]
+            pair.append(jnp.concatenate([real, imag], axis=0).astype(BF16))
+        found = dot(table_x[...], jnp.concatenate(pair, axis=1))
+        for place in range(2):
+            for s in range(spaces):
+                send_ref[s, 0, (y + place) * part : (y + place + 1) * part, :] = found[
+                    s * part : (s + 1) * part, place * LANES : (place + 1) * LANES
+                ]
+
+
+def forward_plain(field_ref, table_z, table_x, send_ref, real_ref, imag_ref, *, planes, spaces):
+    def load(c, start, step):
+        return field_ref[c, start : start + step, :]
+
+    z_then_x(load, table_z, table_x, send_ref, real_ref, imag_ref, planes, spaces)
+
+
+def slope(values):
+    normal_cdf = 0.5 * (1.0 + lax.erf(values * (1.0 / math.sqrt(2.0))))
+    density = jnp.exp(-0.5 * values * values) * (1.0 / math.sqrt(2.0 * math.pi))
+    return normal_cdf + values * density
+
+
+def forward_cot(
+    pre_ref, cot_ref, table_z, table_x, send_ref, out_ref, real_ref, imag_ref, *, planes, spaces
+):
+    def load(c, start, step):
+        pre = pre_ref[c, start : start + step, :].astype(F32)
+        cot = cot_ref[c, start : start + step, :].astype(F32)
+        made = (cot * slope(pre)).astype(BF16)
+        out_ref[c, start : start + step, :] = made
+        return made
+
+    z_then_x(load, table_z, table_x, send_ref, real_ref, imag_ref, planes, spaces)
+
+
+def whole(shape):
+    return pl.BlockSpec(shape, lambda *_: (0,) * len(shape))
+
+
+def forward(fields, planes, spaces, cot):
+    channels, rows, _ = fields[0].shape
+    groups = channels // GROUP
+    part = 4 * MX // spaces
+    field_spec = pl.BlockSpec((GROUP, rows, NZ), lambda g: (g, 0, 0))
+    send_shape = jax.ShapeDtypeStruct((spaces, groups, planes * part, LANES), F32)
+    send_spec = pl.BlockSpec((spaces, 1, planes * part, LANES), lambda g: (0, g, 0, 0))
+    out_shape, out_specs = (send_shape,), (send_spec,)
+    if cot:
+        out_shape += (jax.ShapeDtypeStruct(fields[0].shape, BF16),)
+        out_specs += (field_spec,)
+    return pl.pallas_call(
+        functools.partial(forward_cot if cot else forward_plain, planes=planes, spaces=spaces),
+        out_shape=out_shape,
+        grid=(groups,),
+        in_specs=[field_spec] * len(fields)
+        + [whole((GROUP * NZ, 2 * LANES)), whole((4 * MX, 2 * NX))],
+        out_specs=out_specs,
+        scratch_shapes=[pltpu.VMEM((rows, LANES), F32), pltpu.VMEM((rows, LANES), F32)],
+        compiler_params=params(),
+        cost_estimate=pl.CostEstimate(
+            flops=2 * 8 * channels * rows * NZ * 4 * MZ,
+            bytes_accessed=2 * len(fields) * channels * rows * NZ,
+            transcendentals=0,
+        ),
+        name="forward_e" if cot else "forward_u",
+    )(*fields, z_forward_table(), x_forward_table(spaces))
+
+
+def unfold_y(received_ref, high, low, lines, store, groups, kx_local):
+    width = kx_local * 2 * MY
+    for g in range(groups):
+        data = received_ref[:, g].reshape(-1, LANES)
+        found = dot_split(high[...], low[...], data)
+        for part in range(2):
+            lines[part, g * LANES : (g + 1) * LANES, :] = found[
+                part * width : (part + 1) * width, :
+            ].T
+    channels = groups * GROUP
+    for part in range(2):
+        for kz in range(MZ):
+            piece = lines[part, pl.ds(kz, channels, stride=MZ), :]
+            for j in range(kx_local):
+                store(
+                    part,
+                    (j * MZ + kz) * 2 * MY,
+                    piece[:, j * 2 * MY : (j + 1) * 2 * MY],
+                )
+
+
+def spectrum_u(received_ref, high, low, hat_ref, lines, *, groups, kx_local):
+    def store(part, column, values):
+        hat_ref[part, :, column : column + 2 * MY] = values
+
+    unfold_y(received_ref, high, low, lines, store, groups, kx_local)
+
+
+def finish_u(received, kx_local):
+    spaces, groups, rows, _ = received.shape
+    channels = groups * GROUP
+    modes = kx_local * MZ * 2 * MY
+    high, low = y_forward_table(kx_local)
+    return pl.pallas_call(
+        functools.partial(spectrum_u, groups=groups, kx_local=kx_local),
+        out_shape=jax.ShapeDtypeStruct((2, channels, modes), F32),
+        scratch_shapes=[pltpu.VMEM((2, channels * MZ, kx_local * 2 * MY), F32)],
+        compiler_params=pltpu.CompilerParams(vmem_limit_bytes=VMEM_LIMIT),
+        name="finish_u",
+    )(received, high, low)
+
+
+def spectrum_e(
+    received_ref,
+    weight_ref,
+    high,
+    low,
+    inv_high,
+    inv_low,
+    hat_ref,
+    send_ref,
+    lines,
+    rounded,
+    back,
+    *,
+    groups,
+    kx_local,
+    per_step,
+):
+    step = pl.program_id(0)
+    channels = groups * GROUP
+    modes = kx_local * MZ * 2 * MY
+    width = kx_local * 2 * MY
+
+    @pl.when(step == 0)
+    def _():
+        def store(part, column, values):
+            hat_ref[part, :, column : column + 2 * MY] = values
+            kz = (column // (2 * MY)) % MZ
+            scale = (1.0 if kz == 0 else 2.0) / float(NX * NY * NZ)
+            rounded[part, :, column : column + 2 * MY] = values.astype(BF16).astype(F32) * scale
+
+        unfold_y(received_ref, high, low, lines, store, groups, kx_local)
+
+    tile = min(modes, 512)
+    for i in range(per_step):
+        for start in range(0, modes, tile):
+            lane = slice(start, start + tile)
+            real = rounded[0, :, lane]
+            imag = rounded[1, :, lane]
+            weight_real = weight_ref[0, i, :, lane].astype(F32)
+            weight_imag = weight_ref[1, i, :, lane].astype(F32)
+            row = step * per_step + i
+            back[0, pl.ds(row, 1), lane] = jnp.sum(
+                weight_real * real + weight_imag * imag, axis=0, keepdims=True
+            )
+            back[1, pl.ds(row, 1), lane] = jnp.sum(
+                weight_real * imag - weight_imag * real, axis=0, keepdims=True
+            )
+
+    @pl.when(step == pl.num_programs(0) - 1)
+    def _():
+        for part in range(2):
+            for kz in range(MZ):
+                pieces = [
+                    back[part, :, (j * MZ + kz) * 2 * MY : (j * MZ + kz + 1) * 2 * MY]
+                    for j in range(kx_local)
+                ]
+                lines[part, pl.ds(kz, channels, stride=MZ), :] = jnp.concatenate(pieces, axis=1)
+        for g in range(groups):
+            data = jnp.concatenate(
+                [lines[part, g * LANES : (g + 1) * LANES, :].T for part in range(2)], axis=0
+            )
+            found = dot_split(inv_high[...], inv_low[...], data)
+            send_ref[:, g] = found.reshape(send_ref.shape[0], -1, LANES)
+
+
+def finish_e(received, weight, kx_local):
+    spaces, groups, rows, _ = received.shape
+    channels = groups * GROUP
+    modes = kx_local * MZ * 2 * MY
+    per_step = 4
+    high, low = y_forward_table(kx_local)
+    inv_high, inv_low = y_inverse_table(kx_local)
+    return pl.pallas_call(
+        functools.partial(spectrum_e, groups=groups, kx_local=kx_local, per_step=per_step),
+        out_shape=(
+            jax.ShapeDtypeStruct((2, channels, modes), F32),
+            jax.ShapeDtypeStruct(received.shape, F32),
+        ),
+        grid=(channels // per_step,),
+        in_specs=[
+            whole(received.shape),
+            pl.BlockSpec((2, per_step, channels, modes), lambda i: (0, i, 0, 0)),
+            whole(high.shape),
+            whole(low.shape),
+            whole(inv_high.shape),
+            whole(inv_low.shape),
+        ],
+        out_specs=(whole((2, channels, modes)), whole(received.shape)),
+        scratch_shapes=[
+            pltpu.VMEM((2, channels * MZ, kx_local * 2 * MY), F32),
+            pltpu.VMEM((2, channels, modes), F32),
+            pltpu.VMEM((2, channels, modes), F32),
+        ],
+        compiler_params=params(),
+        name="finish_e",
+    )(received, weight, high, low, inv_high, inv_low)
+
+
+def mix_body(input_ref, cot_ref, spread_ref, mixed_ref, skip_ref, total, *, planes, count):
+    step = pl.program_id(0)
+    channels = input_ref.shape[0]
+    side = channels * planes
+
+    @pl.when(step == 0)
+    def _():
+        total[...] = jnp.zeros_like(total)
+
+    cots, lefts = [], []
+    for k in range(count):
+        rows = slice(k * planes, (k + 1) * planes)
+        cots.append(cot_ref[:, rows, :].reshape(side, NZ))
+        lefts.append(input_ref[:, rows, :].reshape(side, NZ))
+    cot = jnp.concatenate(cots, axis=1)
+    left = jnp.concatenate(lefts, axis=1)
+    total[...] += lax.dot_general(
+        left, cot, (((1,), (1,)), ((), ())), preferred_element_type=F32
+    )
+    mixed = dot(spread_ref[...], cot).astype(BF16)
+    for k in range(count):
+        mixed_ref[:, k * planes : (k + 1) * planes, :] = mixed[
+            :, k * NZ : (k + 1) * NZ
+        ].reshape(channels, planes, NZ)
+
+    @pl.when(step == pl.num_programs(0) - 1)
+    def _():
+        row = lax.broadcasted_iota(jnp.int32, (side, side), 0)
+        column = lax.broadcasted_iota(jnp.int32, (side, side), 1)
+        kept = jnp.where(row % planes == column % planes, total[...], 0.0)
+        pick = (
+            lax.broadcasted_iota(jnp.int32, (side, channels), 0) // planes
+            == lax.broadcasted_iota(jnp.int32, (side, channels), 1)
+        ).astype(F32)
+        half = lax.dot_general(
+            kept, pick, (((1,), (0,)), ((), ())), precision=lax.Precision.HIGHEST,
+            preferred_element_type=F32,
+        )
+        skip_ref[...] = lax.dot_general(
+            pick, half, (((0,), (0,)), ((), ())), precision=lax.Precision.HIGHEST,
+            preferred_element_type=F32,
+        )
+
+
+def mix(inputs, cot, spread, planes):
+    channels, rows, _ = inputs.shape
+    count = 4
+    side = channels * planes
+    spec = pl.BlockSpec((channels, count * planes, NZ), lambda x: (0, x, 0))
+    return pl.pallas_call(
+        functools.partial(mix_body, planes=planes, count=count),
+        out_shape=(
+            jax.ShapeDtypeStruct(inputs.shape, BF16),
+            jax.ShapeDtypeStruct((channels, channels), F32),
+        ),
+        grid=(NX // count,),
+        in_specs=[spec, spec, whole((side, side))],
+        out_specs=(spec, whole((channels, channels))),
+        scratch_shapes=[pltpu.VMEM((side, side), F32)],
+        compiler_params=params(),
+        cost_estimate=pl.CostEstimate(
+            flops=4 * NX * side * side * NZ,
+            bytes_accessed=6 * channels * rows * NZ,
+            transcendentals=0,
+        ),
+        name="mix",
+    )(inputs, cot, spread)
+
+
+def to_grid_body(
+    received_ref, mixed_ref, table_x, table_z, out_ref, real_ref, imag_ref, *, planes, spaces
+):
+    part = 4 * MX // spaces
+    rows = NX * planes
+    for y in range(0, planes, 2):
+        pair = [
+            jnp.concatenate(
+                [received_ref[s, 0, at * part : (at + 1) * part, :] for s in range(spaces)], axis=0
+            ).astype(BF16)
+            for at in (y, y + 1)
+        ]
+        found = dot(table_x[...], jnp.concatenate(pair, axis=1))
+        for place in range(2):
+            lane = slice(place * LANES, (place + 1) * LANES)
+            real_ref[pl.ds(y + place, NX, stride=planes), :] = found[:NX, lane]
+            imag_ref[pl.ds(y + place, NX, stride=planes), :] = found[NX:, lane]
+    step = min(rows, 256)
+    for start in range(0, rows, step):
+        line = jnp.concatenate(
+            [real_ref[start : start + step, :], imag_ref[start : start + step, :]], axis=1
+        ).astype(BF16)
+        found = dot(line, table_z[...])
+        for c in range(GROUP):
+            mixed = mixed_ref[c, start : start + step, :].astype(F32)
+            out_ref[c, start : start + step, :] = (
+                found[:, c * NZ : (c + 1) * NZ] + mixed
+            ).astype(BF16)
+
+
+def grid_of(received, mixed, planes):
+    spaces, groups, rows, _ = received.shape
+    spec = pl.BlockSpec((GROUP, NX * planes, NZ), lambda g: (g, 0, 0))
+    return pl.pallas_call(
+        functools.partial(to_grid_body, planes=planes, spaces=spaces),
+        out_shape=jax.ShapeDtypeStruct(mixed.shape, BF16),
+        grid=(groups,),
+        in_specs=[
+            pl.BlockSpec((spaces, 1, rows, LANES), lambda g: (0, g, 0, 0)),
+            spec,
+            whole((2 * NX, 4 * MX)),
+            whole((2 * LANES, GROUP * NZ)),
+        ],
+        out_specs=spec,
+        scratch_shapes=[
+            pltpu.VMEM((NX * planes, LANES), F32),
+            pltpu.VMEM((NX * planes, LANES), F32),
+        ],
+        input_output_aliases={1: 0},
+        compiler_params=params(),
+        name="to_grid",
+    )(received, mixed, x_inverse_table(spaces), z_inverse_table())
+
+
+def cross_body(left_ref, right_ref, out_ref, *, samples):
+    lanes = out_ref.shape[-1]
+    channels = left_ref.shape[2]
+    own = right_ref.shape[2]
+    kz = lax.broadcasted_iota(jnp.int32, (own, lanes), 1) // (2 * MY) % MZ
+    scale = jnp.where(kz == 0, 1.0, 2.0) / float(NX * NY * NZ)
+    rights = [
+        (right_ref[b, 0] * scale, right_ref[b, 1] * scale) for b in range(samples)
+    ]
+    for i in range(channels):
+        real = imag = None
+        for b in range(samples):
+            left_real = left_ref[b, 0, i : i + 1, :]
+            left_imag = left_ref[b, 1, i : i + 1, :]
+            right_real, right_imag = rights[b]
+            one = left_real * right_real + left_imag * right_imag
+            two = left_real * right_imag - left_imag * right_real
+            real = one if real is None else real + one
+            imag = two if imag is None else imag + two
+        out_ref[0, i] = real
+        out_ref[1, i] = imag
+
+
+def cross(left, right):
+    samples, _, channels, modes = left.shape
+    own = right.shape[2]
+    lanes = 2 * MY * MZ
+    return pl.pallas_call(
+        functools.partial(cross_body, samples=samples),
+        out_shape=jax.ShapeDtypeStruct((2, channels, own, modes), F32),
+        grid=(modes // lanes,),
+        in_specs=[
+            pl.BlockSpec((samples, 2, channels, lanes), lambda k: (0, 0, 0, k)),
+            pl.BlockSpec((samples, 2, own, lanes), lambda k: (0, 0, 0, k)),
+        ],
+        out_specs=pl.BlockSpec((2, channels, own, lanes), lambda k: (0, 0, 0, k)),
+        compiler_params=params(),
+        name="cross",
+    )(left, right)
+
+
+def exchange(values):
+    return lax.all_to_all(values, "space", split_axis=0, concat_axis=0, tiled=True)
 
 
 HIGHEST = lax.Precision.HIGHEST
@@ -40,12 +531,6 @@
     )
 
 
-def gelu_slope(values):
-    normal_cdf = 0.5 * (1.0 + jax.scipy.special.erf(values * (1.0 / math.sqrt(2.0))))
-    density = jnp.exp(-0.5 * values * values) * (1.0 / math.sqrt(2.0 * math.pi))
-    return normal_cdf + values * density
-
-
 def local_spectrum(grid_in):
     cos_x, sin_x = phase_table(NX, 2 * MX, True)
     table_x = jnp.stack([cos_x, -sin_x], axis=1).astype(jnp.bfloat16)
@@ -112,10 +597,10 @@
     return summed / math.sqrt(grid_in.shape[0] * lax.axis_size("batch") * NX * NY * NZ)
 
 
-def on_device(inputs, pre_act, cotangent, spectral_weight, skip_weight):
+def general(inputs, pre_act, cotangent, spectral_weight, skip_weight):
     samples = inputs.shape[0]
     channels = inputs.shape[1]
-    slope_pre = gelu_slope(pre_act.astype(jnp.float32))
+    slope_pre = slope(pre_act.astype(jnp.float32))
     cot_pre = (cotangent.astype(jnp.float32) * slope_pre).astype(jnp.bfloat16)
     spec_u, spec_e = both_along_y(
         (
@@ -153,6 +638,41 @@
     return (grad_inputs, grad_spectral, grad_skip)
 
 
+def on_device(inputs, pre_act, cotangent, spectral_weight, skip_weight):
+    samples, channels, _, planes, _ = inputs.shape
+    spaces = lax.axis_size("space")
+    batches = lax.axis_size("batch")
+    if samples != 1 or (2 * MX) % spaces or planes % 16 or channels % GROUP:
+        return general(inputs, pre_act, cotangent, spectral_weight, skip_weight)
+    kx_local = 2 * MX // spaces
+    flat = (channels, NX * planes, NZ)
+    inputs, pre_act, cotangent = (v.reshape(flat) for v in (inputs, pre_act, cotangent))
+    (send_u,) = forward((inputs,), planes, spaces, False)
+    received_u = exchange(send_u)
+    send_e, cot_pre = forward((pre_act, cotangent), planes, spaces, True)
+    received_e = exchange(send_e)
+    spread = jnp.einsum("io,yv->iyov", skip_weight, jnp.eye(planes, dtype=BF16))
+    spread = spread.reshape(channels * planes, channels * planes)
+    mixed, skip_part = mix(inputs, cot_pre, spread, planes)
+    skip_all = lax.all_gather(skip_part, ("batch", "space"))
+    hat_u = finish_u(received_u, kx_local)
+    all_u = lax.all_gather(hat_u, "batch")
+    hat_e, send_back = finish_e(received_e, spectral_weight, kx_local)
+    own = channels // batches
+    modes = hat_e.shape[-1]
+    parts_e = hat_e.reshape(2, batches, own, modes).swapaxes(0, 1)
+    own_e = lax.all_to_all(parts_e, "batch", split_axis=0, concat_axis=0, tiled=True)
+    received_back = exchange(send_back)
+    grad_spectral = cross(all_u, own_e)
+    grad_inputs = grid_of(received_back, mixed, planes)
+    grad_skip = jnp.sum(skip_all, axis=0) / math.sqrt(samples * batches * NX * NY * NZ)
+    return (
+        grad_inputs.reshape(samples, channels, NX, planes, NZ),
+        grad_spectral,
+        grad_skip,
+    )
+
+
 def solution(mesh):
     placed = (
         P("batch", None, None, "space", None),

time: 562 us -> 314 us (0.56)
  matrix products: 256 us -> 0 us
  local copies, waits for them, and re-layouts: 143 us -> 12.1 us
  Pallas kernels: 0 us -> 117 us
  other arithmetic: 65.2 us -> 3.03 us
  waiting for transfers between devices: 17.9 us -> 69 us
  blocking collectives: 41.4 us -> 82.1 us
    dot_general x11 -> x0, matrix products: 256 us -> none  [the longest x2 87.3 us: local_spectrum(): jnp.einsum('scpayz,pzqk->scqyak', section_x, forward_block(cos_z, sin_z),...]
    pallas_call x0 -> x7, Pallas kernels: none -> 117 us  [the longest x1 38.7 us: mix(): pl.pallas_call(functools.partial(mix_body, planes=planes, count=count), o...]
    all_gather x0 -> x1, blocking collectives: none -> 70.2 us  [on_device(): skip_all = lax.all_gather(skip_part, ('batch', 'space'))]
    unnamed x12 -> x8, local copies, waits for them, and re-layouts: 59.9 us -> 2.65 us
    all_to_all x3, waiting for transfers between devices: 17.9 us -> 68.9 us  [exchange(): lax.all_to_all(values, 'space', split_axis=0, concat_axis=0, tiled=True)]
    psum x1 -> x0, blocking collectives: 41.4 us -> none  [skip_gradient(): summed = lax.psum(partial_sum, ('batch', 'space'))]
    all_to_all x7 -> x0, local copies, waits for them, and re-layouts: 35.8 us -> none  [the longest x2 13.7 us: on_device(): lax.all_to_all(grid_y, 'space', split_axis=3, concat_axis=4, tiled=True)]
    all_to_all x3 -> x0, other arithmetic: 22 us -> none  [the longest x1 7.34 us: on_device(): lax.all_to_all(grid_y, 'space', split_axis=3, concat_axis=4, tiled=True)]
  transfers between devices with their start and end apart: 4 -> 4, of which waited for: 1 -> 2; matrix products, arithmetic and copies ran while one was open for 58% -> 4% of each run, Pallas kernels for 0% -> 24%
where the time goes in v1:
time: 314 us; the launch traced here: 312 us
  Pallas kernels  117 us (37%)
  blocking collectives  82.1 us (26%)
  waiting for transfers between devices  69 us (22%)
  starting transfers between devices  14.9 us (5%)
  between operations  14.1 us (4%)
  local copies, waits for them, and re-layouts  12.1 us (4%)
    all_gather x1, blocking collectives, on_device(): skip_all = lax.all_gather(skip_part, ('batch', 'space'))  70.2 us
    all_to_all x3, waiting for transfers between devices, exchange(): lax.all_to_all(values, 'space', split_axis=0, concat_axis=0, tiled=True)  68.9 us
    pallas_call x1, Pallas kernels, mix(): pl.pallas_call(functools.partial(mix_body, planes=planes, count=count), o...  38.7 us
    pallas_call x2, Pallas kernels, forward(): pl.pallas_call(functools.partial(forward_cot if cot else forward_plain, p...  36.3 us
    pallas_call x1, Pallas kernels, grid_of(): pl.pallas_call(functools.partial(to_grid_body, planes=planes, spaces=spac...  16.1 us
    pallas_call x1, Pallas kernels, finish_e(): pl.pallas_call(functools.partial(spectrum_e, groups=groups, kx_local=kx_l...  15.3 us
    all_to_all x3, starting transfers between devices, exchange(): lax.all_to_all(values, 'space', split_axis=0, concat_axis=0, tiled=True)  14.7 us
    all_to_all x1, blocking collectives, on_device(): lax.all_to_all(parts_e, 'batch', split_axis=0, concat_axis=0, tiled=True)  11.9 us
  transfers between devices with their start and end apart: 4, of which 2 were waited for; matrix products, arithmetic and copies ran while one was open for 4% of the time, Pallas kernels for 24%

profile of v1, /device:TPU:0, one launch (start us, length us, event | category | flops | bytes accessed | tf_op | source)
XLA Modules:
  0.0 312.1 jit_solution(7267402661724188066)
XLA Ops:
  7.2 24.9 %forward_e.1 = (f32[8,4,128,128]{3,2,1,0:T(8,128)}, bf16[32,2048,128]{2,1,0:T(8,128)(2,1)}) custom-call(bf16[32,2048,128]{2,1,0:T(8,128)(2,1)} %bitcast.15, bf16[32,2048,128]{2,1,0:T(8,128)(2,1)} %bitcast.16, bf16[1024,256]{1,0:T(8,128)(2,1)} %constant.21.clone.table_z, bf16[64,256]{1,0:T(8,128)(2,1)} %constant.22.clone.table_x), custom_call_target="tpu_custom_call" | custom-call | flops 8589934592 | bytes 33554432 | tf_op jit(solution)/shard_map/forward_e/pallas_call | solution.py:181
  32.1 7.3 %all-to-all-start = ((f32[8,4,128,128]{3,2,1,0:T(8,128)}), f32[8,4,128,128]{3,2,1,0:T(8,128)S(1)}, u32[]{:S(2)}, u32[]{:S(2)}) async-start(f32[8,4,128,128]{3,2,1,0:T(8,128)} %get-tuple-element.9), calls=%async_computation | async-start | bytes 4194304 | tf_op jit(solution)/shard_map/all_to_all | solution.py:504
  39.4 11.4 %forward_u.1 = f32[8,4,128,128]{3,2,1,0:T(8,128)} custom-call(bf16[32,2048,128]{2,1,0:T(8,128)(2,1)} %bitcast.20, bf16[1024,256]{1,0:T(8,128)(2,1)} %constant.21.clone.table_z, bf16[64,256]{1,0:T(8,128)(2,1)} %constant.22.clone.table_x), custom_call_target="tpu_custom_call" | custom-call | flops 8589934592 | bytes 16777216 | tf_op jit(solution)/shard_map/forward_u/pallas_call | solution.py:181
  50.7 36.9 %all-to-all-done.received_ref = f32[8,4,128,128]{3,2,1,0:T(8,128)S(1)} async-done(((f32[8,4,128,128]{3,2,1,0:T(8,128)}), f32[8,4,128,128]{3,2,1,0:T(8,128)S(1)}, u32[]{:S(2)}, u32[]{:S(2)}) %all-to-all-start) | async-done | bytes 2097184 | tf_op jit(solution)/shard_map/all_to_all | solution.py:504
  87.6 1.3 copy-done.2
  88.9 3.6 %all-to-all-start.2 = ((f32[8,4,128,128]{3,2,1,0:T(8,128)}), f32[8,4,128,128]{3,2,1,0:T(8,128)S(1)}, u32[]{:S(2)}, u32[]{:S(2)}) async-start(f32[8,4,128,128]{3,2,1,0:T(8,128)} %forward_u.1), calls=%async_computation.2 | async-start | bytes 4194304 | tf_op jit(solution)/shard_map/all_to_all | solution.py:504
  92.6 15.3 %finish_e.1 = (f32[2,32,2048]{2,1,0:T(8,128)}, f32[8,4,128,128]{3,2,1,0:T(8,128)}) custom-call(f32[8,4,128,128]{3,2,1,0:T(8,128)} %copy-done.2, bf16[2,32,32,2048]{3,2,1,0:T(8,128)(2,1)} %weight_ref.1, bf16[256,1024]{1,0:T(8,128)(2,1)} %constant.23.clone.high, bf16[256,1024]{1,0:T(8,128)(2,1)} %constant.24.clone.low, ...), custom_call_target="tpu_custom_call" | custom-call | tf_op jit(solution)/shard_map/finish_e/pallas_call | solution.py:313
  107.9 1.1 copy_bitcast_fusion
  108.9 32.1 %all-to-all-done.2.received_ref = f32[8,4,128,128]{3,2,1,0:T(8,128)S(1)} async-done(((f32[8,4,128,128]{3,2,1,0:T(8,128)}), f32[8,4,128,128]{3,2,1,0:T(8,128)S(1)}, u32[]{:S(2)}, u32[]{:S(2)}) %all-to-all-start.2) | async-done | bytes 2097184 | tf_op jit(solution)/shard_map/all_to_all | solution.py:504
  141.0 11.9 %all_to_all.20.right_ref = f32[4,2,8,2048]{3,2,1,0:T(8,128)} all-to-all(f32[4,2,8,2048]{3,2,1,0:T(8,128)S(1)} %copy_bitcast_fusion), channel_id=1, replica_groups=mesh['batch'=4,'space'=8] {'batch'}, dimensions={0} | all-to-all | bytes 1048576 | tf_op jit(solution)/shard_map/all_to_all | solution.py:664
  152.9 3.8 %all-to-all-start.1 = ((f32[8,4,128,128]{3,2,1,0:T(8,128)}), f32[8,4,128,128]{3,2,1,0:T(8,128)S(1)}, u32[]{:S(2)}, u32[]{:S(2)}) async-start(f32[8,4,128,128]{3,2,1,0:T(8,128)} %get-tuple-element.10), calls=%async_computation.1 | async-start | bytes 4194304 | tf_op jit(solution)/shard_map/all_to_all | solution.py:504
  156.7 0.2 all-gather.4.cloned.1.call-start
  156.9 4.8 %finish_u.1 = f32[2,32,2048]{2,1,0:T(8,128)} custom-call(f32[8,4,128,128]{3,2,1,0:T(8,128)} %copy-done.1, bf16[256,1024]{1,0:T(8,128)(2,1)} %constant.23.clone.high, bf16[256,1024]{1,0:T(8,128)(2,1)} %constant.24.clone.low), custom_call_target="tpu_custom_call" | custom-call | tf_op jit(solution)/shard_map/finish_u/pallas_call | solution.py:232
  161.7 0.0 all-gather.4.cloned.1.call-update
  161.7 2.4 multiply_bitcast_fusion
  164.1 8.4 %reshape.27.spread_ref = bf16[512,512]{1,0:T(8,128)(2,1)} reshape(bf16[32,16,32,16]{3,2,1,0:T(8,128)(2,1)} %multiply_bitcast_fusion) | data formatting | bytes 1048576 | tf_op jit(solution)/shard_map/reshape | solution.py:655
  172.5 38.7 %mix.1 = (bf16[32,2048,128]{2,1,0:T(8,128)(2,1)}, f32[32,32]{1,0:T(8,128)}) custom-call(bf16[32,2048,128]{2,1,0:T(8,128)(2,1)} %bitcast.21, bf16[32,2048,128]{2,1,0:T(8,128)(2,1)} %get-tuple-element.11.cot_ref, bf16[512,512]{1,0:T(8,128)(2,1)} %reshape.27.spread_ref), custom_call_target="tpu_custom_call" | custom-call | flops 17179869184 | bytes 50331648 | tf_op jit(solution)/shard_map/mix/pallas_call | solution.py:388
  211.2 70.2 %all-gather.1 = f32[1024,32]{1,0:T(8,128)S(1)} all-gather(f32[32,32]{1,0:T(8,128)} %get-tuple-element.14), channel_id=3, replica_groups=mesh['batch'=4,'space'=8] {'batch','space'}, dimensions={0}, use_global_device_ids=true | all-gather | bytes 135168 | tf_op jit(solution)/shard_map/all_gather | solution.py:657
  281.4 0.1 reduce_sum.9
  281.5 0.6 broadcast_multiply_fusion
  282.1 5.7 %cross.1 = f32[2,32,8,2048]{3,2,1,0:T(8,128)} custom-call(f32[4,2,32,2048]{3,2,1,0:T(8,128)} %bitcast.18, f32[4,2,8,2048]{3,2,1,0:T(8,128)} %all_to_all.20.right_ref), custom_call_target="tpu_custom_call" | custom-call | tf_op jit(solution)/shard_map/cross/pallas_call | solution.py:489
  287.8 0.0 all-to-all-done.1.received_ref
  287.8 1.3 copy-done
  289.1 16.1 %to_grid.1 = bf16[32,2048,128]{2,1,0:T(8,128)(2,1)} custom-call(f32[8,4,128,128]{3,2,1,0:T(8,128)} %copy-done, bf16[32,2048,128]{2,1,0:T(8,128)(2,1)} %get-tuple-element.12.mixed_ref, bf16[256,64]{1,0:T(8,128)(2,1)} %constant.27.clone.table_x, bf16[256,1024]{1,0:T(8,128)(2,1)} %constant.28.clone.table_z), custom_call_target="tpu_custom_call", output_to_operand_aliasing={{}: (1, {})} | custom-call | tf_op jit(solution)/shard_map/to_grid/pallas_call | solution.py:441
  (8 shorter events, 0.0 us)
Async XLA Ops:
  32.1 55.5 %all-to-all-start = ((f32[8,4,128,128]{3,2,1,0:T(8,128)}), f32[8,4,128,128]{3,2,1,0:T(8,128)S(1)}, u32[]{:S(2)}, u32[]{:S(2)}) async-start(f32[8,4,128,128]{3,2,1,0:T(8,128)} %get-tuple-element.9), calls=%async_computation | async-start | bytes 4194304 | tf_op jit(solution)/shard_map/all_to_all | solution.py:504
  87.6 1.3 copy-start.2
  88.9 52.1 %all-to-all-start.2 = ((f32[8,4,128,128]{3,2,1,0:T(8,128)}), f32[8,4,128,128]{3,2,1,0:T(8,128)S(1)}, u32[]{:S(2)}, u32[]{:S(2)}) async-start(f32[8,4,128,128]{3,2,1,0:T(8,128)} %forward_u.1), calls=%async_computation.2 | async-start | bytes 4194304 | tf_op jit(solution)/shard_map/all_to_all | solution.py:504
  141.0 11.9 %copy-start.1 = (f32[8,4,128,128]{3,2,1,0:T(8,128)}, f32[8,4,128,128]{3,2,1,0:T(8,128)S(1)}, u32[]{:S(2)}) copy-start(f32[8,4,128,128]{3,2,1,0:T(8,128)S(1)} %all-to-all-done.2.received_ref) | copy-start | bytes 6291460
  152.9 8.8 %copy-start.3 = (bf16[32,32]{1,0:T(8,128)(2,1)S(1)}, bf16[32,32]{1,0:T(8,128)(2,1)}, u32[]{:S(2)}) copy-start(bf16[32,32]{1,0:T(8,128)(2,1)} %param.21) | copy-start | bytes 6148
  152.9 134.9 %all-to-all-start.1 = ((f32[8,4,128,128]{3,2,1,0:T(8,128)}), f32[8,4,128,128]{3,2,1,0:T(8,128)S(1)}, u32[]{:S(2)}, u32[]{:S(2)}) async-start(f32[8,4,128,128]{3,2,1,0:T(8,128)} %get-tuple-element.10), calls=%async_computation.1 | async-start | bytes 4194304 | tf_op jit(solution)/shard_map/all_to_all | solution.py:504
  156.7 125.4 %all-gather.4.cloned.1.call-start = ((), (), s32[]{:S(2)}) async-start(), calls=%async_computation.4 | async-start | bytes 2621440 | tf_op jit(solution)/shard_map/all_gather | solution.py:659
  287.8 1.3 copy-start
Sparse Core Ops, SparseCore 0:
  161.8 22.8 all-gather.3

commit v2 on v0

--- a/solution.py
+++ b/solution.py
@@ -1,8 +1,13 @@
+import functools
 import math
 
 import jax
 import jax.numpy as jnp
+import ml_dtypes
+import numpy as np
 from jax import lax
+from jax.experimental import pallas as pl
+from jax.experimental.pallas import tpu as pltpu
 from jax.sharding import PartitionSpec as P
 
 NX = 128
@@ -11,6 +16,766 @@
 MX = 16
 MY = 16
 MZ = 16
+GROUP = 8
+LANES = GROUP * MZ
+BF16 = jnp.bfloat16
+F32 = jnp.float32
+VMEM_LIMIT = 56 * 1024 * 1024
+
+
+def cost(microseconds):
+    return pl.CostEstimate(flops=int(microseconds * 2e9), bytes_accessed=1, transcendentals=0)
+
+
+def waves(length, count, signed):
+    points = np.arange(length)
+    orders = np.arange(count)
+    if signed:
+        orders = np.where(orders < count // 2, orders, orders - count)
+    radians = np.mod(points[:, None] * orders[None, :], length) * (2.0 * math.pi / length)
+    return np.cos(radians), np.sin(radians)
+
+
+def rounded_table(table):
+    return np.asarray(table, np.float32).astype(ml_dtypes.bfloat16)
+
+
+def z_forward_table():
+    cos, sin = waves(NZ, MZ, False)
+    table = np.zeros((GROUP, NZ, 2, GROUP, MZ))
+    for c in range(GROUP):
+        table[c, :, 0, c, :] = cos
+        table[c, :, 1, c, :] = -sin
+    return jnp.asarray(rounded_table(table.reshape(GROUP * NZ, 2 * LANES)))
+
+
+def z_inverse_table():
+    cos, sin = waves(NZ, MZ, False)
+    table = np.zeros((2, GROUP, MZ, GROUP, NZ))
+    for c in range(GROUP):
+        table[0, c, :, c, :] = cos.T
+        table[1, c, :, c, :] = -sin.T
+    return jnp.asarray(rounded_table(table.reshape(2 * LANES, GROUP * NZ)))
+
+
+def x_forward_table(spaces):
+    cos, sin = waves(NX, 2 * MX, True)
+    cos = cos.T.reshape(spaces, 2 * MX // spaces, NX)
+    sin = sin.T.reshape(spaces, 2 * MX // spaces, NX)
+    table = np.stack([np.stack([cos, sin], axis=2), np.stack([-sin, cos], axis=2)], axis=1)
+    return jnp.asarray(rounded_table(table.reshape(4 * MX, 2 * NX)))
+
+
+def x_inverse_table(spaces):
+    cos, sin = waves(NX, 2 * MX, True)
+    cos = cos.reshape(NX, spaces, 2 * MX // spaces)
+    sin = sin.reshape(NX, spaces, 2 * MX // spaces)
+    table = np.stack([np.stack([cos, -sin], axis=2), np.stack([sin, cos], axis=2)], axis=0)
+    return jnp.asarray(rounded_table(table.reshape(2 * NX, 4 * MX)))
+
+
+def split_table(table):
+    high = rounded_table(table)
+    low = rounded_table(table - high.astype(np.float64))
+    return jnp.asarray(np.concatenate([high, high, low], axis=-1))
+
+
+def y_forward_table(kx_local):
+    cos, sin = waves(NY, 2 * MY, True)
+    table = np.zeros((2, kx_local, 2 * MY, NY, 2, kx_local))
+    for j in range(kx_local):
+        table[0, j, :, :, 0, j] = cos.T
+        table[0, j, :, :, 1, j] = sin.T
+        table[1, j, :, :, 0, j] = -sin.T
+        table[1, j, :, :, 1, j] = cos.T
+    table = table.reshape(4 * MY * kx_local, 2, NY * kx_local)
+    return split_table(table.swapaxes(0, 1))
+
+
+def y_inverse_table(kx_local):
+    cos, sin = waves(NY, 2 * MY, True)
+    table = np.zeros((NY, 2, kx_local, 2, kx_local, 2 * MY))
+    for j in range(kx_local):
+        table[:, 0, j, 0, j, :] = cos
+        table[:, 0, j, 1, j, :] = -sin
+        table[:, 1, j, 0, j, :] = sin
+        table[:, 1, j, 1, j, :] = cos
+    return split_table(table.reshape(2, NY * kx_local, 4 * MY * kx_local))
+
+
+def dot(left, right):
+    return lax.dot_general(left, right, (((1,), (0,)), ((), ())), preferred_element_type=F32)
+
+
+def dot_split(table, values):
+    high = values.astype(BF16)
+    low = (values - high.astype(F32)).astype(BF16)
+    return dot(table, jnp.concatenate([high, low, high], axis=0))
+
+
+def params(count=1):
+    return pltpu.CompilerParams(
+        vmem_limit_bytes=VMEM_LIMIT, dimension_semantics=("arbitrary",) * count
+    )
+
+
+def z_then_x(load, table_z, table_x, send_ref, real_ref, imag_ref, planes, spaces, blocks):
+    rows = NX * planes // blocks
+    block = pl.program_id(1)
+    step = min(rows, 512)
+    for start in range(0, rows, step):
+        line = jnp.concatenate([load(c, start, step) for c in range(GROUP)], axis=1)
+        found = dot(line, table_z[...])
+        place = pl.ds(pl.multiple_of(block * rows + start, step), step)
+        real_ref[place, :] = found[:, :LANES]
+        imag_ref[place, :] = found[:, LANES:]
+    part = 4 * MX // spaces
+
+    @pl.when(block == blocks - 1)
+    def _():
+        for y in range(0, planes, 2):
+            pair = []
+            for at in (y, y + 1):
+                real = real_ref[pl.ds(at, NX, stride=planes), :]
+                imag = imag_ref[pl.ds(at, NX, stride=planes), :]
+                pair.append(jnp.concatenate([real, imag], axis=0).astype(BF16))
+            found = dot(table_x[...], jnp.concatenate(pair, axis=1))
+            for place in range(2):
+                for s in range(spaces):
+                    relay, side = s % (spaces // 2), s // (spaces // 2)
+                    rows_of = slice((y + place) * part, (y + place + 1) * part)
+                    send_ref[relay, side, rows_of, :] = found[
+                        s * part : (s + 1) * part, place * LANES : (place + 1) * LANES
+                    ]
+
+
+def forward_plain(
+    field_ref, table_z, table_x, *refs, planes, spaces, blocks
+):
+    send_ref, real_ref, imag_ref = refs[-3:]
+
+    def load(c, start, step):
+        return field_ref[c, start : start + step, :]
+
+    z_then_x(load, table_z, table_x, send_ref, real_ref, imag_ref, planes, spaces, blocks)
+
+
+def slope(values):
+    normal_cdf = 0.5 * (1.0 + lax.erf(values * (1.0 / math.sqrt(2.0))))
+    density = jnp.exp(-0.5 * values * values) * (1.0 / math.sqrt(2.0 * math.pi))
+    return normal_cdf + values * density
+
+
+def forward_cot(pre_ref, cot_ref, table_z, table_x, *refs, planes, spaces, blocks):
+    send_ref, out_ref, real_ref, imag_ref = refs[-4:]
+
+    def load(c, start, step):
+        pre = pre_ref[c, start : start + step, :].astype(F32)
+        cot = cot_ref[c, start : start + step, :].astype(F32)
+        made = (cot * slope(pre)).astype(BF16)
+        out_ref[c, start : start + step, :] = made
+        return made
+
+    z_then_x(load, table_z, table_x, send_ref, real_ref, imag_ref, planes, spaces, blocks)
+
+
+def whole(shape):
+    return pl.BlockSpec(shape, lambda *_: (0,) * len(shape))
+
+
+ANYWHERE = pl.BlockSpec(memory_space=pl.ANY)
+
+
+def forward(fields, first, groups, planes, spaces, cot, after=()):
+    channels, rows, _ = fields[0].shape
+    blocks = 1
+    part = 4 * MX // spaces
+    field_spec = pl.BlockSpec((GROUP, rows // blocks, NZ), lambda g, r: (g + first, r, 0))
+    send_shape = jax.ShapeDtypeStruct((spaces // 2, 2, groups * planes * part, LANES), F32)
+    send_spec = pl.BlockSpec((spaces // 2, 2, planes * part, LANES), lambda g, r: (0, 0, g, 0))
+    out_shape, out_specs = (send_shape,), (send_spec,)
+    if cot:
+        out_shape += (jax.ShapeDtypeStruct(fields[0].shape, BF16),)
+        out_specs += (field_spec,)
+    body = forward_cot if cot else forward_plain
+    return pl.pallas_call(
+        functools.partial(body, planes=planes, spaces=spaces, blocks=blocks),
+        out_shape=out_shape,
+        grid=(groups, blocks),
+        in_specs=[field_spec] * len(fields)
+        + [whole((GROUP * NZ, 2 * LANES)), whole((4 * MX, 2 * NX))]
+        + [ANYWHERE] * len(after),
+        out_specs=out_specs,
+        scratch_shapes=[pltpu.VMEM((rows, LANES), F32), pltpu.VMEM((rows, LANES), F32)],
+        compiler_params=params(2),
+        cost_estimate=cost(25 if cot else 11),
+        name="forward_e" if cot else "forward_u",
+    )(*fields, z_forward_table(), x_forward_table(spaces), *after)
+
+
+def half_sums(near_ref, table, g, count):
+    relays = near_ref.shape[0]
+    per_group = table.shape[2] // 3 // relays
+    data = jnp.concatenate(
+        [
+            jnp.concatenate(
+                [
+                    near_ref[r, 0, at * per_group : (at + 1) * per_group, :]
+                    for at in range(g, g + count)
+                ],
+                axis=1,
+            )
+            for r in range(relays)
+        ],
+        axis=0,
+    )
+    return dot_split(table[0], data)
+
+
+def partial_body(half_ref, near_ref, table, *refs):
+    out_ref = refs[-1]
+    for g in range(0, out_ref.shape[0], 2):
+        found = half_sums(near_ref, table, g, 2)
+        out_ref[g] = found[:, :LANES]
+        out_ref[g + 1] = found[:, LANES:]
+
+
+def table_spec(table, side):
+    return pl.BlockSpec((1,) + table.shape[1:], lambda *at: (side(at[-1][0]), 0, 0))
+
+
+def near_spec(near, side):
+    shape = (near.shape[0], 1) + near.shape[2:]
+    return pl.BlockSpec(shape, lambda *at: (0, side(at[-1][0]), 0, 0))
+
+
+def own_side(half):
+    return half
+
+
+def other_side(half):
+    return 1 - half
+
+
+def fixed(shape):
+    return pl.BlockSpec(shape, lambda *at: (0,) * len(shape))
+
+
+def partial_sums(half, near, groups, kx_local, name, after=()):
+    table = y_forward_table(kx_local)
+    shape = (groups, table.shape[1], LANES)
+    return pl.pallas_call(
+        partial_body,
+        out_shape=jax.ShapeDtypeStruct(shape, F32),
+        grid_spec=pltpu.PrefetchScalarGridSpec(
+            num_scalar_prefetch=1,
+            grid=(1,),
+            in_specs=[near_spec(near, other_side), table_spec(table, own_side)]
+            + [ANYWHERE] * len(after),
+            out_specs=fixed(shape),
+        ),
+        compiler_params=params(),
+        cost_estimate=cost(3),
+        name=name,
+    )(half, near, table, *after)
+
+
+def unfold_y(near_ref, far_ref, table, lines, store, kx_local):
+    width = kx_local * 2 * MY
+    groups = far_ref.shape[0]
+    channels = groups * GROUP
+    for g in range(0, groups, 2):
+        pair = half_sums(near_ref, table, g, 2)
+        for at in (g, g + 1):
+            found = pair[:, (at - g) * LANES : (at - g + 1) * LANES] + far_ref[at]
+            for part in range(2):
+                lines[part, at * LANES : (at + 1) * LANES, :] = found[
+                    part * width : (part + 1) * width, :
+                ].T
+    for part in range(2):
+        for kz in range(MZ):
+            piece = lines[part, pl.ds(kz, channels, stride=MZ), :]
+            for j in range(kx_local):
+                store(
+                    part,
+                    (j * MZ + kz) * 2 * MY,
+                    piece[:, j * 2 * MY : (j + 1) * 2 * MY],
+                )
+
+
+def fold_modes(back, lines, send_ref, kx_local):
+    channels = back.shape[1]
+    for part in range(2):
+        for kz in range(MZ):
+            pieces = [
+                back[part, :, (j * MZ + kz) * 2 * MY : (j * MZ + kz + 1) * 2 * MY]
+                for j in range(kx_local)
+            ]
+            lines[part, pl.ds(kz, channels, stride=MZ), :] = jnp.concatenate(pieces, axis=1)
+    width = kx_local * 2 * MY
+    for g in range(channels // GROUP):
+        for part in range(2):
+            row = (2 * g + part) * width
+            send_ref[row : row + width, :] = lines[part, g * LANES : (g + 1) * LANES, :].T
+
+
+SUBLANES = 8
+
+
+def spectrum_u(half_ref, near_ref, far_ref, table, skip_ref, *refs, kx_local):
+    hat_ref, lines = refs[-2:]
+    channels = skip_ref.shape[0]
+
+    def store(part, column, values):
+        hat_ref[part * channels : (part + 1) * channels, column : column + 2 * MY] = values
+
+    unfold_y(near_ref, far_ref, table, lines, store, kx_local)
+    hat_ref[2 * channels :, :] = jnp.zeros((SUBLANES, hat_ref.shape[1]), F32)
+    for k in range(channels // SUBLANES):
+        hat_ref[2 * channels :, k * LANES : (k + 1) * LANES] = skip_ref[
+            k * SUBLANES : (k + 1) * SUBLANES, :
+        ]
+
+
+def finish_u(half, near, far, skip, kx_local, after=()):
+    channels = far.shape[0] * GROUP
+    table = y_forward_table(kx_local)
+    shape = (2 * channels + SUBLANES, kx_local * MZ * 2 * MY)
+    return pl.pallas_call(
+        functools.partial(spectrum_u, kx_local=kx_local),
+        out_shape=jax.ShapeDtypeStruct(shape, F32),
+        grid_spec=pltpu.PrefetchScalarGridSpec(
+            num_scalar_prefetch=1,
+            grid=(1,),
+            in_specs=[
+                near_spec(near, own_side),
+                fixed(far.shape),
+                table_spec(table, own_side),
+                fixed(skip.shape),
+            ]
+            + [ANYWHERE] * len(after),
+            out_specs=fixed(shape),
+            scratch_shapes=[pltpu.VMEM((2, channels * MZ, kx_local * 2 * MY), F32)],
+        ),
+        compiler_params=params(),
+        cost_estimate=cost(4),
+        name="finish_u",
+    )(half, near, far, table, skip, *after)
+
+
+def mode_scale(kz):
+    return (1.0 if kz == 0 else 2.0) / float(NX * NY * NZ)
+
+
+def through_weight(weight_ref, rounded, back, per_step, modes):
+    step = pl.program_id(0)
+    for start in range(0, modes, 128):
+        lane = slice(start, start + 128)
+        real = rounded[0, :, lane]
+        imag = rounded[1, :, lane]
+        reals, imags = [], []
+        for i in range(per_step):
+            weight_real = weight_ref[0, i, :, lane].astype(F32)
+            weight_imag = weight_ref[1, i, :, lane].astype(F32)
+            reals.append(
+                jnp.sum(weight_real * real + weight_imag * imag, axis=0, keepdims=True)
+            )
+            imags.append(
+                jnp.sum(weight_real * imag - weight_imag * real, axis=0, keepdims=True)
+            )
+        rows = pl.ds(pl.multiple_of(step * per_step, per_step), per_step)
+        back[0, rows, lane] = jnp.concatenate(reals, axis=0)
+        back[1, rows, lane] = jnp.concatenate(imags, axis=0)
+
+
+def spectrum_e(half_ref, near_ref, far_ref, weight_ref, table, *refs, kx_local, per_step):
+    hat_ref, rounded, send_ref, lines, back = refs[-5:]
+
+    @pl.when(pl.program_id(0) == 0)
+    def _():
+        def store(part, column, values):
+            hat_ref[part, :, column : column + 2 * MY] = values
+            rounded[part, :, column : column + 2 * MY] = values.astype(BF16).astype(
+                F32
+            ) * mode_scale((column // (2 * MY)) % MZ)
+
+        unfold_y(near_ref, far_ref, table, lines, store, kx_local)
+
+    through_weight(weight_ref, rounded, back, per_step, kx_local * MZ * 2 * MY)
+
+    @pl.when(pl.program_id(0) == pl.num_programs(0) - 1)
+    def _():
+        fold_modes(back, lines, send_ref, kx_local)
+
+
+def spectrum_rest(rounded, weight_ref, skip_ref, send_ref, lines, back, *, kx_local, per_step):
+    through_weight(weight_ref, rounded, back, per_step, kx_local * MZ * 2 * MY)
+
+    @pl.when(pl.program_id(0) == pl.num_programs(0) - 1)
+    def _():
+        fold_modes(back, lines, send_ref, kx_local)
+        skip = jnp.sum(skip_ref[...], axis=0)
+        channels = rounded.shape[1]
+        first = send_ref.shape[0] - channels
+        for k in range(channels // SUBLANES):
+            send_ref[first + k * SUBLANES : first + (k + 1) * SUBLANES, :] = skip[
+                :, k * LANES : (k + 1) * LANES
+            ]
+
+
+def finish_e(half, near, far, weight, kx_local, after=()):
+    channels = far.shape[0] * GROUP
+    modes = kx_local * MZ * 2 * MY
+    per_step = 8
+    near_half = channels // 2
+    table = y_forward_table(kx_local)
+    spectrum = jax.ShapeDtypeStruct((2, channels, modes), F32)
+    send = jax.ShapeDtypeStruct((far.shape[0] // 2 * far.shape[1], LANES), F32)
+    return pl.pallas_call(
+        functools.partial(spectrum_e, kx_local=kx_local, per_step=per_step),
+        out_shape=(spectrum, spectrum, send),
+        grid_spec=pltpu.PrefetchScalarGridSpec(
+            num_scalar_prefetch=1,
+            grid=(near_half // per_step,),
+            in_specs=[
+                near_spec(near, own_side),
+                fixed(far.shape),
+                pl.BlockSpec((2, per_step, channels, modes), lambda i, at: (0, i, 0, 0)),
+                table_spec(table, own_side),
+            ]
+            + [ANYWHERE] * len(after),
+            out_specs=(fixed(spectrum.shape), fixed(spectrum.shape), fixed(send.shape)),
+            scratch_shapes=[
+                pltpu.VMEM((2, channels * MZ, kx_local * 2 * MY), F32),
+                pltpu.VMEM((2, near_half, modes), F32),
+            ],
+        ),
+        compiler_params=params(),
+        cost_estimate=cost(8),
+        name="finish_e",
+    )(half, near, far, weight, table, *after)
+
+
+def finish_rest(rounded, weight, all_u, kx_local):
+    _, channels, modes = rounded.shape
+    per_step = 8
+    rest = channels // 2
+    steps = rest // per_step
+    rows = rest // GROUP * 2 * kx_local * 2 * MY + channels
+    skip_block = (all_u.shape[0], SUBLANES, channels // SUBLANES * LANES)
+    send = jax.ShapeDtypeStruct((rows, LANES), F32)
+    return pl.pallas_call(
+        functools.partial(spectrum_rest, kx_local=kx_local, per_step=per_step),
+        out_shape=send,
+        grid=(steps,),
+        in_specs=[
+            whole(rounded.shape),
+            pl.BlockSpec((2, per_step, channels, modes), lambda i: (0, i + steps, 0, 0)),
+            pl.BlockSpec(skip_block, lambda i: (0, 2 * channels // SUBLANES, 0)),
+        ],
+        out_specs=whole(send.shape),
+        scratch_shapes=[
+            pltpu.VMEM((2, rest * MZ, kx_local * 2 * MY), F32),
+            pltpu.VMEM((2, rest, modes), F32),
+        ],
+        compiler_params=params(),
+        cost_estimate=cost(5),
+        name="finish_rest",
+    )(rounded, weight, all_u)
+
+
+def expand_body(half_ref, own_ref, far_ref, table, *refs, groups):
+    send_ref = refs[-1]
+    relays = send_ref.shape[0]
+    per_group = table.shape[1] // relays
+    modes = table.shape[2] // 3
+    half = half_ref[0]
+    for ref, side in ((own_ref, half), (far_ref, 1 - half)):
+        for g in range(0, groups, 2):
+            data = jnp.concatenate(
+                [ref[at * modes : (at + 1) * modes, :] for at in (g, g + 1)], axis=1
+            )
+            found = dot_split(table[0], data)
+            for r in range(relays):
+                for at in (g, g + 1):
+                    send_ref[r, side, at * per_group : (at + 1) * per_group, :] = found[
+                        r * per_group : (r + 1) * per_group,
+                        (at - g) * LANES : (at - g + 1) * LANES,
+                    ]
+    left = own_ref.shape[0] - groups * modes
+    if left:
+        total = own_ref[groups * modes :, :] + far_ref[groups * modes :, :]
+        for r in range(relays):
+            send_ref[r, 0, groups * per_group :, :] = total
+            send_ref[r, 1, groups * per_group :, :] = total
+
+
+def expand(half, own, far, relays, groups, kx_local, after=()):
+    table = y_inverse_table(kx_local)
+    left = own.shape[0] - groups * table.shape[2] // 3
+    shape = (relays, 2, groups * table.shape[1] // relays + left, LANES)
+    return pl.pallas_call(
+        functools.partial(expand_body, groups=groups),
+        out_shape=jax.ShapeDtypeStruct(shape, F32),
+        grid_spec=pltpu.PrefetchScalarGridSpec(
+            num_scalar_prefetch=1,
+            grid=(1,),
+            in_specs=[fixed(own.shape), fixed(far.shape), table_spec(table, own_side)]
+            + [ANYWHERE] * len(after),
+            out_specs=fixed(shape),
+        ),
+        compiler_params=params(),
+        cost_estimate=cost(4),
+        name="expand",
+    )(half, own, far, table, *after)
+
+
+PLANES = 8
+
+
+def mix_body(input_ref, cot_ref, weight_ref, *refs, planes, count):
+    mixed_ref, skip_ref, total, spread = refs[-4:]
+    step = pl.program_id(0)
+    channels = input_ref.shape[0]
+    side = channels * PLANES
+
+    def pick(shape, axis):
+        line = lax.broadcasted_iota(jnp.int32, shape, axis) // PLANES
+        return line == lax.broadcasted_iota(jnp.int32, shape, 1 - axis)
+
+    def same_plane():
+        row = lax.broadcasted_iota(jnp.int32, (side, side), 0)
+        column = lax.broadcasted_iota(jnp.int32, (side, side), 1)
+        return row % PLANES == column % PLANES
+
+    @pl.when(step == 0)
+    def _():
+        total[...] = jnp.zeros_like(total)
+        tall = dot(pick((side, channels), 0).astype(BF16), weight_ref[...]).astype(BF16)
+        wide = dot(tall, pick((channels, side), 1).astype(BF16))
+        spread[...] = jnp.where(same_plane(), wide, 0.0).astype(BF16)
+
+    mixed = [[] for _ in range(count)]
+    for first in range(0, planes, PLANES):
+        cots, lefts = [], []
+        for k in range(count):
+            rows = slice(k * planes, (k + 1) * planes)
+            near = slice(first, first + PLANES)
+            cots.append(cot_ref[:, rows, :].astype(F32)[:, near].reshape(side, NZ))
+            lefts.append(input_ref[:, rows, :].astype(F32)[:, near].reshape(side, NZ))
+        cot = jnp.concatenate(cots, axis=1).astype(BF16)
+        left = jnp.concatenate(lefts, axis=1).astype(BF16)
+        total[...] += lax.dot_general(
+            left, cot, (((1,), (1,)), ((), ())), preferred_element_type=F32
+        )
+        found = dot(spread[...], cot)
+        for k in range(count):
+            mixed[k].append(found[:, k * NZ : (k + 1) * NZ].reshape(channels, PLANES, NZ))
+    for k in range(count):
+        mixed_ref[:, k * planes : (k + 1) * planes, :] = jnp.concatenate(
+            mixed[k], axis=1
+        ).astype(BF16)
+
+    @pl.when(step == pl.num_programs(0) - 1)
+    def _():
+        kept = jnp.where(same_plane(), total[...], 0.0)
+        half = lax.dot_general(
+            kept,
+            pick((side, LANES), 0).astype(F32),
+            (((1,), (0,)), ((), ())),
+            precision=lax.Precision.HIGHEST,
+            preferred_element_type=F32,
+        )
+        skip_ref[...] = lax.dot_general(
+            pick((channels, side), 1).astype(F32),
+            half,
+            (((1,), (0,)), ((), ())),
+            precision=lax.Precision.HIGHEST,
+            preferred_element_type=F32,
+        )
+
+
+def mix(inputs, cot, weight, planes, after=()):
+    channels, rows, _ = inputs.shape
+    count = 16
+    side = channels * PLANES
+    spec = pl.BlockSpec((channels, count * planes, NZ), lambda x: (0, x, 0))
+    return pl.pallas_call(
+        functools.partial(mix_body, planes=planes, count=count),
+        out_shape=(
+            jax.ShapeDtypeStruct(inputs.shape, BF16),
+            jax.ShapeDtypeStruct((channels, LANES), F32),
+        ),
+        grid=(NX // count,),
+        in_specs=[spec, spec, whole((channels, channels))] + [ANYWHERE] * len(after),
+        out_specs=(spec, whole((channels, LANES))),
+        scratch_shapes=[pltpu.VMEM((side, side), F32), pltpu.VMEM((side, side), BF16)],
+        compiler_params=params(),
+        cost_estimate=cost(22),
+        name="mix",
+    )(inputs, cot, weight, *after)
+
+
+def x_then_z(
+    received_ref, mixed_ref, table_x, table_z, out_ref, real_ref, imag_ref, planes, blocks
+):
+    relays = received_ref.shape[0]
+    part = 2 * MX // relays
+    rows = NX * planes // blocks
+    block = pl.program_id(1)
+
+    @pl.when(block == 0)
+    def _():
+        for y in range(0, planes, 2):
+            pair = [
+                jnp.concatenate(
+                    [
+                        received_ref[r, side, at * part : (at + 1) * part, :]
+                        for side in range(2)
+                        for r in range(relays)
+                    ],
+                    axis=0,
+                ).astype(BF16)
+                for at in (y, y + 1)
+            ]
+            found = dot(table_x[...], jnp.concatenate(pair, axis=1))
+            for place in range(2):
+                lane = slice(place * LANES, (place + 1) * LANES)
+                real_ref[pl.ds(y + place, NX, stride=planes), :] = found[:NX, lane]
+                imag_ref[pl.ds(y + place, NX, stride=planes), :] = found[NX:, lane]
+
+    step = min(rows, 256)
+    for start in range(0, rows, step):
+        place = pl.ds(pl.multiple_of(block * rows + start, step), step)
+        line = jnp.concatenate([real_ref[place, :], imag_ref[place, :]], axis=1).astype(BF16)
+        found = dot(line, table_z[...])
+        for c in range(GROUP):
+            mixed = mixed_ref[c, start : start + step, :].astype(F32)
+            out_ref[c, start : start + step, :] = (
+                found[:, c * NZ : (c + 1) * NZ] + mixed
+            ).astype(BF16)
+
+
+def grid_plain(*refs, planes, blocks):
+    x_then_z(*refs, planes, blocks)
+
+
+def grid_skip(received_ref, skip_ref, *refs, planes, blocks, root):
+    mixed_ref, table_x, table_z = refs[:3]
+    out_ref, total_ref, real_ref, imag_ref = refs[-4:]
+
+    @pl.when((pl.program_id(0) == 0) & (pl.program_id(1) == 0))
+    def _():
+        total = jnp.sum(skip_ref[:, 0], axis=0)
+        total_ref[...] = total[:, : total_ref.shape[1]] / root
+
+    x_then_z(
+        received_ref, mixed_ref, table_x, table_z, out_ref, real_ref, imag_ref, planes, blocks
+    )
+
+
+def grid_of(received, mixed, first, groups, planes, root=None, after=()):
+    relays, _, rows, _ = received.shape
+    channels = mixed.shape[0]
+    blocks = 1
+    part = 2 * MX // relays
+    per_group = planes * part
+    spec = pl.BlockSpec((GROUP, NX * planes // blocks, NZ), lambda g, r: (g + first, r, 0))
+    in_specs = [
+        pl.BlockSpec((relays, 2, per_group, LANES), lambda g, r: (0, 0, g, 0)),
+        spec,
+        whole((2 * NX, 4 * MX)),
+        whole((2 * LANES, GROUP * NZ)),
+    ]
+    operands = [received, mixed, x_inverse_table(2 * relays), z_inverse_table()]
+    out_shape = (jax.ShapeDtypeStruct(mixed.shape, BF16),)
+    out_specs = (spec,)
+    body = functools.partial(grid_plain, planes=planes, blocks=blocks)
+    if root is not None:
+        extra = groups * per_group // channels
+        in_specs.insert(1, pl.BlockSpec((relays, 1, channels, LANES), lambda g, r: (0, 0, extra, 0)))
+        operands.insert(1, received)
+        out_shape += (jax.ShapeDtypeStruct((channels, channels), F32),)
+        out_specs += (whole((channels, channels)),)
+        body = functools.partial(grid_skip, planes=planes, blocks=blocks, root=root)
+    operands += after
+    in_specs += [ANYWHERE] * len(after)
+    return pl.pallas_call(
+        body,
+        out_shape=out_shape,
+        grid=(groups, blocks),
+        in_specs=in_specs,
+        out_specs=out_specs,
+        scratch_shapes=[
+            pltpu.VMEM((NX * planes, LANES), F32),
+            pltpu.VMEM((NX * planes, LANES), F32),
+        ],
+        input_output_aliases={1 if root is None else 2: 0},
+        compiler_params=params(2),
+        cost_estimate=cost(9),
+        name="to_grid",
+    )(*operands)
+
+
+def cross_body(own_ref, left_ref, right_ref, *refs, samples):
+    out_ref = refs[-1]
+    lanes = out_ref.shape[-1]
+    channels = left_ref.shape[1] // 2
+    own = right_ref.shape[2]
+    kz = lax.broadcasted_iota(jnp.int32, (own, lanes), 1) // (2 * MY) % MZ
+    scale = jnp.where(kz == 0, 1.0, 2.0) / float(NX * NY * NZ)
+    rights = [
+        (right_ref[b, 0] * scale, right_ref[b, 1] * scale) for b in range(samples)
+    ]
+    for i in range(channels):
+        real = imag = None
+        for b in range(samples):
+            left_real = left_ref[b, i : i + 1, :]
+            left_imag = left_ref[b, channels + i : channels + i + 1, :]
+            right_real, right_imag = rights[b]
+            one = left_real * right_real + left_imag * right_imag
+            two = left_real * right_imag - left_imag * right_real
+            real = one if real is None else real + one
+            imag = two if imag is None else imag + two
+        out_ref[0, i] = real
+        out_ref[1, i] = imag
+
+
+def cross(left, right, place, own, after=()):
+    samples, _, channels, modes = right.shape
+    lanes = 2 * MY * MZ
+    return pl.pallas_call(
+        functools.partial(cross_body, samples=samples),
+        out_shape=jax.ShapeDtypeStruct((2, channels, own, modes), F32),
+        grid_spec=pltpu.PrefetchScalarGridSpec(
+            num_scalar_prefetch=1,
+            grid=(modes // lanes,),
+            in_specs=[
+                pl.BlockSpec((samples, 2 * channels, lanes), lambda k, at: (0, 0, k)),
+                pl.BlockSpec((samples, 2, own, lanes), lambda k, at: (0, 0, at[0], k)),
+            ]
+            + [ANYWHERE] * len(after),
+            out_specs=pl.BlockSpec((2, channels, own, lanes), lambda k, at: (0, 0, 0, k)),
+        ),
+        compiler_params=params(),
+        cost_estimate=cost(6),
+        name="cross",
+    )(place, left, right, *after)
+
+
+def exchange_near(values):
+    spaces = lax.axis_size("space")
+    groups = [list(range(spaces // 2)), list(range(spaces // 2, spaces))]
+    return lax.all_to_all(
+        values, "space", split_axis=0, concat_axis=0, axis_index_groups=groups, tiled=True
+    )
+
+
+def exchange_far(values, turned=False):
+    spaces = lax.axis_size("space")
+    pairs = [(s, (s + spaces // 2) % spaces) for s in range(spaces)]
+    pairs = pairs[::-1] if turned else pairs
+    return lax.ppermute(values, "space", pairs)
 
 
 HIGHEST = lax.Precision.HIGHEST
@@ -40,12 +805,6 @@
     )
 
 
-def gelu_slope(values):
-    normal_cdf = 0.5 * (1.0 + jax.scipy.special.erf(values * (1.0 / math.sqrt(2.0))))
-    density = jnp.exp(-0.5 * values * values) * (1.0 / math.sqrt(2.0 * math.pi))
-    return normal_cdf + values * density
-
-
 def local_spectrum(grid_in):
     cos_x, sin_x = phase_table(NX, 2 * MX, True)
     table_x = jnp.stack([cos_x, -sin_x], axis=1).astype(jnp.bfloat16)
@@ -112,10 +871,10 @@
     return summed / math.sqrt(grid_in.shape[0] * lax.axis_size("batch") * NX * NY * NZ)
 
 
-def on_device(inputs, pre_act, cotangent, spectral_weight, skip_weight):
+def general(inputs, pre_act, cotangent, spectral_weight, skip_weight):
     samples = inputs.shape[0]
     channels = inputs.shape[1]
-    slope_pre = gelu_slope(pre_act.astype(jnp.float32))
+    slope_pre = slope(pre_act.astype(jnp.float32))
     cot_pre = (cotangent.astype(jnp.float32) * slope_pre).astype(jnp.bfloat16)
     spec_u, spec_e = both_along_y(
         (
@@ -153,6 +912,54 @@
     return (grad_inputs, grad_spectral, grad_skip)
 
 
+def on_device(inputs, pre_act, cotangent, spectral_weight, skip_weight):
+    samples, channels, _, planes, _ = inputs.shape
+    spaces = lax.axis_size("space")
+    batches = lax.axis_size("batch")
+    if samples != 1 or spaces % 2 or (2 * MX) % spaces or planes % 16 or channels % (4 * GROUP):
+        return general(inputs, pre_act, cotangent, spectral_weight, skip_weight)
+    kx_local = 2 * MX // spaces
+    flat = (channels, NX * planes, NZ)
+    groups = channels // GROUP
+    inputs, pre_act, cotangent = (v.reshape(flat) for v in (inputs, pre_act, cotangent))
+    half = (lax.axis_index("space") // (spaces // 2)).astype(jnp.int32).reshape(1)
+    batch = lax.axis_index("batch").astype(jnp.int32).reshape(1)
+    middle = groups // 2
+    (send_u,) = forward((inputs,), 0, groups, planes, spaces, False)
+    near_u = exchange_near(send_u)
+    send_e, cot_pre = forward(
+        (pre_act, cotangent), 0, groups, planes, spaces, True, after=(send_u,)
+    )
+    near_e = exchange_near(send_e)
+    part_u = partial_sums(half, near_u, groups, kx_local, "partial_u", after=(send_e,))
+    far_u = exchange_far(part_u)
+    mixed, skip_part = mix(inputs, cot_pre, skip_weight, planes, after=(part_u,))
+    hat_u = finish_u(half, near_u, far_u, skip_part, kx_local)
+    all_u = lax.all_gather(hat_u, "batch")
+    part_e = partial_sums(half, near_e, groups, kx_local, "partial_e", after=(hat_u,))
+    far_e = exchange_far(part_e)
+    hat_e, rounded, modes_a = finish_e(
+        half, near_e, far_e, spectral_weight, kx_local, after=(hat_u,)
+    )
+    far_a = exchange_far(modes_a)
+    all_e = lax.all_gather(hat_e, "batch")
+    modes_b = finish_rest(rounded, spectral_weight, all_u, kx_local)
+    far_b = exchange_far(modes_b, turned=True)
+    send_a = expand(half, modes_a, far_a, spaces // 2, middle, kx_local, after=(modes_b,))
+    near_a = exchange_near(send_a)
+    send_b = expand(half, modes_b, far_b, spaces // 2, middle, kx_local, after=(send_a,))
+    near_b = exchange_near(send_b)
+    grad_spectral = cross(all_u, all_e, batch, channels // batches, after=(send_b,))
+    (grad_inputs,) = grid_of(near_a, mixed, 0, middle, planes)
+    root = math.sqrt(samples * batches * NX * NY * NZ)
+    grad_inputs, grad_skip = grid_of(near_b, grad_inputs, middle, middle, planes, root, (grad_spectral,))
+    return (
+        grad_inputs.reshape(samples, channels, NX, planes, NZ),
+        grad_spectral,
+        grad_skip,
+    )
+
+
 def solution(mesh):
     placed = (
         P("batch", None, None, "space", None),

time: 562 us -> 207 us (0.37)
  matrix products: 256 us -> 0 us
  local copies, waits for them, and re-layouts: 143 us -> 4.07 us
  Pallas kernels: 0 us -> 109 us
  other arithmetic: 65.2 us -> 0 us
  blocking collectives: 41.4 us -> 0 us
  waiting for transfers between devices: 17.9 us -> 52.3 us
  starting transfers between devices: 17.9 us -> 26.1 us
    dot_general x11 -> x0, matrix products: 256 us -> none  [the longest x2 87.3 us: local_spectrum(): jnp.einsum('scpayz,pzqk->scqyak', section_x, forward_block(cos_z, sin_z),...]
    pallas_call x0 -> x13, Pallas kernels: none -> 109 us  [the longest x2 36.3 us: forward(): pl.pallas_call(functools.partial(body, planes=planes, spaces=spaces, bloc...]
    unnamed x12 -> x16, local copies, waits for them, and re-layouts: 59.9 us -> 4.07 us
    ppermute x0 -> x4, waiting for transfers between devices: none -> 52.2 us  [exchange_far(): return lax.ppermute(values, 'space', pairs)]
    psum x1 -> x0, blocking collectives: 41.4 us -> none  [skip_gradient(): summed = lax.psum(partial_sum, ('batch', 'space'))]
    all_to_all x7 -> x0, local copies, waits for them, and re-layouts: 35.8 us -> none  [the longest x2 13.7 us: on_device(): lax.all_to_all(grid_y, 'space', split_axis=3, concat_axis=4, tiled=True)]
    reshape x4 -> x0, local copies, waits for them, and re-layouts: 26.3 us -> none  [the longest x2 24.4 us: local_spectrum(): section_z.reshape(section_z.shape[0], section_z.shape[1], 2, section_z.sh...]
    all_to_all x3 -> x0, other arithmetic: 22 us -> none  [the longest x1 7.34 us: on_device(): lax.all_to_all(grid_y, 'space', split_axis=3, concat_axis=4, tiled=True)]
  transfers between devices with their start and end apart: 4 -> 10, of which waited for: 1 -> 4; matrix products, arithmetic and copies ran while one was open for 58% -> 0% of each run, Pallas kernels for 0% -> 43%
where the time goes in v2:
time: 207 us; the launch traced here: 206 us
  Pallas kernels  109 us (53%)
  waiting for transfers between devices  52.3 us (25%)
  starting transfers between devices  26.1 us (13%)
  between operations  14.1 us (7%)
  local copies, waits for them, and re-layouts  4.07 us (2%)
    ppermute x4, waiting for transfers between devices, exchange_far(): return lax.ppermute(values, 'space', pairs)  52.2 us
    pallas_call x2, Pallas kernels, forward(): pl.pallas_call(functools.partial(body, planes=planes, spaces=spaces, bloc...  36.3 us
    pallas_call x1, Pallas kernels, mix(): pl.pallas_call(functools.partial(mix_body, planes=planes, count=count), o...  22.3 us
    all_to_all x4, starting transfers between devices, exchange_near(): lax.all_to_all(values, 'space', split_axis=0, concat_axis=0, axis_index_g...  19.9 us
    pallas_call x2, Pallas kernels, grid_of(): pl.pallas_call(body, out_shape=out_shape, grid=(groups, blocks), in_specs...  17.4 us
    pallas_call x1, Pallas kernels, finish_e(): pl.pallas_call(functools.partial(spectrum_e, kx_local=kx_local, per_step=...  7.5 us
    ppermute x4, starting transfers between devices, exchange_far(): return lax.ppermute(values, 'space', pairs)  5.94 us
    pallas_call x2, Pallas kernels, expand(): pl.pallas_call(functools.partial(expand_body, groups=groups), out_shape=j...  5.86 us
  transfers between devices with their start and end apart: 10, of which 4 were waited for; matrix products, arithmetic and copies ran while one was open for 0% of the time, Pallas kernels for 43%

profile of v2, /device:TPU:0, one launch (start us, length us, event | category | flops | bytes accessed | tf_op | source)
XLA Modules:
  0.0 206.0 jit_solution(8521280750662920576)
XLA Ops:
  7.2 11.4 %forward_u.1.refs_0_ = f32[4,2,512,128]{3,2,1,0:T(8,128)} custom-call(bf16[32,2048,128]{2,1,0:T(8,128)(2,1)} %bitcast.10, bf16[1024,256]{1,0:T(8,128)(2,1)} %constant.36.clone.table_z, bf16[64,256]{1,0:T(8,128)(2,1)} %constant.37.clone.table_x), custom_call_target="tpu_custom_call" | custom-call | flops 22000001024 | bytes 1 | tf_op jit(solution)/shard_map/forward_u/pallas_call | solution.py:201
  18.5 5.2 %all-to-all-start.1 = ((f32[4,2,512,128]{3,2,1,0:T(8,128)}), f32[4,2,512,128]{3,2,1,0:T(8,128)S(1)}, u32[]{:S(2)}, u32[]{:S(2)}) async-start(f32[4,2,512,128]{3,2,1,0:T(8,128)} %forward_u.1.refs_0_), calls=%async_computation.1 | async-start | bytes 4194304 | tf_op jit(solution)/shard_map/all_to_all | solution.py:769
  23.8 24.9 %forward_e.1 = (f32[4,2,512,128]{3,2,1,0:T(8,128)}, bf16[32,2048,128]{2,1,0:T(8,128)(2,1)}) custom-call(bf16[32,2048,128]{2,1,0:T(8,128)(2,1)} %bitcast.8, bf16[32,2048,128]{2,1,0:T(8,128)(2,1)} %bitcast.9, bf16[1024,256]{1,0:T(8,128)(2,1)} %constant.36.clone.table_z, bf16[64,256]{1,0:T(8,128)(2,1)} %constant.37.clone.table_x, ...), custom_call_target="tpu_custom_call" | custom-call | flops 49999998976 | bytes 1 | tf_op jit(solution)/shard_map/forward_e/pallas_call | solution.py:201
  48.7 4.5 %all-to-all-start = ((f32[4,2,512,128]{3,2,1,0:T(8,128)}), f32[4,2,512,128]{3,2,1,0:T(8,128)}, u32[]{:S(2)}, u32[]{:S(2)}) async-start(f32[4,2,512,128]{3,2,1,0:T(8,128)} %get-tuple-element.12.refs_0_), calls=%async_computation | async-start | bytes 4194304 | tf_op jit(solution)/shard_map/all_to_all | solution.py:769
  53.3 2.9 %partial_u.1.refs_0_ = f32[4,256,128]{2,1,0:T(8,128)} custom-call(s32[1]{0:T(128)} %bitcast.half_ref, f32[4,2,512,128]{3,2,1,0:T(8,128)} %copy-done, bf16[2,256,1536]{2,1,0:T(8,128)(2,1)} %constant.38.clone.table, f32[4,2,512,128]{3,2,1,0:T(8,128)} %get-tuple-element.12.refs_0_), custom_call_target="tpu_custom_call" | custom-call | flops 6000000000 | bytes 1 | tf_op jit(solution)/shard_map/partial_u/pallas_call | solution.py:267
  56.1 2.6 %collective-permute-start = (f32[4,256,128]{2,1,0:T(8,128)}, f32[4,256,128]{2,1,0:T(8,128)S(1)}, u32[]{:S(2)}, u32[]{:S(2)}) collective-permute-start(f32[4,256,128]{2,1,0:T(8,128)} %partial_u.1.refs_0_), channel_id=1, source_target_pairs={{0,4},{1,5},{2,6},{3,7},{4,0},{5,1},{6,2},{7,3},{8,12},{9,13},{10,... | collective-permute-start | bytes 1572872 | tf_op jit(solution)/shard_map/ppermute | solution.py:778
  58.7 22.3 %mix.1 = (bf16[32,2048,128]{2,1,0:T(8,128)(2,1)}, f32[32,128]{1,0:T(8,128)}) custom-call(bf16[32,2048,128]{2,1,0:T(8,128)(2,1)} %bitcast.11, bf16[32,2048,128]{2,1,0:T(8,128)(2,1)} %get-tuple-element.13.cot_ref, bf16[32,32]{1,0:T(8,128)(2,1)} %weight_ref.3, f32[4,256,128]{2,1,0:T(8,128)} %partial_u.1.refs_0_), custom_call_target="tpu_custom_call" | custom-call | flops 44000002048 | bytes 1 | tf_op jit(solution)/shard_map/mix/pallas_call | solution.py:603
  81.0 6.2 %collective-permute-done.far_ref = f32[4,256,128]{2,1,0:T(8,128)S(1)} collective-permute-done((f32[4,256,128]{2,1,0:T(8,128)}, f32[4,256,128]{2,1,0:T(8,128)S(1)}, u32[]{:S(2)}, u32[]{:S(2)}) %collective-permute-start) | collective-permute-done | bytes 524320 | tf_op jit(solution)/shard_map/ppermute | solution.py:778
  88.0 3.7 %finish_u.1.refs_0_ = f32[72,2048]{1,0:T(8,128)} custom-call(s32[1]{0:T(128)} %bitcast.half_ref, f32[4,2,512,128]{3,2,1,0:T(8,128)} %copy-done, f32[4,256,128]{2,1,0:T(8,128)} %copy-done.3, bf16[2,256,1536]{2,1,0:T(8,128)(2,1)} %constant.38.clone.table, f32[32,128]{1,0:T(8,128)} %get-tuple-element.14.skip_ref), custom_call_target="tpu_custom_call" | custom-call | flops 8000000000 | bytes 1 | tf_op jit(solution)/shard_map/finish_u/pallas_call | solution.py:344
  91.9 2.8 %partial_e.1 = f32[4,256,128]{2,1,0:T(8,128)} custom-call(s32[1]{0:T(128)} %bitcast.half_ref, f32[4,2,512,128]{3,2,1,0:T(8,128)} %all-to-all-done.near_ref, bf16[2,256,1536]{2,1,0:T(8,128)(2,1)} %constant.38.clone.table, f32[72,2048]{1,0:T(8,128)} %finish_u.1.refs_0_), custom_call_target="tpu_custom_call" | custom-call | flops 6000000000 | bytes 1 | tf_op jit(solution)/shard_map/partial_e/pallas_call | solution.py:267
  94.8 3.3 %collective-permute-start.1 = (f32[4,256,128]{2,1,0:T(8,128)}, f32[4,256,128]{2,1,0:T(8,128)S(1)}, u32[]{:S(2)}, u32[]{:S(2)}) collective-permute-start(f32[4,256,128]{2,1,0:T(8,128)} %partial_e.1), channel_id=1, source_target_pairs={{0,4},{1,5},{2,6},{3,7},{4,0},{5,1},{6,2},{7,3},{8,12},{9,13},{10,... | collective-permute-start | bytes 1572872 | tf_op jit(solution)/shard_map/ppermute | solution.py:778
  98.0 22.5 %collective-permute-done.1.far_ref = f32[4,256,128]{2,1,0:T(8,128)S(1)} collective-permute-done((f32[4,256,128]{2,1,0:T(8,128)}, f32[4,256,128]{2,1,0:T(8,128)S(1)}, u32[]{:S(2)}, u32[]{:S(2)}) %collective-permute-start.1) | collective-permute-done | bytes 524320 | tf_op jit(solution)/shard_map/ppermute | solution.py:778
  121.3 7.5 %finish_e.1 = (f32[2,32,2048]{2,1,0:T(8,128)}, f32[2,32,2048]{2,1,0:T(8,128)}, f32[512,128]{1,0:T(8,128)}) custom-call(s32[1]{0:T(128)} %bitcast.half_ref, f32[4,2,512,128]{3,2,1,0:T(8,128)} %all-to-all-done.near_ref, f32[4,256,128]{2,1,0:T(8,128)} %copy-done.4, bf16[2,32,32,2048]{3,2,1,0:T(8,128)(2,1)} %weight_ref.5, ...), custom_call_target="tpu_custom_call" | custom-call | flops 16000000000 | bytes 1 | tf_op jit(solution)/shard_map/finish_e/pallas_call | solution.py:434
  128.9 4.9 %finish_rest.1.refs_0_.own_ref = f32[544,128]{1,0:T(8,128)} custom-call(f32[2,32,2048]{2,1,0:T(8,128)} %get-tuple-element.15.rounded, bf16[2,32,32,2048]{3,2,1,0:T(8,128)(2,1)} %weight_ref.5, f32[4,72,2048]{2,1,0:T(8,128)} %bitcast.12), custom_call_target="tpu_custom_call" | custom-call | flops 10000000000 | bytes 1 | tf_op jit(solution)/shard_map/finish_rest/pallas_call | solution.py:467
  133.8 8.3 %collective-permute-done.3.far_ref = f32[512,128]{1,0:T(8,128)S(1)} collective-permute-done((f32[512,128]{1,0:T(8,128)}, f32[512,128]{1,0:T(8,128)S(1)}, u32[]{:S(2)}, u32[]{:S(2)}) %collective-permute-start.3) | collective-permute-done | bytes 262176 | tf_op jit(solution)/shard_map/ppermute | solution.py:778
  142.8 2.9 %expand.2.refs_0_ = f32[4,2,256,128]{3,2,1,0:T(8,128)} custom-call(s32[1]{0:T(128)} %bitcast.half_ref, f32[512,128]{1,0:T(8,128)} %get-tuple-element.16.own_ref, f32[512,128]{1,0:T(8,128)} %copy-done.7, bf16[2,512,768]{2,1,0:T(8,128)(2,1)} %constant.39.clone.table, f32[544,128]{1,0:T(8,128)} %finish_rest.1.refs_0_.own_ref), custom_call_target="tpu_custom_call" | custom-call | flops 8000000000 | bytes 1 | tf_op jit(solution)/shard_map/expand/pallas_call | solution.py:517
  145.7 3.5 %all-to-all-start.3 = ((f32[4,2,256,128]{3,2,1,0:T(8,128)}), f32[4,2,256,128]{3,2,1,0:T(8,128)S(1)}, u32[]{:S(2)}, u32[]{:S(2)}) async-start(f32[4,2,256,128]{3,2,1,0:T(8,128)} %expand.2.refs_0_), calls=%async_computation.3 | async-start | bytes 2097152 | tf_op jit(solution)/shard_map/all_to_all | solution.py:769
  149.3 15.2 %collective-permute-done.2.far_ref = f32[544,128]{1,0:T(8,128)S(1)} collective-permute-done((f32[544,128]{1,0:T(8,128)S(1)}, f32[544,128]{1,0:T(8,128)S(1)}, u32[]{:S(2)}, u32[]{:S(2)}) %collective-permute-start.2) | collective-permute-done | bytes 278560 | tf_op jit(solution)/shard_map/ppermute | solution.py:778
  165.2 3.0 %expand.3.refs_0_ = f32[4,2,288,128]{3,2,1,0:T(8,128)} custom-call(s32[1]{0:T(128)} %bitcast.half_ref, f32[544,128]{1,0:T(8,128)} %finish_rest.1.refs_0_.own_ref, f32[544,128]{1,0:T(8,128)} %copy-done.6, bf16[2,512,768]{2,1,0:T(8,128)(2,1)} %constant.39.clone.table, f32[4,2,256,128]{3,2,1,0:T(8,128)} %expand.2.refs_0_), custom_call_target="tpu_custom_call" | custom-call | flops 8000000000 | bytes 1 | tf_op jit(solution)/shard_map/expand/pallas_call | solution.py:517
  168.2 6.7 %all-to-all-start.2 = ((f32[4,2,288,128]{3,2,1,0:T(8,128)}), f32[4,2,288,128]{3,2,1,0:T(8,128)S(1)}, u32[]{:S(2)}, u32[]{:S(2)}) async-start(f32[4,2,288,128]{3,2,1,0:T(8,128)} %expand.3.refs_0_), calls=%async_computation.2 | async-start | bytes 2359296 | tf_op jit(solution)/shard_map/all_to_all | solution.py:769
  174.9 5.8 %cross.1.refs_3_ = f32[2,32,8,2048]{3,2,1,0:T(8,128)} custom-call(s32[1]{0:T(128)} %bitcast.5.own_ref, f32[4,72,2048]{2,1,0:T(8,128)} %bitcast.13, f32[4,2,32,2048]{3,2,1,0:T(8,128)} %bitcast.14, f32[4,2,288,128]{3,2,1,0:T(8,128)} %expand.3.refs_0_), custom_call_target="tpu_custom_call" | custom-call | flops 12000000000 | bytes 1 | tf_op jit(solution)/shard_map/cross/pallas_call | solution.py:747
  180.6 8.7 %to_grid.2.refs_0_ = bf16[32,2048,128]{2,1,0:T(8,128)(2,1)} custom-call(f32[4,2,256,128]{3,2,1,0:T(8,128)} %copy-done.2, bf16[32,2048,128]{2,1,0:T(8,128)(2,1)} %get-tuple-element.17.refs_1_, bf16[256,64]{1,0:T(8,128)(2,1)} %constant.40.clone.refs_2_.refs_1_, bf16[256,1024]{1,0:T(8,128)(2,1)} %constant.41.clone.refs_3_.refs_2_), custom_call_target="tpu_custom_call", output_to_operand_aliasing={{}: (1, {})} | custom-call | flops 17999998976 | bytes 1 | tf_op jit(solution)/shard_map/to_grid/pallas_call | solution.py:703
  189.4 1.0 copy-done.1
  190.4 8.7 %to_grid.3 = (bf16[32,2048,128]{2,1,0:T(8,128)(2,1)}, f32[32,32]{1,0:T(8,128)}) custom-call(f32[4,2,288,128]{3,2,1,0:T(8,128)} %copy-done.1, f32[4,2,288,128]{3,2,1,0:T(8,128)} %copy-done.1, bf16[32,2048,128]{2,1,0:T(8,128)(2,1)} %to_grid.2.refs_0_, bf16[256,64]{1,0:T(8,128)(2,1)} %constant.40.clone.refs_2_.refs_1_, ...), custom_call_target="tpu_custom_call", output_to_operand_aliasing={{0}: (2, {})} | custom-call | flops 17999998976 | bytes 1 | tf_op jit(solution)/shard_map/to_grid/pallas_call | solution.py:703
  (27 shorter events, 3.5 us)
Async XLA Ops:
  18.5 30.2 %all-to-all-start.1 = ((f32[4,2,512,128]{3,2,1,0:T(8,128)}), f32[4,2,512,128]{3,2,1,0:T(8,128)S(1)}, u32[]{:S(2)}, u32[]{:S(2)}) async-start(f32[4,2,512,128]{3,2,1,0:T(8,128)} %forward_u.1.refs_0_), calls=%async_computation.1 | async-start | bytes 4194304 | tf_op jit(solution)/shard_map/all_to_all | solution.py:769
  48.7 4.5 %copy-start = (f32[4,2,512,128]{3,2,1,0:T(8,128)}, f32[4,2,512,128]{3,2,1,0:T(8,128)S(1)}, u32[]{:S(2)}) copy-start(f32[4,2,512,128]{3,2,1,0:T(8,128)S(1)} %all-to-all-done.1.near_ref) | copy-start | bytes 6291460
  48.7 43.2 %all-to-all-start = ((f32[4,2,512,128]{3,2,1,0:T(8,128)}), f32[4,2,512,128]{3,2,1,0:T(8,128)}, u32[]{:S(2)}, u32[]{:S(2)}) async-start(f32[4,2,512,128]{3,2,1,0:T(8,128)} %get-tuple-element.12.refs_0_), calls=%async_computation | async-start | bytes 4194304 | tf_op jit(solution)/shard_map/all_to_all | solution.py:769
  53.2 75.7 %all-gather.5.cloned.1.call-start = ((), (), s32[]{:S(2)}) async-start(), calls=%async_computation.4 | async-start | bytes 2949120 | tf_op jit(solution)/shard_map/all_gather | solution.py:938
  56.1 31.1 %collective-permute-start = (f32[4,256,128]{2,1,0:T(8,128)}, f32[4,256,128]{2,1,0:T(8,128)S(1)}, u32[]{:S(2)}, u32[]{:S(2)}) collective-permute-start(f32[4,256,128]{2,1,0:T(8,128)} %partial_u.1.refs_0_), channel_id=1, source_target_pairs={{0,4},{1,5},{2,6},{3,7},{4,0},{5,1},{6,2},{7,3},{8,12},{9,13},{10,... | collective-permute-start | bytes 1572872 | tf_op jit(solution)/shard_map/ppermute | solution.py:778
  87.2 0.8 copy-start.3
  91.7 83.2 %all-gather.7.cloned.1.call-start = ((), (), s32[]{:S(2)}) async-start(), calls=%async_computation.5 | async-start | bytes 2621440 | tf_op jit(solution)/shard_map/all_gather | solution.py:945
  94.8 25.8 %collective-permute-start.1 = (f32[4,256,128]{2,1,0:T(8,128)}, f32[4,256,128]{2,1,0:T(8,128)S(1)}, u32[]{:S(2)}, u32[]{:S(2)}) collective-permute-start(f32[4,256,128]{2,1,0:T(8,128)} %partial_e.1), channel_id=1, source_target_pairs={{0,4},{1,5},{2,6},{3,7},{4,0},{5,1},{6,2},{7,3},{8,12},{9,13},{10,... | collective-permute-start | bytes 1572872 | tf_op jit(solution)/shard_map/ppermute | solution.py:778
  120.5 0.8 copy-start.4
  128.8 13.3 %collective-permute-start.3 = (f32[512,128]{1,0:T(8,128)}, f32[512,128]{1,0:T(8,128)S(1)}, u32[]{:S(2)}, u32[]{:S(2)}) collective-permute-start(f32[512,128]{1,0:T(8,128)} %get-tuple-element.16.own_ref), channel_id=1, source_target_pairs={{0,4},{1,5},{2,6},{3,7},{4,0},{5,1},{6,2},{7,3},{8,12},{9,13},{10,... | collective-permute-start | bytes 786440 | tf_op jit(solution)/shard_map/ppermute | solution.py:778
  133.8 15.5 %copy-start.5 = (f32[544,128]{1,0:T(8,128)S(1)}, f32[544,128]{1,0:T(8,128)}, u32[]{:S(2)}) copy-start(f32[544,128]{1,0:T(8,128)} %finish_rest.1.refs_0_.own_ref) | copy-start | bytes 835588
  142.1 0.7 copy-start.7
  145.7 22.5 %all-to-all-start.3 = ((f32[4,2,256,128]{3,2,1,0:T(8,128)}), f32[4,2,256,128]{3,2,1,0:T(8,128)S(1)}, u32[]{:S(2)}, u32[]{:S(2)}) async-start(f32[4,2,256,128]{3,2,1,0:T(8,128)} %expand.2.refs_0_), calls=%async_computation.3 | async-start | bytes 2097152 | tf_op jit(solution)/shard_map/all_to_all | solution.py:769
  149.2 15.2 %collective-permute-start.2 = (f32[544,128]{1,0:T(8,128)S(1)}, f32[544,128]{1,0:T(8,128)S(1)}, u32[]{:S(2)}, u32[]{:S(2)}) collective-permute-start(f32[544,128]{1,0:T(8,128)S(1)} %copy-done.5), channel_id=1, source_target_pairs={{7,3},{6,2},{5,1},{4,0},{3,7},{2,6},{1,5},{0,4},{15,11},{14,10},{1... | collective-permute-start | bytes 835592 | tf_op jit(solution)/shard_map/ppermute | solution.py:778
  164.5 0.7 copy-start.6
  168.2 12.5 %copy-start.2 = (f32[4,2,256,128]{3,2,1,0:T(8,128)}, f32[4,2,256,128]{3,2,1,0:T(8,128)S(1)}, u32[]{:S(2)}) copy-start(f32[4,2,256,128]{3,2,1,0:T(8,128)S(1)} %all-to-all-done.3.refs_0_) | copy-start | bytes 3145732
  168.2 21.2 %all-to-all-start.2 = ((f32[4,2,288,128]{3,2,1,0:T(8,128)}), f32[4,2,288,128]{3,2,1,0:T(8,128)S(1)}, u32[]{:S(2)}, u32[]{:S(2)}) async-start(f32[4,2,288,128]{3,2,1,0:T(8,128)} %expand.3.refs_0_), calls=%async_computation.2 | async-start | bytes 2359296 | tf_op jit(solution)/shard_map/all_to_all | solution.py:769
  189.4 1.0 copy-start.1
Sparse Core Ops, SparseCore 0:
  91.8 26.4 all-gather.4
  129.0 24.4 all-gather.6

commit v3 on v2

--- a/solution.py
+++ b/solution.py
@@ -20,7 +20,7 @@
 LANES = GROUP * MZ
 BF16 = jnp.bfloat16
 F32 = jnp.float32
-VMEM_LIMIT = 56 * 1024 * 1024
+VMEM_LIMIT = 62 * 1024 * 1024
 
 
 def cost(microseconds):
@@ -66,12 +66,14 @@
     return jnp.asarray(rounded_table(table.reshape(4 * MX, 2 * NX)))
 
 
-def x_inverse_table(spaces):
+def x_inverse_table(relays):
     cos, sin = waves(NX, 2 * MX, True)
-    cos = cos.reshape(NX, spaces, 2 * MX // spaces)
-    sin = sin.reshape(NX, spaces, 2 * MX // spaces)
-    table = np.stack([np.stack([cos, -sin], axis=2), np.stack([sin, cos], axis=2)], axis=0)
-    return jnp.asarray(rounded_table(table.reshape(2 * NX, 4 * MX)))
+    cos = cos.reshape(NX, 2, relays, MX // relays)
+    sin = sin.reshape(NX, 2, relays, MX // relays)
+    table = np.stack([np.stack([cos, -sin], axis=3), np.stack([sin, cos], axis=3)], axis=0)
+    place = np.arange(relays)
+    table = np.stack([table[:, :, :, place ^ r] for r in range(relays)])
+    return jnp.asarray(rounded_table(table.reshape(relays, 2 * NX, 4 * MX)))
 
 
 def split_table(table):
@@ -232,12 +234,15 @@
     return dot_split(table[0], data)
 
 
-def partial_body(half_ref, near_ref, table, *refs):
+def partial_body(half_ref, near_ref, table, *refs, groups, riding):
     out_ref = refs[-1]
-    for g in range(0, out_ref.shape[0], 2):
+    rows = table.shape[1]
+    for g in range(0, groups, 2):
         found = half_sums(near_ref, table, g, 2)
-        out_ref[g] = found[:, :LANES]
-        out_ref[g + 1] = found[:, LANES:]
+        out_ref[g * rows : (g + 1) * rows, :] = found[:, :LANES]
+        out_ref[(g + 1) * rows : (g + 2) * rows, :] = found[:, LANES:]
+    if riding:
+        out_ref[groups * rows :, :] = refs[0][...]
 
 
 def table_spec(table, side):
@@ -261,33 +266,36 @@
     return pl.BlockSpec(shape, lambda *at: (0,) * len(shape))
 
 
-def partial_sums(half, near, groups, kx_local, name, after=()):
+def partial_sums(half, near, groups, kx_local, name, riding=(), after=()):
     table = y_forward_table(kx_local)
-    shape = (groups, table.shape[1], LANES)
+    rows = groups * table.shape[1] + sum(v.shape[0] for v in riding)
     return pl.pallas_call(
-        partial_body,
-        out_shape=jax.ShapeDtypeStruct(shape, F32),
+        functools.partial(partial_body, groups=groups, riding=bool(riding)),
+        out_shape=jax.ShapeDtypeStruct((rows, LANES), F32),
         grid_spec=pltpu.PrefetchScalarGridSpec(
             num_scalar_prefetch=1,
             grid=(1,),
             in_specs=[near_spec(near, other_side), table_spec(table, own_side)]
+            + [fixed(v.shape) for v in riding]
             + [ANYWHERE] * len(after),
-            out_specs=fixed(shape),
+            out_specs=fixed((rows, LANES)),
         ),
         compiler_params=params(),
         cost_estimate=cost(3),
         name=name,
-    )(half, near, table, *after)
+    )(half, near, table, *riding, *after)
 
 
 def unfold_y(near_ref, far_ref, table, lines, store, kx_local):
     width = kx_local * 2 * MY
-    groups = far_ref.shape[0]
-    channels = groups * GROUP
+    channels = lines.shape[1] // MZ
+    groups = channels // GROUP
     for g in range(0, groups, 2):
         pair = half_sums(near_ref, table, g, 2)
         for at in (g, g + 1):
-            found = pair[:, (at - g) * LANES : (at - g + 1) * LANES] + far_ref[at]
+            found = pair[:, (at - g) * LANES : (at - g + 1) * LANES] + far_ref[
+                2 * at * width : 2 * (at + 1) * width, :
+            ]
             for part in range(2):
                 lines[part, at * LANES : (at + 1) * LANES, :] = found[
                     part * width : (part + 1) * width, :
@@ -322,37 +330,26 @@
 SUBLANES = 8
 
 
-def spectrum_u(half_ref, near_ref, far_ref, table, skip_ref, *refs, kx_local):
+def spectrum_u(half_ref, near_ref, far_ref, table, *refs, kx_local):
     hat_ref, lines = refs[-2:]
-    channels = skip_ref.shape[0]
+    channels = hat_ref.shape[0] // 2
 
     def store(part, column, values):
         hat_ref[part * channels : (part + 1) * channels, column : column + 2 * MY] = values
 
     unfold_y(near_ref, far_ref, table, lines, store, kx_local)
-    hat_ref[2 * channels :, :] = jnp.zeros((SUBLANES, hat_ref.shape[1]), F32)
-    for k in range(channels // SUBLANES):
-        hat_ref[2 * channels :, k * LANES : (k + 1) * LANES] = skip_ref[
-            k * SUBLANES : (k + 1) * SUBLANES, :
-        ]
-
-
-def finish_u(half, near, far, skip, kx_local, after=()):
-    channels = far.shape[0] * GROUP
+
+
+def finish_u(half, near, far, channels, kx_local, after=()):
     table = y_forward_table(kx_local)
-    shape = (2 * channels + SUBLANES, kx_local * MZ * 2 * MY)
+    shape = (2 * channels, kx_local * MZ * 2 * MY)
     return pl.pallas_call(
         functools.partial(spectrum_u, kx_local=kx_local),
         out_shape=jax.ShapeDtypeStruct(shape, F32),
         grid_spec=pltpu.PrefetchScalarGridSpec(
             num_scalar_prefetch=1,
             grid=(1,),
-            in_specs=[
-                near_spec(near, own_side),
-                fixed(far.shape),
-                table_spec(table, own_side),
-                fixed(skip.shape),
-            ]
+            in_specs=[near_spec(near, own_side), fixed(far.shape), table_spec(table, own_side)]
             + [ANYWHERE] * len(after),
             out_specs=fixed(shape),
             scratch_shapes=[pltpu.VMEM((2, channels * MZ, kx_local * 2 * MY), F32)],
@@ -360,7 +357,7 @@
         compiler_params=params(),
         cost_estimate=cost(4),
         name="finish_u",
-    )(half, near, far, table, skip, *after)
+    )(half, near, far, table, *after)
 
 
 def mode_scale(kz):
@@ -388,18 +385,44 @@
         back[1, rows, lane] = jnp.concatenate(imags, axis=0)
 
 
-def spectrum_e(half_ref, near_ref, far_ref, weight_ref, table, *refs, kx_local, per_step):
-    hat_ref, rounded, send_ref, lines, back = refs[-5:]
+def spectrum_e(
+    batch_ref,
+    half_ref,
+    near_ref,
+    far_ref,
+    weight_ref,
+    table,
+    skip_ref,
+    *refs,
+    kx_local,
+    per_step,
+    batches,
+):
+    rounded, send_ref, hat, lines, back = refs[-5:]
+    own_refs = refs[-5 - batches : -5]
+    channels = skip_ref.shape[0]
+    own = channels // batches
 
     @pl.when(pl.program_id(0) == 0)
     def _():
         def store(part, column, values):
-            hat_ref[part, :, column : column + 2 * MY] = values
+            hat[part, :, column : column + 2 * MY] = values
             rounded[part, :, column : column + 2 * MY] = values.astype(BF16).astype(
                 F32
             ) * mode_scale((column // (2 * MY)) % MZ)
 
         unfold_y(near_ref, far_ref, table, lines, store, kx_local)
+        skip = skip_ref[...] + far_ref[far_ref.shape[0] - channels :, :]
+        for d in range(batches):
+            first = jnp.bitwise_xor(batch_ref[0], d) * own
+            rows = pl.ds(pl.multiple_of(first, own), own)
+            own_refs[d][:own, :] = hat[0, rows, :]
+            own_refs[d][own : 2 * own, :] = hat[1, rows, :]
+            own_refs[d][2 * own :, :] = jnp.zeros((SUBLANES, hat.shape[2]), F32)
+            for k in range(channels // SUBLANES):
+                own_refs[d][2 * own :, k * LANES : (k + 1) * LANES] = skip[
+                    k * SUBLANES : (k + 1) * SUBLANES, :
+                ]
 
     through_weight(weight_ref, rounded, back, per_step, kx_local * MZ * 2 * MY)
 
@@ -408,44 +431,41 @@
         fold_modes(back, lines, send_ref, kx_local)
 
 
-def spectrum_rest(rounded, weight_ref, skip_ref, send_ref, lines, back, *, kx_local, per_step):
+def spectrum_rest(rounded, weight_ref, *refs, kx_local, per_step):
+    send_ref, lines, back = refs[-3:]
     through_weight(weight_ref, rounded, back, per_step, kx_local * MZ * 2 * MY)
 
     @pl.when(pl.program_id(0) == pl.num_programs(0) - 1)
     def _():
         fold_modes(back, lines, send_ref, kx_local)
-        skip = jnp.sum(skip_ref[...], axis=0)
-        channels = rounded.shape[1]
-        first = send_ref.shape[0] - channels
-        for k in range(channels // SUBLANES):
-            send_ref[first + k * SUBLANES : first + (k + 1) * SUBLANES, :] = skip[
-                :, k * LANES : (k + 1) * LANES
-            ]
-
-
-def finish_e(half, near, far, weight, kx_local, after=()):
-    channels = far.shape[0] * GROUP
+
+
+def finish_e(batch, half, near, far, weight, skip, kx_local, batches, after=()):
+    channels = skip.shape[0]
     modes = kx_local * MZ * 2 * MY
     per_step = 8
     near_half = channels // 2
     table = y_forward_table(kx_local)
+    own = jax.ShapeDtypeStruct((2 * channels // batches + SUBLANES, modes), F32)
     spectrum = jax.ShapeDtypeStruct((2, channels, modes), F32)
-    send = jax.ShapeDtypeStruct((far.shape[0] // 2 * far.shape[1], LANES), F32)
-    return pl.pallas_call(
-        functools.partial(spectrum_e, kx_local=kx_local, per_step=per_step),
-        out_shape=(spectrum, spectrum, send),
+    send = jax.ShapeDtypeStruct((near_half // GROUP * 2 * kx_local * 2 * MY, LANES), F32)
+    *owns, rounded, sent = pl.pallas_call(
+        functools.partial(spectrum_e, kx_local=kx_local, per_step=per_step, batches=batches),
+        out_shape=(own,) * batches + (spectrum, send),
         grid_spec=pltpu.PrefetchScalarGridSpec(
-            num_scalar_prefetch=1,
+            num_scalar_prefetch=2,
             grid=(near_half // per_step,),
             in_specs=[
                 near_spec(near, own_side),
                 fixed(far.shape),
-                pl.BlockSpec((2, per_step, channels, modes), lambda i, at: (0, i, 0, 0)),
+                pl.BlockSpec((2, per_step, channels, modes), lambda i, *at: (0, i, 0, 0)),
                 table_spec(table, own_side),
+                fixed(skip.shape),
             ]
             + [ANYWHERE] * len(after),
-            out_specs=(fixed(spectrum.shape), fixed(spectrum.shape), fixed(send.shape)),
+            out_specs=(fixed(own.shape),) * batches + (fixed(spectrum.shape), fixed(send.shape)),
             scratch_shapes=[
+                pltpu.VMEM((2, channels, modes), F32),
                 pltpu.VMEM((2, channels * MZ, kx_local * 2 * MY), F32),
                 pltpu.VMEM((2, near_half, modes), F32),
             ],
@@ -453,17 +473,16 @@
         compiler_params=params(),
         cost_estimate=cost(8),
         name="finish_e",
-    )(half, near, far, weight, table, *after)
-
-
-def finish_rest(rounded, weight, all_u, kx_local):
+    )(batch, half, near, far, weight, table, skip, *after)
+    return owns, rounded, sent
+
+
+def finish_rest(rounded, weight, kx_local, after=()):
     _, channels, modes = rounded.shape
     per_step = 8
     rest = channels // 2
     steps = rest // per_step
-    rows = rest // GROUP * 2 * kx_local * 2 * MY + channels
-    skip_block = (all_u.shape[0], SUBLANES, channels // SUBLANES * LANES)
-    send = jax.ShapeDtypeStruct((rows, LANES), F32)
+    send = jax.ShapeDtypeStruct((rest // GROUP * 2 * kx_local * 2 * MY, LANES), F32)
     return pl.pallas_call(
         functools.partial(spectrum_rest, kx_local=kx_local, per_step=per_step),
         out_shape=send,
@@ -471,8 +490,8 @@
         in_specs=[
             whole(rounded.shape),
             pl.BlockSpec((2, per_step, channels, modes), lambda i: (0, i + steps, 0, 0)),
-            pl.BlockSpec(skip_block, lambda i: (0, 2 * channels // SUBLANES, 0)),
-        ],
+        ]
+        + [ANYWHERE] * len(after),
         out_specs=whole(send.shape),
         scratch_shapes=[
             pltpu.VMEM((2, rest * MZ, kx_local * 2 * MY), F32),
@@ -481,53 +500,75 @@
         compiler_params=params(),
         cost_estimate=cost(5),
         name="finish_rest",
-    )(rounded, weight, all_u)
-
-
-def expand_body(half_ref, own_ref, far_ref, table, *refs, groups):
-    send_ref = refs[-1]
-    relays = send_ref.shape[0]
+    )(rounded, weight, *after)
+
+
+def expand_body(
+    half_ref, relay_ref, own_ref, far_ref, table, *refs, groups, channels, relays, riding
+):
+    send_refs = refs[-relays - 1 : -1]
+    lines = refs[-1]
     per_group = table.shape[1] // relays
     modes = table.shape[2] // 3
     half = half_ref[0]
+    at_line = 0
     for ref, side in ((own_ref, half), (far_ref, 1 - half)):
         for g in range(0, groups, 2):
             data = jnp.concatenate(
                 [ref[at * modes : (at + 1) * modes, :] for at in (g, g + 1)], axis=1
             )
-            found = dot_split(table[0], data)
-            for r in range(relays):
+            lines[at_line] = dot_split(table[0], data)
+            for d in range(relays):
+                place = jnp.bitwise_xor(relay_ref[0], d) * per_group
+                rows = pl.ds(pl.multiple_of(place, per_group), per_group)
                 for at in (g, g + 1):
-                    send_ref[r, side, at * per_group : (at + 1) * per_group, :] = found[
-                        r * per_group : (r + 1) * per_group,
-                        (at - g) * LANES : (at - g + 1) * LANES,
+                    send_refs[d][side, at * per_group : (at + 1) * per_group, :] = lines[
+                        at_line, rows, (at - g) * LANES : (at - g + 1) * LANES
                     ]
-    left = own_ref.shape[0] - groups * modes
-    if left:
-        total = own_ref[groups * modes :, :] + far_ref[groups * modes :, :]
-        for r in range(relays):
-            send_ref[r, 0, groups * per_group :, :] = total
-            send_ref[r, 1, groups * per_group :, :] = total
-
-
-def expand(half, own, far, relays, groups, kx_local, after=()):
+            at_line += 1
+    if channels:
+        skip = sum(ref[...] for ref in refs[:riding])
+        for d in range(relays):
+            for side in range(2):
+                for k in range(channels // SUBLANES):
+                    row = groups * per_group + k * SUBLANES
+                    send_refs[d][side, row : row + SUBLANES, :] = skip[
+                        :, k * LANES : (k + 1) * LANES
+                    ]
+
+
+def expand(half, relay, own, far, relays, groups, kx_local, riding=(), channels=0, after=()):
     table = y_inverse_table(kx_local)
-    left = own.shape[0] - groups * table.shape[2] // 3
-    shape = (relays, 2, groups * table.shape[1] // relays + left, LANES)
+    shape = (2, groups * table.shape[1] // relays + channels, LANES)
+    skip_specs = [
+        pl.BlockSpec(
+            (SUBLANES, channels // SUBLANES * LANES),
+            lambda *at: (riding[0].shape[0] // SUBLANES - 1, 0),
+        )
+        for _ in riding
+    ]
     return pl.pallas_call(
-        functools.partial(expand_body, groups=groups),
-        out_shape=jax.ShapeDtypeStruct(shape, F32),
+        functools.partial(
+            expand_body, groups=groups, channels=channels, relays=relays, riding=len(riding)
+        ),
+        out_shape=(jax.ShapeDtypeStruct(shape, F32),) * relays,
         grid_spec=pltpu.PrefetchScalarGridSpec(
-            num_scalar_prefetch=1,
+            num_scalar_prefetch=2,
             grid=(1,),
-            in_specs=[fixed(own.shape), fixed(far.shape), table_spec(table, own_side)]
+            in_specs=[
+                fixed(own.shape),
+                fixed(far.shape),
+                pl.BlockSpec((1,) + table.shape[1:], lambda i, half, relay: (half[0], 0, 0)),
+            ]
+            + skip_specs
             + [ANYWHERE] * len(after),
-            out_specs=fixed(shape),
+            out_specs=(fixed(shape),) * relays,
+            scratch_shapes=[pltpu.VMEM((groups, table.shape[1], 2 * LANES), F32)],
         ),
         compiler_params=params(),
-        cost_estimate=cost(4),
+        cost_estimate=cost(60),
         name="expand",
-    )(half, own, far, table, *after)
+    )(half, relay, own, far, table, *riding, *after)
 
 
 PLANES = 8
@@ -617,122 +658,108 @@
 
 
 def x_then_z(
-    received_ref, mixed_ref, table_x, table_z, out_ref, real_ref, imag_ref, planes, blocks
+    received, mixed_ref, table_x, table_z, out_ref, real_ref, imag_ref, planes
 ):
-    relays = received_ref.shape[0]
-    part = 2 * MX // relays
-    rows = NX * planes // blocks
-    block = pl.program_id(1)
-
-    @pl.when(block == 0)
-    def _():
-        for y in range(0, planes, 2):
-            pair = [
-                jnp.concatenate(
-                    [
-                        received_ref[r, side, at * part : (at + 1) * part, :]
-                        for side in range(2)
-                        for r in range(relays)
-                    ],
-                    axis=0,
-                ).astype(BF16)
-                for at in (y, y + 1)
-            ]
-            found = dot(table_x[...], jnp.concatenate(pair, axis=1))
-            for place in range(2):
-                lane = slice(place * LANES, (place + 1) * LANES)
-                real_ref[pl.ds(y + place, NX, stride=planes), :] = found[:NX, lane]
-                imag_ref[pl.ds(y + place, NX, stride=planes), :] = found[NX:, lane]
-
+    part = 2 * MX // len(received)
+    for y in range(0, planes, 2):
+        pair = [
+            jnp.concatenate(
+                [
+                    ref[side, at * part : (at + 1) * part, :]
+                    for side in range(2)
+                    for ref in received
+                ],
+                axis=0,
+            ).astype(BF16)
+            for at in (y, y + 1)
+        ]
+        found = dot(table_x[0], jnp.concatenate(pair, axis=1))
+        for place in range(2):
+            lane = slice(place * LANES, (place + 1) * LANES)
+            real_ref[pl.ds(y + place, NX, stride=planes), :] = found[:NX, lane]
+            imag_ref[pl.ds(y + place, NX, stride=planes), :] = found[NX:, lane]
+    rows = NX * planes
     step = min(rows, 256)
     for start in range(0, rows, step):
-        place = pl.ds(pl.multiple_of(block * rows + start, step), step)
+        place = slice(start, start + step)
         line = jnp.concatenate([real_ref[place, :], imag_ref[place, :]], axis=1).astype(BF16)
         found = dot(line, table_z[...])
         for c in range(GROUP):
-            mixed = mixed_ref[c, start : start + step, :].astype(F32)
-            out_ref[c, start : start + step, :] = (
-                found[:, c * NZ : (c + 1) * NZ] + mixed
-            ).astype(BF16)
-
-
-def grid_plain(*refs, planes, blocks):
-    x_then_z(*refs, planes, blocks)
-
-
-def grid_skip(received_ref, skip_ref, *refs, planes, blocks, root):
-    mixed_ref, table_x, table_z = refs[:3]
-    out_ref, total_ref, real_ref, imag_ref = refs[-4:]
-
-    @pl.when((pl.program_id(0) == 0) & (pl.program_id(1) == 0))
-    def _():
-        total = jnp.sum(skip_ref[:, 0], axis=0)
-        total_ref[...] = total[:, : total_ref.shape[1]] / root
-
-    x_then_z(
-        received_ref, mixed_ref, table_x, table_z, out_ref, real_ref, imag_ref, planes, blocks
-    )
-
-
-def grid_of(received, mixed, first, groups, planes, root=None, after=()):
-    relays, _, rows, _ = received.shape
+            mixed = mixed_ref[c, place, :].astype(F32)
+            out_ref[c, place, :] = (found[:, c * NZ : (c + 1) * NZ] + mixed).astype(BF16)
+
+
+def grid_body(relay_ref, *refs, planes, relays, root):
+    received, refs = refs[:relays], refs[relays:]
+    if root is None:
+        mixed_ref, table_x, table_z = refs[:3]
+        out_ref, real_ref, imag_ref = refs[-3:]
+    else:
+        skips, refs = refs[:relays], refs[relays:]
+        mixed_ref, table_x, table_z = refs[:3]
+        out_ref, total_ref, real_ref, imag_ref = refs[-4:]
+
+        @pl.when(pl.program_id(0) == 0)
+        def _():
+            total = sum(ref[0] for ref in skips)
+            total_ref[...] = total[:, : total_ref.shape[1]] / root
+
+    x_then_z(received, mixed_ref, table_x, table_z, out_ref, real_ref, imag_ref, planes)
+
+
+def grid_of(relay, received, mixed, first, groups, planes, root=None, after=()):
+    relays = len(received)
     channels = mixed.shape[0]
-    blocks = 1
-    part = 2 * MX // relays
-    per_group = planes * part
-    spec = pl.BlockSpec((GROUP, NX * planes // blocks, NZ), lambda g, r: (g + first, r, 0))
-    in_specs = [
-        pl.BlockSpec((relays, 2, per_group, LANES), lambda g, r: (0, 0, g, 0)),
-        spec,
-        whole((2 * NX, 4 * MX)),
-        whole((2 * LANES, GROUP * NZ)),
-    ]
-    operands = [received, mixed, x_inverse_table(2 * relays), z_inverse_table()]
+    per_group = planes * 2 * MX // relays
+    spec = pl.BlockSpec((GROUP, NX * planes, NZ), lambda g, at: (g + first, 0, 0))
+    in_specs = [pl.BlockSpec((2, per_group, LANES), lambda g, at: (0, g, 0))] * relays
+    operands = list(received)
     out_shape = (jax.ShapeDtypeStruct(mixed.shape, BF16),)
     out_specs = (spec,)
-    body = functools.partial(grid_plain, planes=planes, blocks=blocks)
     if root is not None:
         extra = groups * per_group // channels
-        in_specs.insert(1, pl.BlockSpec((relays, 1, channels, LANES), lambda g, r: (0, 0, extra, 0)))
-        operands.insert(1, received)
+        in_specs += [pl.BlockSpec((1, channels, LANES), lambda g, at: (0, extra, 0))] * relays
+        operands += received
         out_shape += (jax.ShapeDtypeStruct((channels, channels), F32),)
-        out_specs += (whole((channels, channels)),)
-        body = functools.partial(grid_skip, planes=planes, blocks=blocks, root=root)
-    operands += after
-    in_specs += [ANYWHERE] * len(after)
+        out_specs += (fixed((channels, channels)),)
+    in_specs += [
+        spec,
+        pl.BlockSpec((1, 2 * NX, 4 * MX), lambda g, at: (at[0], 0, 0)),
+        fixed((2 * LANES, GROUP * NZ)),
+    ] + [ANYWHERE] * len(after)
+    operands += [mixed, x_inverse_table(relays), z_inverse_table(), *after]
     return pl.pallas_call(
-        body,
+        functools.partial(grid_body, planes=planes, relays=relays, root=root),
         out_shape=out_shape,
-        grid=(groups, blocks),
-        in_specs=in_specs,
-        out_specs=out_specs,
-        scratch_shapes=[
-            pltpu.VMEM((NX * planes, LANES), F32),
-            pltpu.VMEM((NX * planes, LANES), F32),
-        ],
-        input_output_aliases={1 if root is None else 2: 0},
-        compiler_params=params(2),
+        grid_spec=pltpu.PrefetchScalarGridSpec(
+            num_scalar_prefetch=1,
+            grid=(groups,),
+            in_specs=in_specs,
+            out_specs=out_specs,
+            scratch_shapes=[
+                pltpu.VMEM((NX * planes, LANES), F32),
+                pltpu.VMEM((NX * planes, LANES), F32),
+            ],
+        ),
+        input_output_aliases={1 + (relays if root is None else 2 * relays): 0},
+        compiler_params=params(),
         cost_estimate=cost(9),
         name="to_grid",
-    )(*operands)
-
-
-def cross_body(own_ref, left_ref, right_ref, *refs, samples):
-    out_ref = refs[-1]
-    lanes = out_ref.shape[-1]
-    channels = left_ref.shape[1] // 2
-    own = right_ref.shape[2]
+    )(relay, *operands)
+
+
+def cross_body(*refs, samples):
+    lefts, rights, out_ref = refs[:samples], refs[samples : 2 * samples], refs[-1]
+    channels, own, lanes = out_ref.shape[1:]
     kz = lax.broadcasted_iota(jnp.int32, (own, lanes), 1) // (2 * MY) % MZ
     scale = jnp.where(kz == 0, 1.0, 2.0) / float(NX * NY * NZ)
-    rights = [
-        (right_ref[b, 0] * scale, right_ref[b, 1] * scale) for b in range(samples)
-    ]
+    scaled = [(ref[:own, :] * scale, ref[own : 2 * own, :] * scale) for ref in rights]
     for i in range(channels):
         real = imag = None
         for b in range(samples):
-            left_real = left_ref[b, i : i + 1, :]
-            left_imag = left_ref[b, channels + i : channels + i + 1, :]
-            right_real, right_imag = rights[b]
+            left_real = lefts[b][i : i + 1, :]
+            left_imag = lefts[b][channels + i : channels + i + 1, :]
+            right_real, right_imag = scaled[b]
             one = left_real * right_real + left_imag * right_imag
             two = left_real * right_imag - left_imag * right_real
             real = one if real is None else real + one
@@ -741,26 +768,23 @@
         out_ref[1, i] = imag
 
 
-def cross(left, right, place, own, after=()):
-    samples, _, channels, modes = right.shape
+def cross(lefts, rights, after=()):
+    rows, modes = lefts[0].shape
+    channels = rows // 2
+    own = (rights[0].shape[0] - SUBLANES) // 2
     lanes = 2 * MY * MZ
     return pl.pallas_call(
-        functools.partial(cross_body, samples=samples),
+        functools.partial(cross_body, samples=len(lefts)),
         out_shape=jax.ShapeDtypeStruct((2, channels, own, modes), F32),
-        grid_spec=pltpu.PrefetchScalarGridSpec(
-            num_scalar_prefetch=1,
-            grid=(modes // lanes,),
-            in_specs=[
-                pl.BlockSpec((samples, 2 * channels, lanes), lambda k, at: (0, 0, k)),
-                pl.BlockSpec((samples, 2, own, lanes), lambda k, at: (0, 0, at[0], k)),
-            ]
-            + [ANYWHERE] * len(after),
-            out_specs=pl.BlockSpec((2, channels, own, lanes), lambda k, at: (0, 0, 0, k)),
-        ),
+        grid=(modes // lanes,),
+        in_specs=[pl.BlockSpec((rows, lanes), lambda k: (0, k))] * len(lefts)
+        + [pl.BlockSpec((2 * own + SUBLANES, lanes), lambda k: (0, k))] * len(rights)
+        + [ANYWHERE] * len(after),
+        out_specs=pl.BlockSpec((2, channels, own, lanes), lambda k: (0, 0, 0, k)),
         compiler_params=params(),
         cost_estimate=cost(6),
         name="cross",
-    )(place, left, right, *after)
+    )(*lefts, *rights, *after)
 
 
 def exchange_near(values):
@@ -769,6 +793,14 @@
     return lax.all_to_all(
         values, "space", split_axis=0, concat_axis=0, axis_index_groups=groups, tiled=True
     )
+
+
+def spread(blocks, axis):
+    size = lax.axis_size(axis)
+    return [blocks[0]] + [
+        lax.ppermute(blocks[d], axis, [(s, s ^ d) for s in range(size)])
+        for d in range(1, len(blocks))
+    ]
 
 
 def exchange_far(values, turned=False):
@@ -916,13 +948,16 @@
     samples, channels, _, planes, _ = inputs.shape
     spaces = lax.axis_size("space")
     batches = lax.axis_size("batch")
-    if samples != 1 or spaces % 2 or (2 * MX) % spaces or planes % 16 or channels % (4 * GROUP):
+    if samples != 1 or spaces < 2 or spaces & (spaces - 1) or (2 * MX) % spaces or planes % 16 or channels % (4 * GROUP):
+        return general(inputs, pre_act, cotangent, spectral_weight, skip_weight)
+    if batches & (batches - 1) or channels % (SUBLANES * batches):
         return general(inputs, pre_act, cotangent, spectral_weight, skip_weight)
     kx_local = 2 * MX // spaces
     flat = (channels, NX * planes, NZ)
     groups = channels // GROUP
     inputs, pre_act, cotangent = (v.reshape(flat) for v in (inputs, pre_act, cotangent))
     half = (lax.axis_index("space") // (spaces // 2)).astype(jnp.int32).reshape(1)
+    relay = (lax.axis_index("space") % (spaces // 2)).astype(jnp.int32).reshape(1)
     batch = lax.axis_index("batch").astype(jnp.int32).reshape(1)
     middle = groups // 2
     (send_u,) = forward((inputs,), 0, groups, planes, spaces, False)
@@ -934,25 +969,37 @@
     part_u = partial_sums(half, near_u, groups, kx_local, "partial_u", after=(send_e,))
     far_u = exchange_far(part_u)
     mixed, skip_part = mix(inputs, cot_pre, skip_weight, planes, after=(part_u,))
-    hat_u = finish_u(half, near_u, far_u, skip_part, kx_local)
-    all_u = lax.all_gather(hat_u, "batch")
-    part_e = partial_sums(half, near_e, groups, kx_local, "partial_e", after=(hat_u,))
+    part_e = partial_sums(half, near_e, groups, kx_local, "partial_e", riding=(skip_part,))
     far_e = exchange_far(part_e)
-    hat_e, rounded, modes_a = finish_e(
-        half, near_e, far_e, spectral_weight, kx_local, after=(hat_u,)
+    hat_u = finish_u(half, near_u, far_u, channels, kx_local, after=(part_e,))
+    all_u = spread([hat_u] * batches, "batch")
+    own_e, rounded, modes_a = finish_e(
+        batch, half, near_e, far_e, spectral_weight, skip_part, kx_local, batches, tuple(all_u[1:])
     )
     far_a = exchange_far(modes_a)
-    all_e = lax.all_gather(hat_e, "batch")
-    modes_b = finish_rest(rounded, spectral_weight, all_u, kx_local)
+    all_e = spread(own_e, "batch")
+    modes_b = finish_rest(rounded, spectral_weight, kx_local)
+    modes_b, far_a = lax.optimization_barrier((modes_b, far_a))
     far_b = exchange_far(modes_b, turned=True)
-    send_a = expand(half, modes_a, far_a, spaces // 2, middle, kx_local, after=(modes_b,))
-    near_a = exchange_near(send_a)
-    send_b = expand(half, modes_b, far_b, spaces // 2, middle, kx_local, after=(send_a,))
-    near_b = exchange_near(send_b)
-    grad_spectral = cross(all_u, all_e, batch, channels // batches, after=(send_b,))
-    (grad_inputs,) = grid_of(near_a, mixed, 0, middle, planes)
+    send_a = expand(half, relay, modes_a, far_a, spaces // 2, middle, kx_local)
+    near_a = spread(send_a, "space")
+    grad_spectral = cross(all_u, all_e, after=send_a[:1])
+    send_b = expand(
+        half,
+        relay,
+        modes_b,
+        far_b,
+        spaces // 2,
+        middle,
+        kx_local,
+        all_e,
+        channels,
+        (grad_spectral,),
+    )
+    near_b = spread(send_b, "space")
+    (grad_inputs,) = grid_of(relay, near_a, mixed, 0, middle, planes, after=send_b[:1])
     root = math.sqrt(samples * batches * NX * NY * NZ)
-    grad_inputs, grad_skip = grid_of(near_b, grad_inputs, middle, middle, planes, root, (grad_spectral,))
+    grad_inputs, grad_skip = grid_of(relay, near_b, grad_inputs, middle, middle, planes, root)
     return (
         grad_inputs.reshape(samples, channels, NX, planes, NZ),
         grad_spectral,

time: 207 us -> 187 us (0.903)
  between operations: 14.1 us -> 0.73 us
  waiting for transfers between devices: 52.3 us -> 44.9 us
    ppermute x4, waiting for transfers between devices: 52.2 us -> 25.3 us  [exchange_far(): return lax.ppermute(values, 'space', pairs)]
    ppermute x0 -> x12, starting transfers between devices: none -> 11 us  [spread(): lax.ppermute(blocks[d], axis, [(s, s ^ d) for s in range(size)])]
    ppermute x0 -> x12, waiting for transfers between devices: none -> 10.5 us  [spread(): lax.ppermute(blocks[d], axis, [(s, s ^ d) for s in range(size)])]
    all_to_all x4 -> x2, starting transfers between devices: 19.9 us -> 9.86 us  [exchange_near(): lax.all_to_all(values, 'space', split_axis=0, concat_axis=0, axis_index_g...]
    all_to_all x4 -> x2, waiting for transfers between devices: 0.04 us -> 9.17 us  [exchange_near(): lax.all_to_all(values, 'space', split_axis=0, concat_axis=0, axis_index_g...]
    unnamed x16 -> x32, local copies, waits for them, and re-layouts: 4.07 us -> 4.33 us
  transfers between devices with their start and end apart: 10 -> 18, of which waited for: 4 -> 8; matrix products, arithmetic and copies ran while one was open for 0% -> 0% of each run, Pallas kernels for 43% -> 44%
where the time goes in v3:
time: 187 us; the launch traced here: 186 us
  Pallas kernels  110 us (59%)
  waiting for transfers between devices  44.9 us (24%)
  starting transfers between devices  26.5 us (14%)
  local copies, waits for them, and re-layouts  4.33 us (2%)
    pallas_call x2, Pallas kernels, forward(): pl.pallas_call(functools.partial(body, planes=planes, spaces=spaces, bloc...  36.3 us
    ppermute x4, waiting for transfers between devices, exchange_far(): return lax.ppermute(values, 'space', pairs)  25.3 us
    pallas_call x1, Pallas kernels, mix(): pl.pallas_call(functools.partial(mix_body, planes=planes, count=count), o...  22.3 us
    pallas_call x2, Pallas kernels, grid_of(): pl.pallas_call(functools.partial(grid_body, planes=planes, relays=relays,...  17.7 us
    ppermute x12, starting transfers between devices, spread(): lax.ppermute(blocks[d], axis, [(s, s ^ d) for s in range(size)])  11 us
    ppermute x12, waiting for transfers between devices, spread(): lax.ppermute(blocks[d], axis, [(s, s ^ d) for s in range(size)])  10.5 us
    all_to_all x2, starting transfers between devices, exchange_near(): lax.all_to_all(values, 'space', split_axis=0, concat_axis=0, axis_index_g...  9.86 us
    all_to_all x2, waiting for transfers between devices, exchange_near(): lax.all_to_all(values, 'space', split_axis=0, concat_axis=0, axis_index_g...  9.17 us
  transfers between devices with their start and end apart: 18, of which 8 were waited for; matrix products, arithmetic and copies ran while one was open for 0% of the time, Pallas kernels for 44%

profile of v3, /device:TPU:0, one launch (start us, length us, event | category | flops | bytes accessed | tf_op | source)
XLA Modules:
  0.0 186.4 jit_solution(15613773559703196414)
XLA Ops:
  0.6 11.4 %forward_u.1.refs_0_ = f32[4,2,512,128]{3,2,1,0:T(8,128)} custom-call(bf16[32,2048,128]{2,1,0:T(8,128)(2,1)} %bitcast.9, bf16[1024,256]{1,0:T(8,128)(2,1)} %constant.46.clone.table_z, bf16[64,256]{1,0:T(8,128)(2,1)} %constant.47.clone.table_x), custom_call_target="tpu_custom_call" | custom-call | flops 22000001024 | bytes 1 | tf_op jit(solution)/shard_map/forward_u/pallas_call | solution.py:203
  12.0 5.2 %all-to-all-start.1 = ((f32[4,2,512,128]{3,2,1,0:T(8,128)}), f32[4,2,512,128]{3,2,1,0:T(8,128)}, u32[]{:S(2)}, u32[]{:S(2)}) async-start(f32[4,2,512,128]{3,2,1,0:T(8,128)} %forward_u.1.refs_0_), calls=%async_computation.1 | async-start | bytes 4194304 | tf_op jit(solution)/shard_map/all_to_all | solution.py:793
  17.2 25.0 %forward_e.1 = (f32[4,2,512,128]{3,2,1,0:T(8,128)}, bf16[32,2048,128]{2,1,0:T(8,128)(2,1)}) custom-call(bf16[32,2048,128]{2,1,0:T(8,128)(2,1)} %bitcast.7, bf16[32,2048,128]{2,1,0:T(8,128)(2,1)} %bitcast.8, bf16[1024,256]{1,0:T(8,128)(2,1)} %constant.46.clone.table_z, bf16[64,256]{1,0:T(8,128)(2,1)} %constant.47.clone.table_x, ...), custom_call_target="tpu_custom_call" | custom-call | flops 49999998976 | bytes 1 | tf_op jit(solution)/shard_map/forward_e/pallas_call | solution.py:203
  43.0 4.6 %all-to-all-start = ((f32[4,2,512,128]{3,2,1,0:T(8,128)}), f32[4,2,512,128]{3,2,1,0:T(8,128)}, u32[]{:S(2)}, u32[]{:S(2)}) async-start(f32[4,2,512,128]{3,2,1,0:T(8,128)} %get-tuple-element.25.refs_0_), calls=%async_computation | async-start | bytes 4194304 | tf_op jit(solution)/shard_map/all_to_all | solution.py:793
  47.6 2.8 %partial_u.1.refs_0_ = f32[1024,128]{1,0:T(8,128)} custom-call(s32[1]{0:T(128)} %bitcast.1.half_ref, f32[4,2,512,128]{3,2,1,0:T(8,128)} %all-to-all-done.1.near_ref, bf16[2,256,1536]{2,1,0:T(8,128)(2,1)} %constant.48.clone.table, f32[4,2,512,128]{3,2,1,0:T(8,128)} %get-tuple-element.25.refs_0_), custom_call_target="tpu_custom_call" | custom-call | flops 6000000000 | bytes 1 | tf_op jit(solution)/shard_map/partial_u/pallas_call | solution.py:272
  50.4 2.7 %collective-permute-start.1 = (f32[1024,128]{1,0:T(8,128)}, f32[1024,128]{1,0:T(8,128)S(1)}, u32[]{:S(2)}, u32[]{:S(2)}) collective-permute-start(f32[1024,128]{1,0:T(8,128)} %partial_u.1.refs_0_), channel_id=1, source_target_pairs={{0,4},{1,5},{2,6},{3,7},{4,0},{5,1},{6,2},{7,3},{8,12},{9,13},{10,... | collective-permute-start | bytes 1572872 | tf_op jit(solution)/shard_map/ppermute | solution.py:810
  53.2 22.3 %mix.1 = (bf16[32,2048,128]{2,1,0:T(8,128)(2,1)}, f32[32,128]{1,0:T(8,128)}) custom-call(bf16[32,2048,128]{2,1,0:T(8,128)(2,1)} %bitcast.10, bf16[32,2048,128]{2,1,0:T(8,128)(2,1)} %get-tuple-element.26.cot_ref, bf16[32,32]{1,0:T(8,128)(2,1)} %weight_ref.3, f32[1024,128]{1,0:T(8,128)} %partial_u.1.refs_0_), custom_call_target="tpu_custom_call" | custom-call | flops 44000002048 | bytes 1 | tf_op jit(solution)/shard_map/mix/pallas_call | solution.py:644
  75.4 8.4 %all-to-all-done.near_ref = f32[4,2,512,128]{3,2,1,0:T(8,128)} async-done(((f32[4,2,512,128]{3,2,1,0:T(8,128)}), f32[4,2,512,128]{3,2,1,0:T(8,128)}, u32[]{:S(2)}, u32[]{:S(2)}) %all-to-all-start) | async-done | bytes 2097184 | tf_op jit(solution)/shard_map/all_to_all | solution.py:793
  83.8 2.8 %partial_e.1.refs_0_ = f32[1056,128]{1,0:T(8,128)} custom-call(s32[1]{0:T(128)} %bitcast.1.half_ref, f32[4,2,512,128]{3,2,1,0:T(8,128)} %all-to-all-done.near_ref, bf16[2,256,1536]{2,1,0:T(8,128)(2,1)} %constant.48.clone.table, f32[32,128]{1,0:T(8,128)} %get-tuple-element.27.refs_0_.skip_ref), custom_call_target="tpu_custom_call" | custom-call | flops 6000000000 | bytes 1 | tf_op jit(solution)/shard_map/partial_e/pallas_call | solution.py:272
  88.0 3.6 %finish_u.1.refs_0_ = f32[64,2048]{1,0:T(8,128)} custom-call(s32[1]{0:T(128)} %bitcast.1.half_ref, f32[4,2,512,128]{3,2,1,0:T(8,128)} %all-to-all-done.1.near_ref, f32[1024,128]{1,0:T(8,128)} %copy-done.3, bf16[2,256,1536]{2,1,0:T(8,128)(2,1)} %constant.48.clone.table, f32[1056,128]{1,0:T(8,128)} %partial_e.1.refs_0_), custom_call_target="tpu_custom_call" | custom-call | flops 8000000000 | bytes 1 | tf_op jit(solution)/shard_map/finish_u/pallas_call | solution.py:346
  93.5 18.9 %collective-permute-done.far_ref = f32[1056,128]{1,0:T(8,128)S(1)} collective-permute-done((f32[1056,128]{1,0:T(8,128)}, f32[1056,128]{1,0:T(8,128)S(1)}, u32[]{:S(2)}, u32[]{:S(2)}) %collective-permute-start) | collective-permute-done | bytes 540704 | tf_op jit(solution)/shard_map/ppermute | solution.py:810
  112.4 4.7 %collective-permute-done.4.refs_2_.refs_3_ = f32[64,2048]{1,0:T(8,128)} collective-permute-done((f32[64,2048]{1,0:T(8,128)}, f32[64,2048]{1,0:T(8,128)}, u32[]{:S(2)}, u32[]{:S(2)}) %collective-permute-start.4) | collective-permute-done | bytes 524320 | tf_op jit(solution)/shard_map/ppermute | solution.py:801
  117.2 7.6 %finish_e.1 = (f32[24,2048]{1,0:T(8,128)}, f32[24,2048]{1,0:T(8,128)}, f32[24,2048]{1,0:T(8,128)}, f32[24,2048]{1,0:T(8,128)}, f32[2,32,2048]{2,1,0:T(8,128)}, /*index=5*/f32[512,128]{1,0:T(8,128)}) custom-call(s32[1]{0:T(128)} %bitcast.2.batch_ref, s32[1]{0:T(128)} %bitcast.1.half_ref, f32[4,2,512,128]{3,2,1,0:T(8,128)} %all-to-all-done.near_ref, ...), custom_call_target="tpu_custom_call" | custom-call | flops 16000000000 | bytes 1 | tf_op jit(solution)/shard_map/finish_e/pallas_call | solution.py:452
  124.8 2.4 %collective-permute-start.5 = (f32[512,128]{1,0:T(8,128)}, f32[512,128]{1,0:T(8,128)S(1)}, u32[]{:S(2)}, u32[]{:S(2)}) collective-permute-start(f32[512,128]{1,0:T(8,128)} %get-tuple-element.29.own_ref), channel_id=1, source_target_pairs={{0,4},{1,5},{2,6},{3,7},{4,0},{5,1},{6,2},{7,3},{8,12},{9,13},{10,... | collective-permute-start | bytes 786440 | tf_op jit(solution)/shard_map/ppermute | solution.py:810
  127.2 4.9 %finish_rest.1.own_ref = f32[512,128]{1,0:T(8,128)} custom-call(f32[2,32,2048]{2,1,0:T(8,128)} %get-tuple-element.28.rounded, bf16[2,32,32,2048]{3,2,1,0:T(8,128)(2,1)} %weight_ref.5), custom_call_target="tpu_custom_call" | custom-call | flops 10000000000 | bytes 1 | tf_op jit(solution)/shard_map/finish_rest/pallas_call | solution.py:486
  132.1 1.8 collective-permute-start.8
  133.9 6.0 %collective-permute-done.5.far_ref = f32[512,128]{1,0:T(8,128)S(1)} collective-permute-done((f32[512,128]{1,0:T(8,128)}, f32[512,128]{1,0:T(8,128)S(1)}, u32[]{:S(2)}, u32[]{:S(2)}) %collective-permute-start.5) | collective-permute-done | bytes 262176 | tf_op jit(solution)/shard_map/ppermute | solution.py:810
  140.6 2.9 %expand.2 = (f32[2,256,128]{2,1,0:T(8,128)}, f32[2,256,128]{2,1,0:T(8,128)}, f32[2,256,128]{2,1,0:T(8,128)}, f32[2,256,128]{2,1,0:T(8,128)}) custom-call(s32[1]{0:T(128)} %bitcast.1.half_ref, s32[1]{0:T(128)} %bitcast.relay_ref, f32[512,128]{1,0:T(8,128)} %get-tuple-element.29.own_ref, f32[512,128]{1,0:T(8,128)} %copy-done.11, ...), custom_call_target="tpu_custom_call" | custom-call | flops 120000004096 | bytes 1 | tf_op jit(solution)/shard_map/expand/pallas_call | solution.py:550
  145.2 2.1 %collective-permute-start.14 = (f32[2,256,128]{2,1,0:T(8,128)}, f32[2,256,128]{2,1,0:T(8,128)S(1)}, u32[]{:S(2)}, u32[]{:S(2)}) collective-permute-start(f32[2,256,128]{2,1,0:T(8,128)} %get-tuple-element.42), channel_id=1, source_target_pairs={{0,2},{1,3},{2,0},{3,1},{4,6},{5,7},{6,4},{7,5},{8,10},{9,11},{10,... | collective-permute-start | bytes 786440 | tf_op jit(solution)/shard_map/ppermute | solution.py:801
  148.0 5.8 %cross.1.refs_4_ = f32[2,32,8,2048]{3,2,1,0:T(8,128)} custom-call(f32[64,2048]{1,0:T(8,128)} %finish_u.1.refs_0_, f32[64,2048]{1,0:T(8,128)} %copy-done.1, f32[64,2048]{1,0:T(8,128)} %copy-done.2, f32[64,2048]{1,0:T(8,128)} %collective-permute-done.4.refs_2_.refs_3_, f32[24,2048]{1,0:T(8,128)} %get-tuple-element.31.refs_4_.refs_0_, f32[24,2048]{1,0:T(8,128)} %copy-done.12, ...), custom_call_target="tpu_custom_call" | custom-call | flops 12000000000 | bytes 1 | tf_op jit(solution)/shard_map/cross/pallas_call | solution.py:776
  154.9 3.0 %expand.3 = (f32[2,288,128]{2,1,0:T(8,128)}, f32[2,288,128]{2,1,0:T(8,128)}, f32[2,288,128]{2,1,0:T(8,128)}, f32[2,288,128]{2,1,0:T(8,128)}) custom-call(s32[1]{0:T(128)} %bitcast.1.half_ref, s32[1]{0:T(128)} %bitcast.relay_ref, f32[512,128]{1,0:T(8,128)} %finish_rest.1.own_ref, f32[512,128]{1,0:T(8,128)} %copy-done.10, ...), custom_call_target="tpu_custom_call" | custom-call | flops 120000004096 | bytes 1 | tf_op jit(solution)/shard_map/expand/pallas_call | solution.py:550
  161.4 4.2 %collective-permute-done.15.refs_3_ = f32[2,256,128]{2,1,0:T(8,128)S(1)} collective-permute-done((f32[2,256,128]{2,1,0:T(8,128)}, f32[2,256,128]{2,1,0:T(8,128)S(1)}, u32[]{:S(2)}, u32[]{:S(2)}) %collective-permute-start.15) | collective-permute-done | bytes 262176 | tf_op jit(solution)/shard_map/ppermute | solution.py:801
  166.4 8.8 %to_grid.2.refs_8_ = bf16[32,2048,128]{2,1,0:T(8,128)(2,1)} custom-call(s32[1]{0:T(128)} %bitcast.relay_ref, f32[2,256,128]{2,1,0:T(8,128)} %get-tuple-element.36.refs_8_.refs_0_, f32[2,256,128]{2,1,0:T(8,128)} %copy-done.7, f32[2,256,128]{2,1,0:T(8,128)} %copy-done.8, f32[2,256,128]{2,1,0:T(8,128)} %copy-done.9, ...), custom_call_target="tpu_custom_call", output_to_operand_aliasing={{}: (5, {})} | custom-call | flops 17999998976 | bytes 1 | tf_op jit(solution)/shard_map/to_grid/pallas_call | solution.py:731
  177.5 8.9 %to_grid.3 = (bf16[32,2048,128]{2,1,0:T(8,128)(2,1)}, f32[32,32]{1,0:T(8,128)}) custom-call(s32[1]{0:T(128)} %bitcast.relay_ref, f32[2,288,128]{2,1,0:T(8,128)} %get-tuple-element.37.refs_7_.refs_0_.refs_4_, f32[2,288,128]{2,1,0:T(8,128)} %copy-done.4, f32[2,288,128]{2,1,0:T(8,128)} %copy-done.5, ...), custom_call_target="tpu_custom_call", output_to_operand_aliasing={{0}: (9, {})} | custom-call | flops 17999998976 | bytes 1 | tf_op jit(solution)/shard_map/to_grid/pallas_call | solution.py:731
  (57 shorter events, 14.7 us)
Async XLA Ops:
  12.0 31.0 %all-to-all-start.1 = ((f32[4,2,512,128]{3,2,1,0:T(8,128)}), f32[4,2,512,128]{3,2,1,0:T(8,128)}, u32[]{:S(2)}, u32[]{:S(2)}) async-start(f32[4,2,512,128]{3,2,1,0:T(8,128)} %forward_u.1.refs_0_), calls=%async_computation.1 | async-start | bytes 4194304 | tf_op jit(solution)/shard_map/all_to_all | solution.py:793
  43.0 40.9 %all-to-all-start = ((f32[4,2,512,128]{3,2,1,0:T(8,128)}), f32[4,2,512,128]{3,2,1,0:T(8,128)}, u32[]{:S(2)}, u32[]{:S(2)}) async-start(f32[4,2,512,128]{3,2,1,0:T(8,128)} %get-tuple-element.25.refs_0_), calls=%async_computation | async-start | bytes 4194304 | tf_op jit(solution)/shard_map/all_to_all | solution.py:793
  50.4 36.8 %collective-permute-start.1 = (f32[1024,128]{1,0:T(8,128)}, f32[1024,128]{1,0:T(8,128)S(1)}, u32[]{:S(2)}, u32[]{:S(2)}) collective-permute-start(f32[1024,128]{1,0:T(8,128)} %partial_u.1.refs_0_), channel_id=1, source_target_pairs={{0,4},{1,5},{2,6},{3,7},{4,0},{5,1},{6,2},{7,3},{8,12},{9,13},{10,... | collective-permute-start | bytes 1572872 | tf_op jit(solution)/shard_map/ppermute | solution.py:810
  86.7 25.7 %collective-permute-start = (f32[1056,128]{1,0:T(8,128)}, f32[1056,128]{1,0:T(8,128)S(1)}, u32[]{:S(2)}, u32[]{:S(2)}) collective-permute-start(f32[1056,128]{1,0:T(8,128)} %partial_e.1.refs_0_), channel_id=1, source_target_pairs={{0,4},{1,5},{2,6},{3,7},{4,0},{5,1},{6,2},{7,3},{8,12},{9,13},{10,... | collective-permute-start | bytes 1622024 | tf_op jit(solution)/shard_map/ppermute | solution.py:810
  91.6 20.8 %collective-permute-start.2 = (f32[64,2048]{1,0:T(8,128)}, f32[64,2048]{1,0:T(8,128)S(1)}, u32[]{:S(2)}, u32[]{:S(2)}) collective-permute-start(f32[64,2048]{1,0:T(8,128)} %finish_u.1.refs_0_), channel_id=1, source_target_pairs={{0,8},{8,0},{16,24},{24,16},{1,9},{9,1},{17,25},{25,17},{2,10},{10... | collective-permute-start | bytes 1572872 | tf_op jit(solution)/shard_map/ppermute | solution.py:801
  91.6 20.8 %collective-permute-start.3 = (f32[64,2048]{1,0:T(8,128)}, f32[64,2048]{1,0:T(8,128)S(1)}, u32[]{:S(2)}, u32[]{:S(2)}) collective-permute-start(f32[64,2048]{1,0:T(8,128)} %finish_u.1.refs_0_), channel_id=1, source_target_pairs={{0,16},{8,24},{16,0},{24,8},{1,17},{9,25},{17,1},{25,9},{2,18},{10... | collective-permute-start | bytes 1572872 | tf_op jit(solution)/shard_map/ppermute | solution.py:801
  93.1 24.0 %collective-permute-start.4 = (f32[64,2048]{1,0:T(8,128)}, f32[64,2048]{1,0:T(8,128)}, u32[]{:S(2)}, u32[]{:S(2)}) collective-permute-start(f32[64,2048]{1,0:T(8,128)} %finish_u.1.refs_0_), channel_id=1, source_target_pairs={{0,24},{8,16},{16,8},{24,0},{1,25},{9,17},{17,9},{25,1},{2,26},{10... | collective-permute-start | bytes 1572872 | tf_op jit(solution)/shard_map/ppermute | solution.py:801
  112.4 4.7 %copy-start = (f32[1056,128]{1,0:T(8,128)}, f32[1056,128]{1,0:T(8,128)S(1)}, u32[]{:S(2)}) copy-start(f32[1056,128]{1,0:T(8,128)S(1)} %collective-permute-done.far_ref) | copy-start | bytes 1622020
  112.4 4.7 %copy-start.1 = (f32[64,2048]{1,0:T(8,128)}, f32[64,2048]{1,0:T(8,128)S(1)}, u32[]{:S(2)}) copy-start(f32[64,2048]{1,0:T(8,128)S(1)} %collective-permute-done.2.refs_0_.refs_1_) | copy-start | bytes 1572868
  112.4 4.7 %copy-start.2 = (f32[64,2048]{1,0:T(8,128)}, f32[64,2048]{1,0:T(8,128)S(1)}, u32[]{:S(2)}) copy-start(f32[64,2048]{1,0:T(8,128)S(1)} %collective-permute-done.3.refs_1_.refs_2_) | copy-start | bytes 1572868
  124.8 15.1 %collective-permute-start.5 = (f32[512,128]{1,0:T(8,128)}, f32[512,128]{1,0:T(8,128)S(1)}, u32[]{:S(2)}, u32[]{:S(2)}) collective-permute-start(f32[512,128]{1,0:T(8,128)} %get-tuple-element.29.own_ref), channel_id=1, source_target_pairs={{0,4},{1,5},{2,6},{3,7},{4,0},{5,1},{6,2},{7,3},{8,12},{9,13},{10,... | collective-permute-start | bytes 786440 | tf_op jit(solution)/shard_map/ppermute | solution.py:810
  127.1 4.9 %copy-start.15 = (f32[24,2048]{1,0:T(8,128)S(1)}, f32[24,2048]{1,0:T(8,128)}, u32[]{:S(2)}) copy-start(f32[24,2048]{1,0:T(8,128)} %get-tuple-element.32) | copy-start | bytes 589828
  127.1 4.9 %copy-start.14 = (f32[24,2048]{1,0:T(8,128)S(1)}, f32[24,2048]{1,0:T(8,128)}, u32[]{:S(2)}) copy-start(f32[24,2048]{1,0:T(8,128)} %get-tuple-element.33) | copy-start | bytes 589828
  132.1 13.2 %collective-permute-start.7 = (f32[24,2048]{1,0:T(8,128)S(1)}, f32[24,2048]{1,0:T(8,128)S(1)}, u32[]{:S(2)}, u32[]{:S(2)}) collective-permute-start(f32[24,2048]{1,0:T(8,128)S(1)} %copy-done.15), channel_id=1, source_target_pairs={{0,8},{8,0},{16,24},{24,16},{1,9},{9,1},{17,25},{25,17},{2,10},{10... | collective-permute-start | bytes 589832 | tf_op jit(solution)/shard_map/ppermute | solution.py:801
  132.1 15.2 %collective-permute-start.8 = (f32[24,2048]{1,0:T(8,128)S(1)}, f32[24,2048]{1,0:T(8,128)S(1)}, u32[]{:S(2)}, u32[]{:S(2)}) collective-permute-start(f32[24,2048]{1,0:T(8,128)S(1)} %copy-done.14), channel_id=1, source_target_pairs={{0,16},{8,24},{16,0},{24,8},{1,17},{9,25},{17,1},{25,9},{2,18},{10... | collective-permute-start | bytes 589832 | tf_op jit(solution)/shard_map/ppermute | solution.py:801
  133.8 13.5 %collective-permute-start.9 = (f32[24,2048]{1,0:T(8,128)}, f32[24,2048]{1,0:T(8,128)}, u32[]{:S(2)}, u32[]{:S(2)}) collective-permute-start(f32[24,2048]{1,0:T(8,128)} %get-tuple-element.34), channel_id=1, source_target_pairs={{0,24},{8,16},{16,8},{24,0},{1,25},{9,17},{17,9},{25,1},{2,26},{10... | collective-permute-start | bytes 589832 | tf_op jit(solution)/shard_map/ppermute | solution.py:801
  139.9 14.3 %collective-permute-start.6 = (f32[512,128]{1,0:T(8,128)}, f32[512,128]{1,0:T(8,128)S(1)}, u32[]{:S(2)}, u32[]{:S(2)}) collective-permute-start(f32[512,128]{1,0:T(8,128)} %finish_rest.1.own_ref), channel_id=1, source_target_pairs={{7,3},{6,2},{5,1},{4,0},{3,7},{2,6},{1,5},{0,4},{15,11},{14,10},{1... | collective-permute-start | bytes 786440 | tf_op jit(solution)/shard_map/ppermute | solution.py:810
  143.5 16.9 %collective-permute-start.13 = (f32[2,256,128]{2,1,0:T(8,128)}, f32[2,256,128]{2,1,0:T(8,128)S(1)}, u32[]{:S(2)}, u32[]{:S(2)}) collective-permute-start(f32[2,256,128]{2,1,0:T(8,128)} %get-tuple-element.41), channel_id=1, source_target_pairs={{0,1},{1,0},{2,3},{3,2},{4,5},{5,4},{6,7},{7,6},{8,9},{9,8},{10,11... | collective-permute-start | bytes 786440 | tf_op jit(solution)/shard_map/ppermute | solution.py:801
  145.2 16.2 %collective-permute-start.14 = (f32[2,256,128]{2,1,0:T(8,128)}, f32[2,256,128]{2,1,0:T(8,128)S(1)}, u32[]{:S(2)}, u32[]{:S(2)}) collective-permute-start(f32[2,256,128]{2,1,0:T(8,128)} %get-tuple-element.42), channel_id=1, source_target_pairs={{0,2},{1,3},{2,0},{3,1},{4,6},{5,7},{6,4},{7,5},{8,10},{9,11},{10,... | collective-permute-start | bytes 786440 | tf_op jit(solution)/shard_map/ppermute | solution.py:801
  147.3 18.4 %collective-permute-start.15 = (f32[2,256,128]{2,1,0:T(8,128)}, f32[2,256,128]{2,1,0:T(8,128)S(1)}, u32[]{:S(2)}, u32[]{:S(2)}) collective-permute-start(f32[2,256,128]{2,1,0:T(8,128)} %get-tuple-element.43), channel_id=1, source_target_pairs={{0,3},{1,2},{2,1},{3,0},{4,7},{5,6},{6,5},{7,4},{8,11},{9,10},{10,... | collective-permute-start | bytes 786440 | tf_op jit(solution)/shard_map/ppermute | solution.py:801
  157.9 17.2 %collective-permute-start.10 = (f32[2,288,128]{2,1,0:T(8,128)}, f32[2,288,128]{2,1,0:T(8,128)S(1)}, u32[]{:S(2)}, u32[]{:S(2)}) collective-permute-start(f32[2,288,128]{2,1,0:T(8,128)} %get-tuple-element.38), channel_id=1, source_target_pairs={{0,1},{1,0},{2,3},{3,2},{4,5},{5,4},{6,7},{7,6},{8,9},{9,8},{10,11... | collective-permute-start | bytes 884744 | tf_op jit(solution)/shard_map/ppermute | solution.py:801
  159.6 15.6 %collective-permute-start.11 = (f32[2,288,128]{2,1,0:T(8,128)}, f32[2,288,128]{2,1,0:T(8,128)S(1)}, u32[]{:S(2)}, u32[]{:S(2)}) collective-permute-start(f32[2,288,128]{2,1,0:T(8,128)} %get-tuple-element.39), channel_id=1, source_target_pairs={{0,2},{1,3},{2,0},{3,1},{4,6},{5,7},{6,4},{7,5},{8,10},{9,11},{10,... | collective-permute-start | bytes 884744 | tf_op jit(solution)/shard_map/ppermute | solution.py:801
  160.4 5.3 %copy-start.7 = (f32[2,256,128]{2,1,0:T(8,128)}, f32[2,256,128]{2,1,0:T(8,128)S(1)}, u32[]{:S(2)}) copy-start(f32[2,256,128]{2,1,0:T(8,128)S(1)} %collective-permute-done.13.refs_1_) | copy-start | bytes 786436
  160.4 16.3 %collective-permute-start.12 = (f32[2,288,128]{2,1,0:T(8,128)}, f32[2,288,128]{2,1,0:T(8,128)S(1)}, u32[]{:S(2)}, u32[]{:S(2)}) collective-permute-start(f32[2,288,128]{2,1,0:T(8,128)} %get-tuple-element.40), channel_id=1, source_target_pairs={{0,3},{1,2},{2,1},{3,0},{4,7},{5,6},{6,5},{7,4},{8,11},{9,10},{10,... | collective-permute-start | bytes 884744 | tf_op jit(solution)/shard_map/ppermute | solution.py:801
  (10 other events, 13.7 us)

commit v4 on v3

--- a/solution.py
+++ b/solution.py
@@ -974,11 +974,11 @@
     hat_u = finish_u(half, near_u, far_u, channels, kx_local, after=(part_e,))
     all_u = spread([hat_u] * batches, "batch")
     own_e, rounded, modes_a = finish_e(
-        batch, half, near_e, far_e, spectral_weight, skip_part, kx_local, batches, tuple(all_u[1:])
+        batch, half, near_e, far_e, spectral_weight, skip_part, kx_local, batches, (hat_u,)
     )
     far_a = exchange_far(modes_a)
     all_e = spread(own_e, "batch")
-    modes_b = finish_rest(rounded, spectral_weight, kx_local)
+    modes_b = finish_rest(rounded, spectral_weight, kx_local, after=tuple(all_u[1:]))
     modes_b, far_a = lax.optimization_barrier((modes_b, far_a))
     far_b = exchange_far(modes_b, turned=True)
     send_a = expand(half, relay, modes_a, far_a, spaces // 2, middle, kx_local)

time: 187 us -> 182 us (0.973)
  waiting for transfers between devices: 44.9 us -> 41.9 us
  starting transfers between devices: 26.5 us -> 24 us
    ppermute x12, waiting for transfers between devices: 10.5 us -> 5.75 us  [spread(): lax.ppermute(blocks[d], axis, [(s, s ^ d) for s in range(size)])]
    ppermute x4, starting transfers between devices: 5.67 us -> 3.29 us  [exchange_far(): return lax.ppermute(values, 'space', pairs)]
    unnamed x32 -> x26, local copies, waits for them, and re-layouts: 4.33 us -> 4.95 us
  transfers between devices with their start and end apart: 18 -> 18, of which waited for: 8 -> 7; matrix products, arithmetic and copies ran while one was open for 0% -> 0% of each run, Pallas kernels for 44% -> 49%
where the time goes in v4:
time: 182 us; the launch traced here: 181 us
  Pallas kernels  110 us (60%)
  waiting for transfers between devices  41.9 us (23%)
  starting transfers between devices  24 us (13%)
  local copies, waits for them, and re-layouts  4.95 us (3%)
    pallas_call x2, Pallas kernels, forward(): pl.pallas_call(functools.partial(body, planes=planes, spaces=spaces, bloc...  36.3 us
    ppermute x4, waiting for transfers between devices, exchange_far(): return lax.ppermute(values, 'space', pairs)  27 us
    pallas_call x1, Pallas kernels, mix(): pl.pallas_call(functools.partial(mix_body, planes=planes, count=count), o...  22.3 us
    pallas_call x2, Pallas kernels, grid_of(): pl.pallas_call(functools.partial(grid_body, planes=planes, relays=relays,...  17.7 us
    ppermute x12, starting transfers between devices, spread(): lax.ppermute(blocks[d], axis, [(s, s ^ d) for s in range(size)])  10.9 us
    all_to_all x2, starting transfers between devices, exchange_near(): lax.all_to_all(values, 'space', split_axis=0, concat_axis=0, axis_index_g...  9.87 us
    all_to_all x2, waiting for transfers between devices, exchange_near(): lax.all_to_all(values, 'space', split_axis=0, concat_axis=0, axis_index_g...  9.18 us
    pallas_call x1, Pallas kernels, finish_e(): pl.pallas_call(functools.partial(spectrum_e, kx_local=kx_local, per_step=...  7.62 us
  transfers between devices with their start and end apart: 18, of which 7 were waited for; matrix products, arithmetic and copies ran while one was open for 0% of the time, Pallas kernels for 49%

profile of v4, /device:TPU:0, one launch (start us, length us, event | category | flops | bytes accessed | tf_op | source)
XLA Modules:
  0.0 181.5 jit_solution(1354643526498628475)
XLA Ops:
  0.6 11.4 %forward_u.1.refs_0_ = f32[4,2,512,128]{3,2,1,0:T(8,128)} custom-call(bf16[32,2048,128]{2,1,0:T(8,128)(2,1)} %bitcast.9, bf16[1024,256]{1,0:T(8,128)(2,1)} %constant.46.clone.table_z, bf16[64,256]{1,0:T(8,128)(2,1)} %constant.47.clone.table_x), custom_call_target="tpu_custom_call" | custom-call | flops 22000001024 | bytes 1 | tf_op jit(solution)/shard_map/forward_u/pallas_call | solution.py:203
  12.0 5.2 %all-to-all-start.1 = ((f32[4,2,512,128]{3,2,1,0:T(8,128)}), f32[4,2,512,128]{3,2,1,0:T(8,128)}, u32[]{:S(2)}, u32[]{:S(2)}) async-start(f32[4,2,512,128]{3,2,1,0:T(8,128)} %forward_u.1.refs_0_), calls=%async_computation.1 | async-start | bytes 4194304 | tf_op jit(solution)/shard_map/all_to_all | solution.py:793
  17.2 24.9 %forward_e.1 = (f32[4,2,512,128]{3,2,1,0:T(8,128)}, bf16[32,2048,128]{2,1,0:T(8,128)(2,1)}) custom-call(bf16[32,2048,128]{2,1,0:T(8,128)(2,1)} %bitcast.7, bf16[32,2048,128]{2,1,0:T(8,128)(2,1)} %bitcast.8, bf16[1024,256]{1,0:T(8,128)(2,1)} %constant.46.clone.table_z, bf16[64,256]{1,0:T(8,128)(2,1)} %constant.47.clone.table_x, ...), custom_call_target="tpu_custom_call" | custom-call | flops 49999998976 | bytes 1 | tf_op jit(solution)/shard_map/forward_e/pallas_call | solution.py:203
  43.0 4.6 %all-to-all-start = ((f32[4,2,512,128]{3,2,1,0:T(8,128)}), f32[4,2,512,128]{3,2,1,0:T(8,128)}, u32[]{:S(2)}, u32[]{:S(2)}) async-start(f32[4,2,512,128]{3,2,1,0:T(8,128)} %get-tuple-element.25.refs_0_), calls=%async_computation | async-start | bytes 4194304 | tf_op jit(solution)/shard_map/all_to_all | solution.py:793
  47.6 2.8 %partial_u.1.refs_0_ = f32[1024,128]{1,0:T(8,128)} custom-call(s32[1]{0:T(128)} %bitcast.1.half_ref, f32[4,2,512,128]{3,2,1,0:T(8,128)} %all-to-all-done.1.near_ref, bf16[2,256,1536]{2,1,0:T(8,128)(2,1)} %constant.48.clone.table, f32[4,2,512,128]{3,2,1,0:T(8,128)} %get-tuple-element.25.refs_0_), custom_call_target="tpu_custom_call" | custom-call | flops 6000000000 | bytes 1 | tf_op jit(solution)/shard_map/partial_u/pallas_call | solution.py:272
  50.4 2.8 %collective-permute-start.1 = (f32[1024,128]{1,0:T(8,128)}, f32[1024,128]{1,0:T(8,128)S(1)}, u32[]{:S(2)}, u32[]{:S(2)}) collective-permute-start(f32[1024,128]{1,0:T(8,128)} %partial_u.1.refs_0_), channel_id=1, source_target_pairs={{0,4},{1,5},{2,6},{3,7},{4,0},{5,1},{6,2},{7,3},{8,12},{9,13},{10,... | collective-permute-start | bytes 1572872 | tf_op jit(solution)/shard_map/ppermute | solution.py:810
  53.2 22.3 %mix.1 = (bf16[32,2048,128]{2,1,0:T(8,128)(2,1)}, f32[32,128]{1,0:T(8,128)}) custom-call(bf16[32,2048,128]{2,1,0:T(8,128)(2,1)} %bitcast.10, bf16[32,2048,128]{2,1,0:T(8,128)(2,1)} %get-tuple-element.26.cot_ref, bf16[32,32]{1,0:T(8,128)(2,1)} %weight_ref.3, f32[1024,128]{1,0:T(8,128)} %partial_u.1.refs_0_), custom_call_target="tpu_custom_call" | custom-call | flops 44000002048 | bytes 1 | tf_op jit(solution)/shard_map/mix/pallas_call | solution.py:644
  75.5 8.4 %all-to-all-done.near_ref = f32[4,2,512,128]{3,2,1,0:T(8,128)} async-done(((f32[4,2,512,128]{3,2,1,0:T(8,128)}), f32[4,2,512,128]{3,2,1,0:T(8,128)}, u32[]{:S(2)}, u32[]{:S(2)}) %all-to-all-start) | async-done | bytes 2097184 | tf_op jit(solution)/shard_map/all_to_all | solution.py:793
  83.9 2.8 %partial_e.1.refs_0_ = f32[1056,128]{1,0:T(8,128)} custom-call(s32[1]{0:T(128)} %bitcast.1.half_ref, f32[4,2,512,128]{3,2,1,0:T(8,128)} %all-to-all-done.near_ref, bf16[2,256,1536]{2,1,0:T(8,128)(2,1)} %constant.48.clone.table, f32[32,128]{1,0:T(8,128)} %get-tuple-element.27.refs_0_.skip_ref), custom_call_target="tpu_custom_call" | custom-call | flops 6000000000 | bytes 1 | tf_op jit(solution)/shard_map/partial_e/pallas_call | solution.py:272
  88.0 3.6 %finish_u.1.refs_0_ = f32[64,2048]{1,0:T(8,128)} custom-call(s32[1]{0:T(128)} %bitcast.1.half_ref, f32[4,2,512,128]{3,2,1,0:T(8,128)} %all-to-all-done.1.near_ref, f32[1024,128]{1,0:T(8,128)} %copy-done.3, bf16[2,256,1536]{2,1,0:T(8,128)(2,1)} %constant.48.clone.table, f32[1056,128]{1,0:T(8,128)} %partial_e.1.refs_0_), custom_call_target="tpu_custom_call" | custom-call | flops 8000000000 | bytes 1 | tf_op jit(solution)/shard_map/finish_u/pallas_call | solution.py:346
  93.5 18.9 %collective-permute-done.far_ref = f32[1056,128]{1,0:T(8,128)S(1)} collective-permute-done((f32[1056,128]{1,0:T(8,128)}, f32[1056,128]{1,0:T(8,128)S(1)}, u32[]{:S(2)}, u32[]{:S(2)}) %collective-permute-start) | collective-permute-done | bytes 540704 | tf_op jit(solution)/shard_map/ppermute | solution.py:810
  113.2 7.6 %finish_e.1 = (f32[24,2048]{1,0:T(8,128)}, f32[24,2048]{1,0:T(8,128)}, f32[24,2048]{1,0:T(8,128)}, f32[24,2048]{1,0:T(8,128)}, f32[2,32,2048]{2,1,0:T(8,128)}, /*index=5*/f32[512,128]{1,0:T(8,128)}) custom-call(s32[1]{0:T(128)} %bitcast.2.batch_ref, s32[1]{0:T(128)} %bitcast.1.half_ref, f32[4,2,512,128]{3,2,1,0:T(8,128)} %all-to-all-done.near_ref, ...), custom_call_target="tpu_custom_call" | custom-call | flops 16000000000 | bytes 1 | tf_op jit(solution)/shard_map/finish_e/pallas_call | solution.py:452
  120.9 1.6 collective-permute-start.8
  123.2 4.9 %finish_rest.1.own_ref = f32[512,128]{1,0:T(8,128)} custom-call(f32[2,32,2048]{2,1,0:T(8,128)} %get-tuple-element.28.rounded, bf16[2,32,32,2048]{3,2,1,0:T(8,128)(2,1)} %weight_ref.5, f32[64,2048]{1,0:T(8,128)} %copy-done.1, f32[64,2048]{1,0:T(8,128)} %copy-done.2, f32[64,2048]{1,0:T(8,128)} %collective-permute-done.4.refs_2_.refs_3_), custom_call_target="tpu_custom_call" | custom-call | flops 10000000000 | bytes 1 | tf_op jit(solution)/shard_map/finish_rest/pallas_call | solution.py:486
  128.1 6.6 %collective-permute-done.5.far_ref = f32[512,128]{1,0:T(8,128)S(1)} collective-permute-done((f32[512,128]{1,0:T(8,128)}, f32[512,128]{1,0:T(8,128)S(1)}, u32[]{:S(2)}, u32[]{:S(2)}) %collective-permute-start.5) | collective-permute-done | bytes 262176 | tf_op jit(solution)/shard_map/ppermute | solution.py:810
  135.4 2.9 %expand.2 = (f32[2,256,128]{2,1,0:T(8,128)}, f32[2,256,128]{2,1,0:T(8,128)}, f32[2,256,128]{2,1,0:T(8,128)}, f32[2,256,128]{2,1,0:T(8,128)}) custom-call(s32[1]{0:T(128)} %bitcast.1.half_ref, s32[1]{0:T(128)} %bitcast.relay_ref, f32[512,128]{1,0:T(8,128)} %get-tuple-element.29.own_ref, f32[512,128]{1,0:T(8,128)} %copy-done.11, ...), custom_call_target="tpu_custom_call" | custom-call | flops 120000004096 | bytes 1 | tf_op jit(solution)/shard_map/expand/pallas_call | solution.py:550
  139.8 2.1 %collective-permute-start.14 = (f32[2,256,128]{2,1,0:T(8,128)}, f32[2,256,128]{2,1,0:T(8,128)S(1)}, u32[]{:S(2)}, u32[]{:S(2)}) collective-permute-start(f32[2,256,128]{2,1,0:T(8,128)} %get-tuple-element.42), channel_id=1, source_target_pairs={{0,2},{1,3},{2,0},{3,1},{4,6},{5,7},{6,4},{7,5},{8,10},{9,11},{10,... | collective-permute-start | bytes 786440 | tf_op jit(solution)/shard_map/ppermute | solution.py:801
  142.0 5.9 %cross.1.refs_4_ = f32[2,32,8,2048]{3,2,1,0:T(8,128)} custom-call(f32[64,2048]{1,0:T(8,128)} %finish_u.1.refs_0_, f32[64,2048]{1,0:T(8,128)} %copy-done.1, f32[64,2048]{1,0:T(8,128)} %copy-done.2, f32[64,2048]{1,0:T(8,128)} %collective-permute-done.4.refs_2_.refs_3_, f32[24,2048]{1,0:T(8,128)} %get-tuple-element.31.refs_4_.refs_0_, f32[24,2048]{1,0:T(8,128)} %copy-done.12, ...), custom_call_target="tpu_custom_call" | custom-call | flops 12000000000 | bytes 1 | tf_op jit(solution)/shard_map/cross/pallas_call | solution.py:776
  150.1 3.0 %expand.3 = (f32[2,288,128]{2,1,0:T(8,128)}, f32[2,288,128]{2,1,0:T(8,128)}, f32[2,288,128]{2,1,0:T(8,128)}, f32[2,288,128]{2,1,0:T(8,128)}) custom-call(s32[1]{0:T(128)} %bitcast.1.half_ref, s32[1]{0:T(128)} %bitcast.relay_ref, f32[512,128]{1,0:T(8,128)} %finish_rest.1.own_ref, f32[512,128]{1,0:T(8,128)} %copy-done.10, ...), custom_call_target="tpu_custom_call" | custom-call | flops 120000004096 | bytes 1 | tf_op jit(solution)/shard_map/expand/pallas_call | solution.py:550
  155.0 1.6 collective-permute-start.12
  156.6 3.9 %collective-permute-done.15.refs_3_ = f32[2,256,128]{2,1,0:T(8,128)S(1)} collective-permute-done((f32[2,256,128]{2,1,0:T(8,128)}, f32[2,256,128]{2,1,0:T(8,128)S(1)}, u32[]{:S(2)}, u32[]{:S(2)}) %collective-permute-start.15) | collective-permute-done | bytes 262176 | tf_op jit(solution)/shard_map/ppermute | solution.py:801
  161.2 8.8 %to_grid.2.refs_8_ = bf16[32,2048,128]{2,1,0:T(8,128)(2,1)} custom-call(s32[1]{0:T(128)} %bitcast.relay_ref, f32[2,256,128]{2,1,0:T(8,128)} %get-tuple-element.36.refs_8_.refs_0_, f32[2,256,128]{2,1,0:T(8,128)} %copy-done.7, f32[2,256,128]{2,1,0:T(8,128)} %copy-done.8, f32[2,256,128]{2,1,0:T(8,128)} %copy-done.9, ...), custom_call_target="tpu_custom_call", output_to_operand_aliasing={{}: (5, {})} | custom-call | flops 17999998976 | bytes 1 | tf_op jit(solution)/shard_map/to_grid/pallas_call | solution.py:731
  170.0 1.9 %collective-permute-done.12.refs_3_.refs_7_ = f32[2,288,128]{2,1,0:T(8,128)S(1)} collective-permute-done((f32[2,288,128]{2,1,0:T(8,128)}, f32[2,288,128]{2,1,0:T(8,128)S(1)}, u32[]{:S(2)}, u32[]{:S(2)}) %collective-permute-start.12) | collective-permute-done | bytes 294944 | tf_op jit(solution)/shard_map/ppermute | solution.py:801
  172.6 8.9 %to_grid.3 = (bf16[32,2048,128]{2,1,0:T(8,128)(2,1)}, f32[32,32]{1,0:T(8,128)}) custom-call(s32[1]{0:T(128)} %bitcast.relay_ref, f32[2,288,128]{2,1,0:T(8,128)} %get-tuple-element.37.refs_7_.refs_0_.refs_4_, f32[2,288,128]{2,1,0:T(8,128)} %copy-done.4, f32[2,288,128]{2,1,0:T(8,128)} %copy-done.5, ...), custom_call_target="tpu_custom_call", output_to_operand_aliasing={{0}: (9, {})} | custom-call | flops 17999998976 | bytes 1 | tf_op jit(solution)/shard_map/to_grid/pallas_call | solution.py:731
  (51 shorter events, 13.4 us)
Async XLA Ops:
  12.0 31.0 %all-to-all-start.1 = ((f32[4,2,512,128]{3,2,1,0:T(8,128)}), f32[4,2,512,128]{3,2,1,0:T(8,128)}, u32[]{:S(2)}, u32[]{:S(2)}) async-start(f32[4,2,512,128]{3,2,1,0:T(8,128)} %forward_u.1.refs_0_), calls=%async_computation.1 | async-start | bytes 4194304 | tf_op jit(solution)/shard_map/all_to_all | solution.py:793
  43.0 40.9 %all-to-all-start = ((f32[4,2,512,128]{3,2,1,0:T(8,128)}), f32[4,2,512,128]{3,2,1,0:T(8,128)}, u32[]{:S(2)}, u32[]{:S(2)}) async-start(f32[4,2,512,128]{3,2,1,0:T(8,128)} %get-tuple-element.25.refs_0_), calls=%async_computation | async-start | bytes 4194304 | tf_op jit(solution)/shard_map/all_to_all | solution.py:793
  50.4 36.8 %collective-permute-start.1 = (f32[1024,128]{1,0:T(8,128)}, f32[1024,128]{1,0:T(8,128)S(1)}, u32[]{:S(2)}, u32[]{:S(2)}) collective-permute-start(f32[1024,128]{1,0:T(8,128)} %partial_u.1.refs_0_), channel_id=1, source_target_pairs={{0,4},{1,5},{2,6},{3,7},{4,0},{5,1},{6,2},{7,3},{8,12},{9,13},{10,... | collective-permute-start | bytes 1572872 | tf_op jit(solution)/shard_map/ppermute | solution.py:810
  86.7 25.7 %collective-permute-start = (f32[1056,128]{1,0:T(8,128)}, f32[1056,128]{1,0:T(8,128)S(1)}, u32[]{:S(2)}, u32[]{:S(2)}) collective-permute-start(f32[1056,128]{1,0:T(8,128)} %partial_e.1.refs_0_), channel_id=1, source_target_pairs={{0,4},{1,5},{2,6},{3,7},{4,0},{5,1},{6,2},{7,3},{8,12},{9,13},{10,... | collective-permute-start | bytes 1622024 | tf_op jit(solution)/shard_map/ppermute | solution.py:810
  91.6 29.2 %collective-permute-start.2 = (f32[64,2048]{1,0:T(8,128)}, f32[64,2048]{1,0:T(8,128)S(1)}, u32[]{:S(2)}, u32[]{:S(2)}) collective-permute-start(f32[64,2048]{1,0:T(8,128)} %finish_u.1.refs_0_), channel_id=1, source_target_pairs={{0,8},{8,0},{16,24},{24,16},{1,9},{9,1},{17,25},{25,17},{2,10},{10... | collective-permute-start | bytes 1572872 | tf_op jit(solution)/shard_map/ppermute | solution.py:801
  91.7 30.8 %collective-permute-start.3 = (f32[64,2048]{1,0:T(8,128)}, f32[64,2048]{1,0:T(8,128)S(1)}, u32[]{:S(2)}, u32[]{:S(2)}) collective-permute-start(f32[64,2048]{1,0:T(8,128)} %finish_u.1.refs_0_), channel_id=1, source_target_pairs={{0,16},{8,24},{16,0},{24,8},{1,17},{9,25},{17,1},{25,9},{2,18},{10... | collective-permute-start | bytes 1572872 | tf_op jit(solution)/shard_map/ppermute | solution.py:801
  93.1 29.6 %collective-permute-start.4 = (f32[64,2048]{1,0:T(8,128)}, f32[64,2048]{1,0:T(8,128)}, u32[]{:S(2)}, u32[]{:S(2)}) collective-permute-start(f32[64,2048]{1,0:T(8,128)} %finish_u.1.refs_0_), channel_id=1, source_target_pairs={{0,24},{8,16},{16,8},{24,0},{1,25},{9,17},{17,9},{25,1},{2,26},{10... | collective-permute-start | bytes 1572872 | tf_op jit(solution)/shard_map/ppermute | solution.py:801
  120.8 13.9 %collective-permute-start.5 = (f32[512,128]{1,0:T(8,128)}, f32[512,128]{1,0:T(8,128)S(1)}, u32[]{:S(2)}, u32[]{:S(2)}) collective-permute-start(f32[512,128]{1,0:T(8,128)} %get-tuple-element.29.own_ref), channel_id=1, source_target_pairs={{0,4},{1,5},{2,6},{3,7},{4,0},{5,1},{6,2},{7,3},{8,12},{9,13},{10,... | collective-permute-start | bytes 786440 | tf_op jit(solution)/shard_map/ppermute | solution.py:810
  120.8 19.0 %collective-permute-start.7 = (f32[24,2048]{1,0:T(8,128)}, f32[24,2048]{1,0:T(8,128)S(1)}, u32[]{:S(2)}, u32[]{:S(2)}) collective-permute-start(f32[24,2048]{1,0:T(8,128)} %get-tuple-element.32), channel_id=1, source_target_pairs={{0,8},{8,0},{16,24},{24,16},{1,9},{9,1},{17,25},{25,17},{2,10},{10... | collective-permute-start | bytes 589832 | tf_op jit(solution)/shard_map/ppermute | solution.py:801
  120.9 1.9 %copy-start.1 = (f32[64,2048]{1,0:T(8,128)}, f32[64,2048]{1,0:T(8,128)S(1)}, u32[]{:S(2)}) copy-start(f32[64,2048]{1,0:T(8,128)S(1)} %collective-permute-done.2.refs_0_.refs_1_) | copy-start | bytes 1572868
  120.9 21.0 %collective-permute-start.8 = (f32[24,2048]{1,0:T(8,128)}, f32[24,2048]{1,0:T(8,128)}, u32[]{:S(2)}, u32[]{:S(2)}) collective-permute-start(f32[24,2048]{1,0:T(8,128)} %get-tuple-element.33), channel_id=1, source_target_pairs={{0,16},{8,24},{16,0},{24,8},{1,17},{9,25},{17,1},{25,9},{2,18},{10... | collective-permute-start | bytes 589832 | tf_op jit(solution)/shard_map/ppermute | solution.py:801
  122.4 19.6 %collective-permute-start.9 = (f32[24,2048]{1,0:T(8,128)}, f32[24,2048]{1,0:T(8,128)}, u32[]{:S(2)}, u32[]{:S(2)}) collective-permute-start(f32[24,2048]{1,0:T(8,128)} %get-tuple-element.34), channel_id=1, source_target_pairs={{0,24},{8,16},{16,8},{24,0},{1,25},{9,17},{17,9},{25,1},{2,26},{10... | collective-permute-start | bytes 589832 | tf_op jit(solution)/shard_map/ppermute | solution.py:801
  134.7 14.6 %collective-permute-start.6 = (f32[512,128]{1,0:T(8,128)}, f32[512,128]{1,0:T(8,128)S(1)}, u32[]{:S(2)}, u32[]{:S(2)}) collective-permute-start(f32[512,128]{1,0:T(8,128)} %finish_rest.1.own_ref), channel_id=1, source_target_pairs={{7,3},{6,2},{5,1},{4,0},{3,7},{2,6},{1,5},{0,4},{15,11},{14,10},{1... | collective-permute-start | bytes 786440 | tf_op jit(solution)/shard_map/ppermute | solution.py:810
  138.4 16.6 %collective-permute-start.13 = (f32[2,256,128]{2,1,0:T(8,128)}, f32[2,256,128]{2,1,0:T(8,128)S(1)}, u32[]{:S(2)}, u32[]{:S(2)}) collective-permute-start(f32[2,256,128]{2,1,0:T(8,128)} %get-tuple-element.41), channel_id=1, source_target_pairs={{0,1},{1,0},{2,3},{3,2},{4,5},{5,4},{6,7},{7,6},{8,9},{9,8},{10,11... | collective-permute-start | bytes 786440 | tf_op jit(solution)/shard_map/ppermute | solution.py:801
  139.8 2.2 %copy-start.12 = (f32[24,2048]{1,0:T(8,128)}, f32[24,2048]{1,0:T(8,128)S(1)}, u32[]{:S(2)}) copy-start(f32[24,2048]{1,0:T(8,128)S(1)} %collective-permute-done.7.refs_5_.refs_1_) | copy-start | bytes 589828
  139.8 16.8 %collective-permute-start.14 = (f32[2,256,128]{2,1,0:T(8,128)}, f32[2,256,128]{2,1,0:T(8,128)S(1)}, u32[]{:S(2)}, u32[]{:S(2)}) collective-permute-start(f32[2,256,128]{2,1,0:T(8,128)} %get-tuple-element.42), channel_id=1, source_target_pairs={{0,2},{1,3},{2,0},{3,1},{4,6},{5,7},{6,4},{7,5},{8,10},{9,11},{10,... | collective-permute-start | bytes 786440 | tf_op jit(solution)/shard_map/ppermute | solution.py:801
  141.9 18.6 %collective-permute-start.15 = (f32[2,256,128]{2,1,0:T(8,128)}, f32[2,256,128]{2,1,0:T(8,128)S(1)}, u32[]{:S(2)}, u32[]{:S(2)}) collective-permute-start(f32[2,256,128]{2,1,0:T(8,128)} %get-tuple-element.43), channel_id=1, source_target_pairs={{0,3},{1,2},{2,1},{3,0},{4,7},{5,6},{6,5},{7,4},{8,11},{9,10},{10,... | collective-permute-start | bytes 786440 | tf_op jit(solution)/shard_map/ppermute | solution.py:801
  153.1 16.9 %collective-permute-start.10 = (f32[2,288,128]{2,1,0:T(8,128)}, f32[2,288,128]{2,1,0:T(8,128)S(1)}, u32[]{:S(2)}, u32[]{:S(2)}) collective-permute-start(f32[2,288,128]{2,1,0:T(8,128)} %get-tuple-element.38), channel_id=1, source_target_pairs={{0,1},{1,0},{2,3},{3,2},{4,5},{5,4},{6,7},{7,6},{8,9},{9,8},{10,11... | collective-permute-start | bytes 884744 | tf_op jit(solution)/shard_map/ppermute | solution.py:801
  154.6 15.4 %collective-permute-start.11 = (f32[2,288,128]{2,1,0:T(8,128)}, f32[2,288,128]{2,1,0:T(8,128)S(1)}, u32[]{:S(2)}, u32[]{:S(2)}) collective-permute-start(f32[2,288,128]{2,1,0:T(8,128)} %get-tuple-element.39), channel_id=1, source_target_pairs={{0,2},{1,3},{2,0},{3,1},{4,6},{5,7},{6,4},{7,5},{8,10},{9,11},{10,... | collective-permute-start | bytes 884744 | tf_op jit(solution)/shard_map/ppermute | solution.py:801
  155.0 5.5 %copy-start.7 = (f32[2,256,128]{2,1,0:T(8,128)}, f32[2,256,128]{2,1,0:T(8,128)S(1)}, u32[]{:S(2)}) copy-start(f32[2,256,128]{2,1,0:T(8,128)S(1)} %collective-permute-done.13.refs_1_) | copy-start | bytes 786436
  155.0 16.9 %collective-permute-start.12 = (f32[2,288,128]{2,1,0:T(8,128)}, f32[2,288,128]{2,1,0:T(8,128)S(1)}, u32[]{:S(2)}, u32[]{:S(2)}) collective-permute-start(f32[2,288,128]{2,1,0:T(8,128)} %get-tuple-element.40), channel_id=1, source_target_pairs={{0,3},{1,2},{2,1},{3,0},{4,7},{5,6},{6,5},{7,4},{8,11},{9,10},{10,... | collective-permute-start | bytes 884744 | tf_op jit(solution)/shard_map/ppermute | solution.py:801
  156.6 3.9 %copy-start.8 = (f32[2,256,128]{2,1,0:T(8,128)}, f32[2,256,128]{2,1,0:T(8,128)S(1)}, u32[]{:S(2)}) copy-start(f32[2,256,128]{2,1,0:T(8,128)S(1)} %collective-permute-done.14.refs_2_) | copy-start | bytes 786436
  170.0 1.9 %copy-start.4 = (f32[2,288,128]{2,1,0:T(8,128)}, f32[2,288,128]{2,1,0:T(8,128)S(1)}, u32[]{:S(2)}) copy-start(f32[2,288,128]{2,1,0:T(8,128)S(1)} %collective-permute-done.10.refs_1_.refs_5_) | copy-start | bytes 884740
  170.0 1.9 %copy-start.5 = (f32[2,288,128]{2,1,0:T(8,128)}, f32[2,288,128]{2,1,0:T(8,128)S(1)}, u32[]{:S(2)}) copy-start(f32[2,288,128]{2,1,0:T(8,128)S(1)} %collective-permute-done.11.refs_2_.refs_6_) | copy-start | bytes 884740
  (7 other events, 5.2 us)
